TPU v7x, 32 devices: a whole 2x2x4 slice. The times are simulated.
32 devices in a mesh: dp: 16 (over z, y, x), mp: 2 (over core).
Axes of the slice: x: 2, y: 2, z: 4, core: 2. Of those that a mesh axis runs over, the one named last changes fastest.
Arguments:
- tokens: bfloat16 [256, 128, 768], P(('dp', 'mp')), may hold values from -6 to 6
- cotangent: bfloat16 [256, 128, 768], P(('dp', 'mp')), may hold values from -6 to 6
- lengths: int32 [256], P(('dp', 'mp')), may hold values from 2 to 128, as said below
- token_types: int32 [256, 128], P(('dp', 'mp')), may hold values from 0 to 1, as said below
- node_pairs: int32 [256, 128, 2], P(('dp', 'mp')), may hold values from 0 to 63, as said below
- laplacian: float32 [256, 64, 16], P(('dp', 'mp')), may hold values from -4 to 4
- qkv_weight: bfloat16 [768, 3, 768], P(None, None, 'mp'), may hold values from -0.21875 to 0.21875
- out_weight: bfloat16 [768, 768], P('mp'), may hold values from -1.75 to 1.75
- up_weight: bfloat16 [768, 768], P(None, 'mp'), may hold values from -0.21875 to 0.21875
- down_weight: bfloat16 [768, 768], P('mp'), may hold values from -0.21875 to 0.21875
- qkv_master: float32 [768, 3, 768], P('dp', None, 'mp'), may hold values from -0.21875 to 0.21875
- qkv_mean: float32 [768, 3, 768], P('dp', None, 'mp'), may hold values from -0.0008544922 to 0.0008544922
- qkv_square: float32 [768, 3, 768], P('dp', None, 'mp'), may hold values from 7.2867343e-09 to 1.1770878e-07
- out_master: float32 [768, 768], P(('mp', 'dp')), may hold values from -0.21875 to 0.21875
- out_mean: float32 [768, 768], P(('mp', 'dp')), may hold values from -0.00036621094 to 0.00036621094
- out_square: float32 [768, 768], P(('mp', 'dp')), may hold values from 7.286734e-10 to 1.17708785e-08
- up_master: float32 [768, 768], P('dp', 'mp'), may hold values from -0.21875 to 0.21875
- up_mean: float32 [768, 768], P('dp', 'mp'), may hold values from -0.0008544922 to 0.0008544922
- up_square: float32 [768, 768], P('dp', 'mp'), may hold values from 7.2867343e-09 to 1.1770878e-07
- down_master: float32 [768, 768], P(('mp', 'dp')), may hold values from -0.21875 to 0.21875
- down_mean: float32 [768, 768], P(('mp', 'dp')), may hold values from -0.00036621094 to 0.00036621094
- down_square: float32 [768, 768], P(('mp', 'dp')), may hold values from 7.286734e-10 to 1.17708785e-08
- norm_params: float32 [4, 768], replicated, may hold values from -1.2 to 3.3, as said below
- norm_mean: float32 [4, 768], P(None, ('dp', 'mp')), may hold values from -0.0034179688 to 0.0034179688
- norm_square: float32 [4, 768], P(None, ('dp', 'mp')), may hold values from 1.1770878e-07 to 1.8777354e-06
- embed_weight: float32 [34, 768], replicated, may hold values from -1 to 1
- embed_mean: float32 [34, 768], P(None, ('dp', 'mp')), may hold values from -0.0034179688 to 0.0034179688
- embed_square: float32 [34, 768], P(None, ('dp', 'mp')), may hold values from 1.1770878e-07 to 1.8777354e-06
Outputs:
- output: bfloat16 [256, 128, 768], P(('dp', 'mp'))
- input_grad: float32 [256, 128, 768], P(('dp', 'mp'))
- clip_norm: float32 [], replicated
- qkv_updated: float32 [768, 3, 768], P('dp', None, 'mp')
- qkv_newmean: float32 [768, 3, 768], P('dp', None, 'mp')
- qkv_newsquare: float32 [768, 3, 768], P('dp', None, 'mp')
- out_updated: float32 [768, 768], P(('mp', 'dp'))
- out_newmean: float32 [768, 768], P(('mp', 'dp'))
- out_newsquare: float32 [768, 768], P(('mp', 'dp'))
- up_updated: float32 [768, 768], P('dp', 'mp')
- up_newmean: float32 [768, 768], P('dp', 'mp')
- up_newsquare: float32 [768, 768], P('dp', 'mp')
- down_updated: float32 [768, 768], P(('mp', 'dp'))
- down_newmean: float32 [768, 768], P(('mp', 'dp'))
- down_newsquare: float32 [768, 768], P(('mp', 'dp'))
- norm_updated: float32 [4, 768], P(None, ('dp', 'mp'))
- norm_newmean: float32 [4, 768], P(None, ('dp', 'mp'))
- norm_newsquare: float32 [4, 768], P(None, ('dp', 'mp'))
- embed_updated: float32 [34, 768], P(None, ('dp', 'mp'))
- embed_newmean: float32 [34, 768], P(None, ('dp', 'mp'))
- embed_newsquare: float32 [34, 768], P(None, ('dp', 'mp'))
Inputs may be any that keep to these rules, and one draw needn't show every extreme that they name: A molecule's tokens fill its first lengths[m] slots; some molecule has exactly 128. `token_types`: 0 for a node token, 1 for an edge token; within a molecule's length the node tokens come first; slots beyond the length hold 0. `node_pairs`: A node token's pair is its own slot twice; an edge token's entries are below its molecule's number of node tokens, which is at most 64; slots beyond the length hold 0. `norm_params`: rows 0 and 2 hold the two norms' gains, rows 1 and 3 their shifts.
All inputs are finite; a program needn't handle non-finite values.
Results may differ from a plain program's by a relative error of at most 0.014.
The roundings to bfloat16 on the way count: a program that leaves them out, or rounds other values in their place, can miss the bound.
Values may be sent and summed in bfloat16 or wider, within the bound.
No kernel may reach another device: no remote copies, remote signals or barrier semaphores. Data moves between devices by JAX's collectives and lax.ppermute only.
A program may use at most 192 MiB of HBM per device.

v0:
```python
from functools import partial
import math

import jax
import jax.numpy as jnp
from jax import lax
from jax.sharding import PartitionSpec as P

HEAD_DIM = 24
STEP = 10


NORM_EPS = 1e-05
BETA_FIRST = 0.9
BETA_SECOND = 0.95
ADAM_EPS = 1e-08
MATRIX_RATE = 0.03
NORM_RATE = 0.5
EMBED_RATE = 0.05
MATRIX_DECAY = 0.1
CLIP_LIMIT = 1.0
MASK_VALUE = -1e30
PRECISE = lax.Precision.HIGHEST


def layer_norm(values, gain_row, shift_row):
    centred = values - jnp.mean(values, axis=-1, keepdims=True)
    spread = jnp.mean(centred * centred, axis=-1, keepdims=True)
    return centred * lax.rsqrt(spread + NORM_EPS) * gain_row + shift_row


def token_features(token_types, node_pairs, laplacian):
    node_iota = jnp.arange(laplacian.shape[1], dtype=jnp.int32)
    left_pick = (node_pairs[:, :, 0:1] == node_iota).astype(jnp.float32)
    right_pick = (node_pairs[:, :, 1:2] == node_iota).astype(jnp.float32)
    left_ident = jnp.einsum("msn,mnl->msl", left_pick, laplacian, precision=PRECISE)
    right_ident = jnp.einsum("msn,mnl->msl", right_pick, laplacian, precision=PRECISE)
    type_pick = (token_types[:, :, None] == jnp.arange(2, dtype=jnp.int32)).astype(jnp.float32)
    return jnp.concatenate([left_ident, right_ident, type_pick], axis=-1)


def adam_step(master, mean_old, square_old, gradient, rate, decay, clip_scale):
    clipped = gradient * clip_scale
    mean_new = BETA_FIRST * mean_old + (1.0 - BETA_FIRST) * clipped
    square_new = BETA_SECOND * square_old + (1.0 - BETA_SECOND) * clipped * clipped
    mean_hat = mean_new / (1.0 - BETA_FIRST**STEP)
    square_hat = square_new / (1.0 - BETA_SECOND**STEP)
    updated = master - rate * (mean_hat / (jnp.sqrt(square_hat) + ADAM_EPS) + decay * master)
    return (updated, mean_new, square_new)


def masked_scores(query_rows, key_rows, key_mask):
    score_scale = 1.0 / math.sqrt(HEAD_DIM)
    raw_scores = jnp.einsum(
        "mqhe,mkhe->mhqk", query_rows, key_rows, preferred_element_type=jnp.float32
    )
    return jnp.where(key_mask[:, None, None, :], raw_scores * score_scale, MASK_VALUE)


def attention_forward(query_rows, key_rows, value_rows, key_mask):
    scaled = masked_scores(query_rows, key_rows, key_mask)
    top_score = jnp.max(scaled, axis=-1, keepdims=True)
    total = jnp.sum(jnp.exp(scaled - top_score), axis=-1, keepdims=True)
    log_total = top_score + jnp.log(total)
    probs_low = jnp.exp(scaled - log_total).astype(jnp.bfloat16)
    mixed = jnp.einsum("mhqk,mkhe->mqhe", probs_low, value_rows, preferred_element_type=jnp.float32)
    return (mixed.astype(jnp.bfloat16), log_total)


def attention_backward(query_rows, key_rows, value_rows, key_mask, log_total, grad_mixed):
    score_scale = 1.0 / math.sqrt(HEAD_DIM)
    probs = jnp.exp(masked_scores(query_rows, key_rows, key_mask) - log_total)
    probs_low = probs.astype(jnp.bfloat16)
    grad_probs = jnp.einsum(
        "mqhe,mkhe->mhqk", grad_mixed, value_rows, preferred_element_type=jnp.float32
    )
    grad_values = jnp.einsum(
        "mhqk,mqhe->mkhe", probs_low, grad_mixed, preferred_element_type=jnp.float32
    )
    inner = jnp.sum(probs * grad_probs, axis=-1, keepdims=True)
    grad_scores = (probs * (grad_probs - inner) * score_scale).astype(jnp.bfloat16)
    grad_queries = jnp.einsum(
        "mhqk,mkhe->mqhe", grad_scores, key_rows, preferred_element_type=jnp.float32
    )
    grad_keys = jnp.einsum(
        "mhqk,mqhe->mkhe", grad_scores, query_rows, preferred_element_type=jnp.float32
    )
    return (
        grad_queries.astype(jnp.bfloat16),
        grad_keys.astype(jnp.bfloat16),
        grad_values.astype(jnp.bfloat16),
    )


def on_device(
    tokens,
    cotangent,
    lengths,
    token_types,
    node_pairs,
    laplacian,
    qkv_weight,
    out_weight,
    up_weight,
    down_weight,
    qkv_master,
    qkv_mean,
    qkv_square,
    out_master,
    out_mean,
    out_square,
    up_master,
    up_mean,
    up_square,
    down_master,
    down_mean,
    down_square,
    norm_params,
    norm_mean,
    norm_square,
    embed_weight,
    embed_mean,
    embed_square,
):
    local_mols, slot_count, width = tokens.shape
    qkv_use, out_use, up_use, down_use = (qkv_weight, out_weight, up_weight, down_weight)
    local_heads = qkv_use.shape[2] // HEAD_DIM
    local_width = local_heads * HEAD_DIM
    features = token_features(token_types, node_pairs, laplacian)
    hidden0 = tokens.astype(jnp.float32) + jnp.einsum(
        "msi,id->msd", features, embed_weight, precision=PRECISE
    )
    normed_a = layer_norm(hidden0, norm_params[0], norm_params[1]).astype(jnp.bfloat16)
    gathered_a, all_lengths = (
        lax.all_gather(normed_a, "mp", axis=0, tiled=True),
        lax.all_gather(lengths, "mp", axis=0, tiled=True),
    )
    group_mols = gathered_a.shape[0]
    projected = jnp.einsum(
        "msd,dce->cmse", gathered_a, qkv_use, preferred_element_type=jnp.float32
    ).astype(jnp.bfloat16)
    key_mask = jnp.arange(slot_count, dtype=jnp.int32)[None, :] < all_lengths[:, None]
    per_block = math.gcd(group_mols, max(1, 512 // slot_count))
    block_count = group_mols // per_block

    def split_blocks(array):
        return array.reshape((block_count, per_block) + array.shape[1:])

    head_view = projected.reshape(3, group_mols, slot_count, local_heads, HEAD_DIM)
    query_blocks = split_blocks(head_view[0])
    key_blocks = split_blocks(head_view[1])
    value_blocks = split_blocks(head_view[2])
    mask_blocks = split_blocks(key_mask)
    mixed_blocks, log_totals = lax.map(
        lambda block_args: attention_forward(*block_args),
        (query_blocks, key_blocks, value_blocks, mask_blocks),
    )
    mixed = mixed_blocks.reshape(group_mols, slot_count, local_width)
    rows_in = mixed
    attn = lax.psum_scatter(
        jnp.einsum("msf,fd->msd", rows_in, out_use, preferred_element_type=jnp.float32).astype(
            jnp.bfloat16
        ),
        "mp",
        scatter_dimension=0,
        tiled=True,
    ).astype(jnp.float32)
    hidden1 = hidden0 + attn
    normed_b = layer_norm(hidden1, norm_params[2], norm_params[3]).astype(jnp.bfloat16)
    gathered_b = lax.all_gather(normed_b, "mp", axis=0, tiled=True)
    pre_act = jnp.einsum("msd,df->msf", gathered_b, up_use, preferred_element_type=jnp.float32)
    gelu_exact = partial(jax.nn.gelu, approximate=False)
    activ = gelu_exact(pre_act).astype(jnp.bfloat16)
    rows_in = lax.slice_in_dim(activ, 0, local_mols * lax.axis_size("mp"), axis=0)
    ffn = lax.psum_scatter(
        jnp.einsum("msf,fd->msd", rows_in, down_use, preferred_element_type=jnp.float32).astype(
            jnp.bfloat16
        ),
        "mp",
        scatter_dimension=0,
        tiled=True,
    ).astype(jnp.float32)
    output = (hidden1 + ffn).astype(jnp.bfloat16)
    gathered_cot = lax.all_gather(cotangent, "mp", axis=0, tiled=True)
    grad_down = jnp.einsum("msf,msd->fd", activ, gathered_cot, preferred_element_type=jnp.float32)
    grad_activ = jnp.einsum(
        "msd,fd->msf", gathered_cot, down_use, preferred_element_type=jnp.float32
    )
    unused_value, gelu_pull = jax.vjp(gelu_exact, pre_act)
    grad_pre = gelu_pull(grad_activ)[0].astype(jnp.bfloat16)
    grad_up = jnp.einsum("msd,msf->df", gathered_b, grad_pre, preferred_element_type=jnp.float32)
    rows_in = grad_pre
    grad_b = lax.psum_scatter(
        jnp.einsum("msf,df->msd", rows_in, up_use, preferred_element_type=jnp.float32).astype(
            jnp.bfloat16
        ),
        "mp",
        scatter_dimension=0,
        tiled=True,
    ).astype(jnp.float32)
    unused_second, norm_pull_b = jax.vjp(layer_norm, hidden1, norm_params[2], norm_params[3])
    grad_h1_part, grad_gain_b, grad_shift_b = norm_pull_b(grad_b)
    grad_h1 = cotangent.astype(jnp.float32) + grad_h1_part
    gathered_grad_attn = lax.all_gather(grad_h1.astype(jnp.bfloat16), "mp", axis=0, tiled=True)
    grad_out = jnp.einsum(
        "msf,msd->fd", mixed, gathered_grad_attn, preferred_element_type=jnp.float32
    )
    grad_mixed = jnp.einsum(
        "msd,fd->msf", gathered_grad_attn, out_use, preferred_element_type=jnp.float32
    ).astype(jnp.bfloat16)
    grad_mixed_blocks = split_blocks(
        grad_mixed.reshape(group_mols, slot_count, local_heads, HEAD_DIM)
    )
    grad_query_blocks, grad_key_blocks, grad_value_blocks = lax.map(
        lambda block_args: attention_backward(*block_args),
        (query_blocks, key_blocks, value_blocks, mask_blocks, log_totals, grad_mixed_blocks),
    )
    grad_projected = jnp.stack(
        [
            grad_query_blocks.reshape(group_mols, slot_count, local_width),
            grad_key_blocks.reshape(group_mols, slot_count, local_width),
            grad_value_blocks.reshape(group_mols, slot_count, local_width),
        ]
    )
    grad_qkv = jnp.einsum(
        "msd,cmse->dce", gathered_a, grad_projected, preferred_element_type=jnp.float32
    )
    rows_in = grad_projected
    grad_a = lax.psum_scatter(
        jnp.einsum("cmse,dce->msd", rows_in, qkv_use, preferred_element_type=jnp.float32).astype(
            jnp.bfloat16
        ),
        "mp",
        scatter_dimension=0,
        tiled=True,
    ).astype(jnp.float32)
    unused_third, norm_pull_a = jax.vjp(layer_norm, hidden0, norm_params[0], norm_params[1])
    grad_h0_part, grad_gain_a, grad_shift_a = norm_pull_a(grad_a)
    input_grad = grad_h1 + grad_h0_part
    grad_embed = jnp.einsum("msi,msd->id", features, input_grad, precision=PRECISE)
    grad_norm = jnp.stack([grad_gain_a, grad_shift_a, grad_gain_b, grad_shift_b])
    reduced_qkv, reduced_out, reduced_up, reduced_down = (
        lax.psum_scatter(grad_qkv, "dp", scatter_dimension=0, tiled=True),
        lax.psum_scatter(grad_out, "dp", scatter_dimension=0, tiled=True),
        lax.psum_scatter(grad_up, "dp", scatter_dimension=0, tiled=True),
        lax.psum_scatter(grad_down, "dp", scatter_dimension=0, tiled=True),
    )
    reduced_norm, reduced_embed = (
        lax.psum_scatter(grad_norm, ("dp", "mp"), scatter_dimension=1, tiled=True),
        lax.psum_scatter(grad_embed, ("dp", "mp"), scatter_dimension=1, tiled=True),
    )
    own_square = (
        jnp.sum(reduced_qkv * reduced_qkv)
        + jnp.sum(reduced_out * reduced_out)
        + jnp.sum(reduced_up * reduced_up)
        + jnp.sum(reduced_down * reduced_down)
        + jnp.sum(reduced_norm * reduced_norm)
        + jnp.sum(reduced_embed * reduced_embed)
    )
    total_square = lax.psum(own_square, ("dp", "mp"))
    clip_norm = jnp.sqrt(total_square)
    clip_scale = jnp.minimum(1.0, CLIP_LIMIT / (clip_norm + 1e-06))
    shard_index = lax.axis_index("dp") * lax.axis_size("mp") + lax.axis_index("mp")
    shard_width = width // (lax.axis_size("dp") * lax.axis_size("mp"))
    norm_own = lax.dynamic_slice_in_dim(norm_params, shard_index * shard_width, shard_width, 1)
    embed_own = lax.dynamic_slice_in_dim(embed_weight, shard_index * shard_width, shard_width, 1)
    qkv_new = adam_step(
        qkv_master, qkv_mean, qkv_square, reduced_qkv, MATRIX_RATE, MATRIX_DECAY, clip_scale
    )
    out_new = adam_step(
        out_master, out_mean, out_square, reduced_out, MATRIX_RATE, MATRIX_DECAY, clip_scale
    )
    up_new = adam_step(
        up_master, up_mean, up_square, reduced_up, MATRIX_RATE, MATRIX_DECAY, clip_scale
    )
    down_new = adam_step(
        down_master, down_mean, down_square, reduced_down, MATRIX_RATE, MATRIX_DECAY, clip_scale
    )
    norm_new = adam_step(norm_own, norm_mean, norm_square, reduced_norm, NORM_RATE, 0.0, clip_scale)
    embed_new = adam_step(
        embed_own, embed_mean, embed_square, reduced_embed, EMBED_RATE, 0.0, clip_scale
    )
    return (
        output,
        input_grad,
        clip_norm,
        qkv_new[0],
        qkv_new[1],
        qkv_new[2],
        out_new[0],
        out_new[1],
        out_new[2],
        up_new[0],
        up_new[1],
        up_new[2],
        down_new[0],
        down_new[1],
        down_new[2],
        norm_new[0],
        norm_new[1],
        norm_new[2],
        embed_new[0],
        embed_new[1],
        embed_new[2],
    )


def solution(mesh):
    return jax.shard_map(
        on_device,
        mesh=mesh,
        in_specs=(
            P(("dp", "mp"), None, None),
            P(("dp", "mp"), None, None),
            P(("dp", "mp")),
            P(("dp", "mp"), None),
            P(("dp", "mp"), None, None),
            P(("dp", "mp"), None, None),
            P(None, None, "mp"),
            P("mp", None),
            P(None, "mp"),
            P("mp", None),
            P("dp", None, "mp"),
            P("dp", None, "mp"),
            P("dp", None, "mp"),
            P(("mp", "dp"), None),
            P(("mp", "dp"), None),
            P(("mp", "dp"), None),
            P("dp", "mp"),
            P("dp", "mp"),
            P("dp", "mp"),
            P(("mp", "dp"), None),
            P(("mp", "dp"), None),
            P(("mp", "dp"), None),
            P(),
            P(None, ("dp", "mp")),
            P(None, ("dp", "mp")),
            P(),
            P(None, ("dp", "mp")),
            P(None, ("dp", "mp")),
        ),
        out_specs=(
            P(("dp", "mp"), None, None),
            P(("dp", "mp"), None, None),
            P(),
            P("dp", None, "mp"),
            P("dp", None, "mp"),
            P("dp", None, "mp"),
            P(("mp", "dp"), None),
            P(("mp", "dp"), None),
            P(("mp", "dp"), None),
            P("dp", "mp"),
            P("dp", "mp"),
            P("dp", "mp"),
            P(("mp", "dp"), None),
            P(("mp", "dp"), None),
            P(("mp", "dp"), None),
            P(None, ("dp", "mp")),
            P(None, ("dp", "mp")),
            P(None, ("dp", "mp")),
            P(None, ("dp", "mp")),
            P(None, ("dp", "mp")),
            P(None, ("dp", "mp")),
        ),
        check_vma=False,
    )
```

profile of v0, /device:TPU:0, one launch (start us, length us, event | category | flops | bytes accessed | tf_op | source)
XLA Modules:
  0.0 1024.7 jit_solution(16726716384819150953)
XLA Ops:
  23.6 11.1 %all-gather.5.cloned.1.call-done = bf16[16,128,768]{2,1,0:T(8,128)(2,1)} async-done(((bf16[8,128,768]{2,1,0:T(8,128)(2,1)}), bf16[16,128,768]{2,1,0:T(8,128)(2,1)}) %all-gather.5.cloned.1.call-update) | async-done | bytes 3145744 | tf_op jit(solution)/shard_map/all_gather | solution.py:135
  52.0 27.9 %while.26 = (s32[]{:T(128)}, bf16[4,4,128,16,24]{2,4,3,1,0:T(8,128)(2,1)}, f32[4,4,16,128,1]{3,2,1,4,0:T(8,128)}, bf16[4,4,128,16,24]{2,4,3,1,0:T(8,128)(2,1)}, ...) while((s32[]{:T(128)}, ...), condition=%wide.region_5.6_spmd, body=%wide.region_2.5_spmd.sunk | while | flops 112386048 | bytes 14422629 | solution.py:154
  86.0 11.8 %reduce-scatter.13.cloned.1.call-done = bf16[8,128,768]{2,1,0:T(8,128)(2,1)} async-done(((bf16[16,128,768]{2,1,0:T(8,128)(2,1)}), bf16[8,128,768]{2,1,0:T(8,128)(2,1)}) %reduce-scatter.13.cloned.1.call-update) | async-done | bytes 1572880 | tf_op jit(solution)/shard_map/reduce_scatter | solution.py:160
  104.6 12.8 %all-gather.7.cloned.1.call-done = bf16[16,128,768]{2,1,0:T(8,128)(2,1)} async-done(((bf16[8,128,768]{2,1,0:T(8,128)(2,1)}), bf16[16,128,768]{2,1,0:T(8,128)(2,1)}) %all-gather.7.cloned.1.call-update) | async-done | bytes 3145744 | tf_op jit(solution)/shard_map/all_gather | solution.py:170
  123.5 8.0 multiply_convert_fusion.1
  143.4 12.2 %reduce-scatter.17.cloned.1.call-done = bf16[8,128,768]{2,1,0:T(8,128)(2,1)} async-done(((bf16[16,128,768]{2,1,0:T(8,128)(2,1)}), bf16[8,128,768]{2,1,0:T(8,128)(2,1)}) %reduce-scatter.17.cloned.1.call-update) | async-done | bytes 1572880 | tf_op jit(solution)/shard_map/reduce_scatter | solution.py:193
  163.5 13.2 %all-gather.11.cloned.1.call-done = bf16[16,128,768]{2,1,0:T(8,128)(2,1)} async-done(((bf16[8,128,768]{2,1,0:T(8,128)(2,1)}), bf16[16,128,768]{2,1,0:T(8,128)(2,1)}) %all-gather.11.cloned.1.call-update) | async-done | bytes 3145744 | tf_op jit(solution)/shard_map/all_gather | solution.py:204
  188.7 107.2 %while.27 = (s32[]{:T(128)}, bf16[4,4,128,16,24]{2,4,3,1,0:T(8,128)(2,1)}, bf16[4,4,128,16,24]{2,4,3,1,0:T(8,128)(2,1)}, bf16[4,4,128,16,24]{2,4,3,1,0:T(8,128)(...) while((s32[]{:T(128)}, ...), condition=%wide.region_15.16_spmd, body=%wide.region_13.15_spmd.sunk | while | flops 266944768 | bytes 73243312 | solution.py:214
  199.8 7.9 fusion.197
  207.7 7.7 fusion.196
  226.5 7.9 fusion.197
  234.5 7.7 fusion.196
  253.3 8.0 fusion.197
  261.3 7.7 fusion.196
  280.1 8.0 fusion.197
  303.6 8.4 bitcast_convert_fusion
  353.6 8.9 fusion.103
  363.8 105.3 %reduce-scatter.25.cloned.1.call-done = f32[48,384]{1,0:T(8,128)} async-done(((f32[768,384]{1,0:T(8,128)}), f32[48,384]{1,0:T(8,128)}) %reduce-scatter.25.cloned.1.call-update) | async-done | bytes 73744 | tf_op jit(solution)/shard_map/reduce_scatter | solution.py:245
  470.6 126.5 %reduce-scatter.27.cloned.1.call-done = f32[24,768]{1,0:T(8,128)} async-done(((f32[384,768]{1,0:T(8,128)}), f32[24,768]{1,0:T(8,128)}) %reduce-scatter.27.cloned.1.call-update) | async-done | bytes 73744 | tf_op jit(solution)/shard_map/reduce_scatter | solution.py:246
  598.6 126.7 %reduce-scatter.23.cloned.1.call-done = f32[24,768]{1,0:T(8,128)} async-done(((f32[384,768]{1,0:T(8,128)}), f32[24,768]{1,0:T(8,128)}) %reduce-scatter.23.cloned.1.call-update) | async-done | bytes 73744 | tf_op jit(solution)/shard_map/reduce_scatter | solution.py:244
  726.8 40.1 %all-reduce.1 = f32[4,768]{1,0:T(4,128)S(1)} all-reduce(f32[4,768]{1,0:T(4,128)S(1)} %pad_maximum_fusion.6), channel_id=10, replica_groups=mesh['dp'=16,'mp'=2] {'dp','mp'}, use_global_device_ids=true, to_apply=%region_31.32.clone | all-reduce | flops 3072 | bytes 24576
  767.5 56.3 %reduce-scatter.29.cloned.1.call-done = f32[34,24]{0,1:T(8,128)} async-done(((f32[34,768]{0,1:T(8,128)}), f32[34,24]{0,1:T(8,128)}) %reduce-scatter.29.cloned.1.call-update) | async-done | bytes 3280
  825.1 137.2 %reduce-scatter.21.cloned.1.call-done = f32[48,3,384]{2,0,1:T(8,128)} async-done(((f32[768,3,384]{2,0,1:T(8,128)}), f32[48,3,384]{2,0,1:T(8,128)}) %reduce-scatter.21.cloned.1.call-update) | async-done | bytes 221200 | tf_op jit(solution)/shard_map/reduce_scatter | solution.py:243
  967.9 40.0 %psum.7 = f32[]{:T(128)} all-reduce(f32[]{:T(128)S(6)} %add.229), channel_id=1, replica_groups=mesh['dp'=16,'mp'=2] {'dp','mp'}, use_global_device_ids=true, to_apply=%region_35.36 | all-reduce | flops 1 | bytes 8 | tf_op jit(solution)/shard_map/psum | solution.py:260
  (225 shorter events, 230.0 us)
Async XLA Ops:
  7.2 27.6 %all-gather.5.cloned.1.call-start = ((), (), s32[]{:S(2)}) async-start(), calls=%async_computation.9 | async-start | bytes 4718592 | tf_op jit(solution)/shard_map/all_gather | solution.py:135
  19.8 78.0 %reduce-scatter.13.cloned.1.call-start = ((), (), s32[]{:S(2)}) async-start(), calls=%async_computation.10 | async-start | bytes 4718592 | tf_op jit(solution)/shard_map/reduce_scatter | solution.py:160
  85.5 31.9 %all-gather.7.cloned.1.call-start = ((), (), s32[]{:S(2)}) async-start(), calls=%async_computation.11 | async-start | bytes 4718592 | tf_op jit(solution)/shard_map/all_gather | solution.py:170
  103.9 28.2 %all-gather.9.cloned.1.call-start = ((), (), s32[]{:S(2)}) async-start(), calls=%async_computation.13 | async-start | bytes 4718592 | tf_op jit(solution)/shard_map/all_gather | solution.py:184
  104.5 51.0 %reduce-scatter.17.cloned.1.call-start = ((), (), s32[]{:S(2)}) async-start(), calls=%async_computation.14 | async-start | bytes 4718592 | tf_op jit(solution)/shard_map/reduce_scatter | solution.py:193
  143.3 33.4 %all-gather.11.cloned.1.call-start = ((), (), s32[]{:S(2)}) async-start(), calls=%async_computation.15 | async-start | bytes 4718592 | tf_op jit(solution)/shard_map/all_gather | solution.py:204
  163.3 169.9 %reduce-scatter.19.cloned.1.call-start = ((), (), s32[]{:S(2)}) async-start(), calls=%async_computation.16 | async-start | bytes 4718592 | tf_op jit(solution)/shard_map/reduce_scatter | solution.py:229
  312.1 27.5 %reduce-scatter.15.cloned.1.call-start = ((), (), s32[]{:S(2)}) async-start(), calls=%async_computation.12 | async-start | bytes 4718592 | tf_op jit(solution)/shard_map/reduce_scatter | solution.py:175
  317.4 151.7 %reduce-scatter.25.cloned.1.call-start = ((), (), s32[]{:S(2)}) async-start(), calls=%async_computation.19 | async-start | bytes 1253376 | tf_op jit(solution)/shard_map/reduce_scatter | solution.py:245
  323.2 273.9 %reduce-scatter.27.cloned.1.call-start = ((), (), s32[]{:S(2)}) async-start(), calls=%async_computation.20 | async-start | bytes 1253376 | tf_op jit(solution)/shard_map/reduce_scatter | solution.py:246
  328.3 397.0 %reduce-scatter.23.cloned.1.call-start = ((), (), s32[]{:S(2)}) async-start(), calls=%async_computation.18 | async-start | bytes 1253376 | tf_op jit(solution)/shard_map/reduce_scatter | solution.py:244
  333.1 490.7 %reduce-scatter.29.cloned.1.call-start = ((), (), s32[]{:S(2)}) async-start(), calls=%async_computation.21 | async-start | bytes 405504
  353.3 609.1 %reduce-scatter.21.cloned.1.call-start = ((), (), s32[]{:S(2)}) async-start(), calls=%async_computation.17 | async-start | bytes 3760128 | tf_op jit(solution)/shard_map/reduce_scatter | solution.py:243
  362.5 648.9 %copy-start.18 = (f32[48,384]{1,0:T(8,128)S(1)}, f32[48,384]{1,0:T(8,128)}, u32[]{:S(2)}) copy-start(f32[48,384]{1,0:T(8,128)} %param.48) | copy-start | bytes 221188
  362.5 648.8 %copy-start.19 = (f32[48,384]{1,0:T(8,128)S(1)}, f32[48,384]{1,0:T(8,128)}, u32[]{:S(2)}) copy-start(f32[48,384]{1,0:T(8,128)} %param.49) | copy-start | bytes 221188
  362.5 650.4 %copy-start.15 = (f32[48,3,384]{2,0,1:T(8,128)S(1)}, f32[48,3,384]{2,0,1:T(8,128)}, u32[]{:S(2)}) copy-start(f32[48,3,384]{2,0,1:T(8,128)} %param.42) | copy-start | bytes 663556
  362.5 650.4 %copy-start.16 = (f32[48,3,384]{2,0,1:T(8,128)S(1)}, f32[48,3,384]{2,0,1:T(8,128)}, u32[]{:S(2)}) copy-start(f32[48,3,384]{2,0,1:T(8,128)} %param.43) | copy-start | bytes 663556
  362.6 650.4 %copy-start.17 = (f32[48,3,384]{2,0,1:T(8,128)S(1)}, f32[48,3,384]{2,0,1:T(8,128)}, u32[]{:S(2)}) copy-start(f32[48,3,384]{2,0,1:T(8,128)} %param.44) | copy-start | bytes 663556
  362.6 652.3 %copy-start.21 = (f32[24,768]{1,0:T(8,128)S(1)}, f32[24,768]{1,0:T(8,128)}, u32[]{:S(2)}) copy-start(f32[24,768]{1,0:T(8,128)} %param.51) | copy-start | bytes 221188
  362.6 652.3 %copy-start.22 = (f32[24,768]{1,0:T(8,128)S(1)}, f32[24,768]{1,0:T(8,128)}, u32[]{:S(2)}) copy-start(f32[24,768]{1,0:T(8,128)} %param.52) | copy-start | bytes 221188
  362.6 652.3 %copy-start.23 = (f32[24,768]{1,0:T(8,128)S(1)}, f32[24,768]{1,0:T(8,128)}, u32[]{:S(2)}) copy-start(f32[24,768]{1,0:T(8,128)} %param.53) | copy-start | bytes 221188
  362.6 652.2 %copy-start.24 = (f32[24,768]{1,0:T(8,128)S(1)}, f32[24,768]{1,0:T(8,128)}, u32[]{:S(2)}) copy-start(f32[24,768]{1,0:T(8,128)} %param.45) | copy-start | bytes 221188
  362.6 652.2 %copy-start.25 = (f32[24,768]{1,0:T(8,128)S(1)}, f32[24,768]{1,0:T(8,128)}, u32[]{:S(2)}) copy-start(f32[24,768]{1,0:T(8,128)} %param.47) | copy-start | bytes 221188
  362.6 652.2 %copy-start.26 = (f32[24,768]{1,0:T(8,128)S(1)}, f32[24,768]{1,0:T(8,128)}, u32[]{:S(2)}) copy-start(f32[24,768]{1,0:T(8,128)} %param.46) | copy-start | bytes 221188
  (30 other events, 3361.4 us)
Sparse Core Ops, SparseCore 0:
  19.9 14.8 all-gather.4
  85.6 12.0 reduce-scatter.12
  104.1 13.2 all-gather.6
  118.9 13.2 all-gather.8
  143.5 12.0 reduce-scatter.16
  163.4 13.2 all-gather.10
  312.2 12.0 reduce-scatter.18
  326.6 12.0 reduce-scatter.14
  343.5 125.5 reduce-scatter.24
  473.7 123.3 reduce-scatter.26
  601.8 123.3 reduce-scatter.22
  730.0 93.7 reduce-scatter.28
  829.7 132.5 reduce-scatter.20
where the time goes:
time: 1030 us; the launch traced here: 1020 us
  waiting for transfers between devices  614 us (60%)
  matrix products  198 us (19%)
  blocking collectives  82.2 us (8%)
  other arithmetic  58.3 us (6%)
  local copies, waits for them, and re-layouts  49.3 us (5%)
  between operations  21.3 us (2%)
    reduce_scatter x1, waiting for transfers between devices, on_device(): lax.psum_scatter(grad_qkv, 'dp', scatter_dimension=0, tiled=True)  137 us
    reduce_scatter x1, waiting for transfers between devices, on_device(): lax.psum_scatter(grad_out, 'dp', scatter_dimension=0, tiled=True)  127 us
    reduce_scatter x1, waiting for transfers between devices, on_device(): lax.psum_scatter(grad_down, 'dp', scatter_dimension=0, tiled=True)  127 us
    reduce_scatter x1, waiting for transfers between devices, on_device(): lax.psum_scatter(grad_up, 'dp', scatter_dimension=0, tiled=True)  105 us
    unnamed x14, waiting for transfers between devices  57 us
    unnamed x2, blocking collectives  42.2 us
    psum x1, blocking collectives, on_device(): total_square = lax.psum(own_square, ('dp', 'mp'))  40 us
    dot_general x4, matrix products, attention_backward(): jnp.einsum('mhqk,mqhe->mkhe', grad_scores, query_rows, preferred_element_...  31.8 us
  transfers between devices with their start and end apart: 13, of which 11 were waited for; matrix products, arithmetic and copies ran while one was open for 7% of the time, Pallas kernels for 0%

commit v1 on v0

v1 whole, which is shorter than its diff:
```python
from functools import partial
import math

import jax
import jax.numpy as jnp
from jax import lax
from jax.experimental import pallas as pl
from jax.experimental.pallas import tpu as pltpu
from jax.sharding import PartitionSpec as P

HEAD_DIM = 24
PAD_DIM = 32
STEP = 10
NORM_EPS = 1e-05
BETA_FIRST = 0.9
BETA_SECOND = 0.95
ADAM_EPS = 1e-08
MATRIX_RATE = 0.03
NORM_RATE = 0.5
EMBED_RATE = 0.05
MATRIX_DECAY = 0.1
CLIP_LIMIT = 1.0
MASK_VALUE = -1e30
SCORE_SCALE = 1.0 / math.sqrt(HEAD_DIM)
LOG2E = 1.4426950408889634
LN2 = 0.6931471805599453
IDENT_ROWS = 40
PAIR = 2
VMEM_BYTES = 60 * 1024 * 1024

F32 = jnp.float32
BF16 = jnp.bfloat16


def dot_nn(lhs, rhs):
    return lax.dot_general(lhs, rhs, (((1,), (0,)), ((), ())), preferred_element_type=F32)


def dot_nt(lhs, rhs):
    return lax.dot_general(lhs, rhs, (((1,), (1,)), ((), ())), preferred_element_type=F32)


def norm_parts(values):
    scale = 1.0 / values.shape[0]
    centred = values - jnp.sum(values, axis=0, keepdims=True) * scale
    spread = jnp.sum(centred * centred, axis=0, keepdims=True) * scale
    return centred, lax.rsqrt(spread + NORM_EPS)


def gelu_parts(x):
    size = jnp.abs(x)
    bell = jnp.exp2((-0.5 * LOG2E) * (x * x))
    t = 1.0 / (1.0 + (0.3275911 / math.sqrt(2.0)) * size)
    poly = t * (
        0.5 * 0.254829592
        + t
        * (
            0.5 * -0.284496736
            + t * (0.5 * 1.421413741 + t * (0.5 * -1.453152027 + t * (0.5 * 1.061405429)))
        )
    )
    tail = poly * bell
    share = jnp.where(x < 0.0, tail, 1.0 - tail)
    return x * share, share + x * bell * (1.0 / math.sqrt(2.0 * math.pi))


def head_rows(values, tail):
    heads = values.shape[0] // HEAD_DIM
    cut = values.reshape(heads, HEAD_DIM, values.shape[1])
    tails = jnp.broadcast_to(tail[None], (heads,) + tail.shape)
    return jnp.concatenate([cut, tails], axis=1).reshape(heads * PAD_DIM, values.shape[1])


def block_columns(rows):
    zero = jnp.zeros((PAD_DIM, rows.shape[1]), rows.dtype)
    columns = []
    for head in range(4):
        pieces = [zero] * 4
        pieces[head] = rows[head * PAD_DIM : (head + 1) * PAD_DIM]
        columns.append(jnp.concatenate(pieces, axis=0))
    return jnp.concatenate(columns, axis=1)


def front_kernel(
    len_ref,
    tok_ref,
    cot_ref,
    typ_ref,
    pair_ref,
    lap_ref,
    est_ref,
    norm_ref,
    qkv_o,
    qkv_p,
    out_o,
    out_p,
    up_o,
    up_p,
    down_o,
    down_p,
    output_ref,
    h0_ref,
    gh1_ref,
    na_ref,
    fs_ref,
    q_ref,
    k_ref,
    v_ref,
    do_ref,
    e_ref,
    gown_ref,
    gpeer_ref,
    lnacc_ref,
    qkvt,
    outt,
    upt,
    downt,
    nb,
    act_s,
    cot_s,
    nbt_s,
    gp_s,
    mix_s,
    ga_s,
    mixf,
    h1_s,
    nrm_s,
    dgel_s,
    rec_s,
):
    step = pl.program_id(0)
    steps = pl.num_programs(0)
    slots = tok_ref.shape[1]
    width = tok_ref.shape[2]
    half = width // 2
    halves = ((qkv_o, out_o, up_o, down_o), (qkv_p, out_p, up_p, down_p))

    @pl.when(step == 0)
    def _():
        for h, (qkv, out, up, down) in enumerate(halves):
            for c in range(3):
                qkvt[h, c * half : (c + 1) * half, :] = qkv[c].T
            outt[h] = out[...].T
            upt[h] = up[...].T
            downt[h] = down[...].T
        for row in range(4):
            nb[row] = jnp.broadcast_to(norm_ref[:, row : row + 1], (width, slots))
        lnacc_ref[...] = jnp.zeros_like(lnacc_ref)

    base = pl.multiple_of(step * PAIR * slots, PAIR * slots)
    span = pl.ds(base, PAIR * slots)

    node_iota = lax.broadcasted_iota(jnp.int32, (lap_ref.shape[2], slots), 0)
    row_iota = lax.broadcasted_iota(jnp.int32, (8, slots), 0)
    lane_iota = lax.broadcasted_iota(jnp.int32, (1, slots), 1)

    for j in range(PAIR):
        lanes = slice(j * slots, (j + 1) * slots)
        lap = lap_ref[j]
        lap1 = lap.astype(BF16)
        rest = lap - lap1.astype(F32)
        lap2 = rest.astype(BF16)
        lap3 = (rest - lap2.astype(F32)).astype(BF16)
        laps = jnp.concatenate([lap1.astype(F32), lap2.astype(F32), lap3.astype(F32)], axis=0)
        laps = laps.astype(BF16)
        left = jnp.where(node_iota == pair_ref[j, 0:1, :], 1.0, 0.0).astype(BF16)
        right = jnp.where(node_iota == pair_ref[j, 1:2, :], 1.0, 0.0).astype(BF16)
        lf = dot_nn(laps, left)
        rf = dot_nn(laps, right)
        types = typ_ref[j]
        kinds = jnp.where((row_iota < 2) & (row_iota == types), 1.0, 0.0)
        none = jnp.zeros((8, slots), F32)
        ident = lap.shape[0]
        f1 = jnp.concatenate([lf[0:ident], rf[0:ident], kinds], axis=0)
        f2 = jnp.concatenate([lf[ident : 2 * ident], rf[ident : 2 * ident], none], axis=0)
        f3 = jnp.concatenate([lf[2 * ident :], rf[2 * ident :], none], axis=0)
        stack = jnp.concatenate([f1, f1, f1, f2, f2, f3, none, none], axis=0).astype(BF16)
        fs_ref[:, lanes] = stack
        h0 = tok_ref[j].T.astype(F32) + dot_nn(est_ref[...], stack)
        h0_ref[:, lanes] = h0
        centred, rec = norm_parts(h0)
        na_ref[:, lanes] = (centred * rec * nb[0] + nb[1]).astype(BF16)
        cot_s[:, pl.ds(pl.multiple_of(base + j * slots, slots), slots)] = cot_ref[j].T

    one_row = jnp.where(row_iota == 0, 1.0, 0.0)
    two_rows = jnp.where(row_iota < 2, 1.0, 0.0)
    for h in range(2):
        proj = dot_nn(qkvt[h], na_ref[...])
        rows = slice(h * (half // HEAD_DIM) * PAD_DIM, (h + 1) * (half // HEAD_DIM) * PAD_DIM)
        for j in range(PAIR):
            lanes = slice(j * slots, (j + 1) * slots)
            length = len_ref[step * PAIR + j]
            bias = jnp.where(lane_iota < length, 0.0, MASK_VALUE)
            bias_row = jnp.where(row_iota == 0, bias, 0.0)
            q = proj[0:half, lanes] * (SCORE_SCALE * LOG2E)
            q_ref[j, rows, :] = head_rows(q, one_row).astype(BF16)
            k_ref[j, rows, :] = head_rows(proj[half : 2 * half, lanes], bias_row).astype(BF16)
            v_ref[j, rows, :] = head_rows(proj[2 * half :, lanes], two_rows).astype(BF16)

    groups = width // (4 * HEAD_DIM)
    for j in range(PAIR):
        lanes = slice(j * slots, (j + 1) * slots)

        def attend(g, carry, j=j, lanes=lanes):
            rows = pl.ds(pl.multiple_of(g * 4 * PAD_DIM, 4 * PAD_DIM), 4 * PAD_DIM)
            keys = k_ref[j, rows, :].T
            vals = v_ref[j, rows, :]
            scores = dot_nn(keys, block_columns(q_ref[j, rows, :]))
            mixes, recs = [], []
            for a in range(4):
                own = scores[:, a * slots : (a + 1) * slots]
                top = jnp.max(own, axis=0, keepdims=True)
                ex = jnp.exp2(own - top).astype(BF16)
                e_ref[j, g * 4 + a] = ex
                got = dot_nn(vals[a * PAD_DIM : (a + 1) * PAD_DIM], ex)
                rec = 1.0 / got[HEAD_DIM : HEAD_DIM + 1]
                rec_s[j, g, a : a + 1, :] = rec
                mixes.append(got[0:HEAD_DIM] * rec)
            out_rows = pl.ds(pl.multiple_of(g * 4 * HEAD_DIM, 4 * HEAD_DIM), 4 * HEAD_DIM)
            mixf[out_rows, lanes] = jnp.concatenate(mixes, axis=0)
            return carry

        lax.fori_loop(0, groups, attend, 0)

    mix = mixf[...].astype(BF16)
    mix_s[:, span] = mix
    attn = dot_nn(outt[0], mix[0:half]) + dot_nn(outt[1], mix[half:])
    for j in range(PAIR):
        lanes = slice(j * slots, (j + 1) * slots)
        h1 = h0_ref[:, lanes] + attn[:, lanes]
        h1_s[:, lanes] = h1
        centred, rec = norm_parts(h1)
        unit = centred * rec
        nrm_s[:, lanes] = unit
        rec_s[j, groups, 0:1, :] = rec
        nbt_s[:, pl.ds(pl.multiple_of(base + j * slots, slots), slots)] = (
            unit * nb[2] + nb[3]
        ).astype(BF16)

    for h in range(2):
        rows = slice(h * half, (h + 1) * half)
        act, slope = gelu_parts(dot_nn(upt[h], nbt_s[:, span]))
        act_s[rows, span] = act.astype(BF16)
        dgel_s[rows, :] = slope
    ffn = dot_nn(downt[0], act_s[0:half, span]) + dot_nn(downt[1], act_s[half:, span])
    for j in range(PAIR):
        lanes = slice(j * slots, (j + 1) * slots)
        output_ref[j] = (h1_s[:, lanes] + ffn[:, lanes]).astype(BF16).T

    for h in range(2):
        rows = slice(h * half, (h + 1) * half)
        back = dot_nn(halves[h][3][...], cot_s[:, span])
        gp_s[rows, span] = (back * dgel_s[rows, :]).astype(BF16)
    grad_b = dot_nn(up_o[...], gp_s[0:half, span]) + dot_nn(up_p[...], gp_s[half:, span])
    inv = 1.0 / width
    for j in range(PAIR):
        lanes = slice(j * slots, (j + 1) * slots)
        cols = pl.ds(pl.multiple_of(base + j * slots, slots), slots)
        gb = grad_b[:, lanes]
        unit = nrm_s[:, lanes]
        lnacc_ref[0] += gb * unit
        lnacc_ref[1] += gb
        f = gb * nb[2]
        f_mean = jnp.sum(f, axis=0, keepdims=True) * inv
        fn_mean = jnp.sum(f * unit, axis=0, keepdims=True) * inv
        gh1 = cot_s[:, cols].astype(F32) + rec_s[j, groups, 0:1, :] * (
            f - f_mean - unit * fn_mean
        )
        gh1_ref[:, lanes] = gh1
        ga_s[:, cols] = gh1.astype(BF16)

    for h in range(2):
        gm = dot_nn(halves[h][1][...], ga_s[:, span])
        for j in range(PAIR):
            lanes = slice(j * slots, (j + 1) * slots)
            for g in range(groups // 2):
                at = h * (groups // 2) + g
                grad = gm[g * 96 : (g + 1) * 96, lanes].reshape(4, HEAD_DIM, slots)
                mixed = mixf[at * 96 : (at + 1) * 96, lanes].reshape(4, HEAD_DIM, slots)
                rec = rec_s[j, at].reshape(8, 1, slots)[0:4]
                inner = -(jnp.sum(grad * mixed, axis=1, keepdims=True) * rec)
                high = inner.astype(BF16).astype(F32)
                low = inner - high
                rows8 = lax.broadcasted_iota(jnp.int32, (4, 8, slots), 1)
                tail = jnp.where(rows8 == 0, high, jnp.where(rows8 == 1, low, 0.0))
                full = jnp.concatenate([grad * rec, tail], axis=1)
                do_ref[j, at * 128 : (at + 1) * 128, :] = (
                    full.reshape(4 * PAD_DIM, slots).astype(BF16)
                )

    @pl.when(step == steps - 1)
    def _():
        owners = gown_ref.shape[0]
        some = half // owners
        for h, g_ref in enumerate((gown_ref, gpeer_ref)):
            rows = slice(h * half, (h + 1) * half)
            gdown = dot_nt(act_s[rows, :], cot_s[...])
            gout = dot_nt(mix_s[rows, :], ga_s[...])
            for o in range(owners):
                both = jnp.concatenate(
                    [gdown[o * some : (o + 1) * some], gout[o * some : (o + 1) * some]], axis=0
                )
                g_ref[o, :, 0:width] = both.astype(g_ref.dtype)
            gup = dot_nt(nbt_s[...], gp_s[rows, :])
            g_ref[:, :, width:] = gup.reshape(owners, 2 * some, half).astype(g_ref.dtype)


def middle_kernel(na_ref, q_ref, k_ref, v_ref, do_ref, e_ref, dx_ref, g_ref):
    step = pl.program_id(0)
    steps = pl.num_programs(0)
    slots = q_ref.shape[2]
    half = dx_ref.shape[0] // 3
    base = pl.multiple_of(step * PAIR * slots, PAIR * slots)
    groups = half // (4 * HEAD_DIM)
    for j in range(PAIR):
        cols = pl.ds(pl.multiple_of(base + j * slots, slots), slots)

        def attend(g, carry, j=j, cols=cols):
            rows = pl.ds(pl.multiple_of(g * 4 * PAD_DIM, 4 * PAD_DIM), 4 * PAD_DIM)
            vals = v_ref[j, rows, :].T
            dos = do_ref[j, rows, :]
            qs = q_ref[j, rows, :]
            ks = k_ref[j, rows, :]
            back = dot_nn(vals, block_columns(dos))
            dq, dk, dv = [], [], []
            for a in range(4):
                cut = slice(a * PAD_DIM, (a + 1) * PAD_DIM)
                ex = e_ref[j, g * 4 + a]
                ds = (ex.astype(F32) * back[:, a * slots : (a + 1) * slots]).astype(BF16)
                dq.append(dot_nn(ks[cut], ds)[0:HEAD_DIM])
                dk.append(dot_nt(qs[cut], ds)[0:HEAD_DIM])
                dv.append(dot_nt(dos[cut], ex)[0:HEAD_DIM])
            for c, (parts, scale) in enumerate(((dq, SCORE_SCALE), (dk, LN2), (dv, None))):
                at = pl.ds(pl.multiple_of(c * half + g * 96, 32), 96)
                whole = jnp.concatenate(parts, axis=0)
                if scale is not None:
                    whole = whole * scale
                dx_ref[at, cols] = whole.astype(BF16)
            return carry

        lax.fori_loop(0, groups, attend, 0)

    @pl.when(step == steps - 1)
    def _():
        for c in range(3):
            grad = dot_nt(na_ref[...], dx_ref[c * half : (c + 1) * half, :])
            g_ref[:, :, c * half : (c + 1) * half] = grad.reshape(
                g_ref.shape[0], g_ref.shape[1], half
            ).astype(g_ref.dtype)


def back_kernel(
    dxo_ref, dxp_ref, qkv_o, qkv_p, h0_ref, gh1_ref, fs_ref, gain_ref, ig_ref, lnacc_ref, ge_ref, nb
):
    step = pl.program_id(0)
    slots = ig_ref.shape[1]
    width = ig_ref.shape[2]
    half = width // 2
    inv = 1.0 / width

    @pl.when(step == 0)
    def _():
        lnacc_ref[...] = jnp.zeros_like(lnacc_ref)
        ge_ref[...] = jnp.zeros_like(ge_ref)
        nb[...] = jnp.broadcast_to(gain_ref[:, 0:1], (width, slots))

    total = None
    for qkv, dx in ((qkv_o, dxo_ref), (qkv_p, dxp_ref)):
        for c in range(3):
            part = dot_nn(qkv[c], dx[c * half : (c + 1) * half, :])
            total = part if total is None else total + part
    for j in range(PAIR):
        lanes = slice(j * slots, (j + 1) * slots)
        ga = total[:, lanes]
        centred, rec = norm_parts(h0_ref[:, lanes])
        unit = centred * rec
        lnacc_ref[0] += ga * unit
        lnacc_ref[1] += ga
        f = ga * nb[...]
        f_mean = jnp.sum(f, axis=0, keepdims=True) * inv
        fn_mean = jnp.sum(f * unit, axis=0, keepdims=True) * inv
        ig = gh1_ref[:, lanes] + rec * (f - f_mean - unit * fn_mean)
        ig_ref[j] = ig.T
        high = ig.astype(BF16)
        rest = ig - high.astype(F32)
        low = rest.astype(BF16)
        least = (rest - low.astype(F32)).astype(BF16)
        fs = fs_ref[:, lanes]
        ge_ref[...] += dot_nt(high, fs) + dot_nt(low, fs) + dot_nt(least, fs)


def whole_spec(shape):
    zeros = (0,) * len(shape)
    return pl.BlockSpec(shape, lambda i: zeros, pipeline_mode=pl.Buffered(1))


def front(lengths, tokens, cotangent, token_types, pairs_t, lap_t, est, norm_t, own, peer):
    mols, slots, width = tokens.shape
    half = width // 2
    heads = width // HEAD_DIM
    toks = mols * slots
    steps = mols // PAIR
    owners = 16
    lead = lambda *rest: pl.BlockSpec((PAIR,) + rest, lambda i: (i,) + (0,) * len(rest))
    col = lambda rows: pl.BlockSpec((rows, PAIR * slots), lambda i: (0, i))
    weights = []
    for pair in zip(own, peer):
        weights += list(pair)
    gshape = (owners, 2 * half // owners, 3 * half)
    outs = [
        (jax.ShapeDtypeStruct((mols, slots, width), BF16), lead(slots, width)),
        (jax.ShapeDtypeStruct((width, toks), F32), col(width)),
        (jax.ShapeDtypeStruct((width, toks), F32), col(width)),
        (jax.ShapeDtypeStruct((width, toks), BF16), col(width)),
        (jax.ShapeDtypeStruct((256, toks), BF16), col(256)),
        (jax.ShapeDtypeStruct((mols, heads * PAD_DIM, slots), BF16), lead(heads * PAD_DIM, slots)),
        (jax.ShapeDtypeStruct((mols, heads * PAD_DIM, slots), BF16), lead(heads * PAD_DIM, slots)),
        (jax.ShapeDtypeStruct((mols, heads * PAD_DIM, slots), BF16), lead(heads * PAD_DIM, slots)),
        (jax.ShapeDtypeStruct((mols, heads * PAD_DIM, slots), BF16), lead(heads * PAD_DIM, slots)),
        (jax.ShapeDtypeStruct((mols, heads, slots, slots), BF16), lead(heads, slots, slots)),
        (jax.ShapeDtypeStruct(gshape, F32), whole_spec(gshape)),
        (jax.ShapeDtypeStruct(gshape, BF16), whole_spec(gshape)),
        (jax.ShapeDtypeStruct((2, width, slots), F32), whole_spec((2, width, slots))),
    ]
    return pl.pallas_call(
        front_kernel,
        grid=(steps,),
        out_shape=[o[0] for o in outs],
        out_specs=[o[1] for o in outs],
        in_specs=[
            pl.BlockSpec(memory_space=pltpu.SMEM),
            lead(slots, width),
            lead(slots, width),
            lead(1, slots),
            lead(2, slots),
            lead(lap_t.shape[1], lap_t.shape[2]),
            whole_spec(est.shape),
            whole_spec(norm_t.shape),
        ]
        + [whole_spec(w.shape) for w in weights],
        scratch_shapes=[
            pltpu.VMEM((2, 3 * half, width), BF16),
            pltpu.VMEM((2, width, half), BF16),
            pltpu.VMEM((2, half, width), BF16),
            pltpu.VMEM((2, width, half), BF16),
            pltpu.VMEM((4, width, slots), F32),
        ]
        + [pltpu.VMEM((width, toks), BF16)] * 6
        + [pltpu.VMEM((width, PAIR * slots), F32)] * 4
        + [pltpu.VMEM((PAIR, heads // 4 + 1, 8, slots), F32)],
        compiler_params=pltpu.CompilerParams(vmem_limit_bytes=VMEM_BYTES),
        cost_estimate=pl.CostEstimate(
            flops=2 * toks * width * width * 15, bytes_accessed=50_000_000, transcendentals=0
        ),
        name="front",
    )(
        lengths,
        tokens,
        cotangent,
        token_types.reshape(mols, 1, slots),
        pairs_t,
        lap_t,
        est,
        norm_t,
        *weights,
    )


def middle(which, dtype, na, q, k, v, do, e):
    mols, heads, slots, _ = e.shape
    width, toks = na.shape
    half = width // 2
    rows = heads // 2 * PAD_DIM
    part = pl.BlockSpec((PAIR, rows, slots), lambda i: (i, which, 0))
    gshape = (16, width // 16, 3 * half)
    return pl.pallas_call(
        middle_kernel,
        grid=(mols // PAIR,),
        out_shape=[
            jax.ShapeDtypeStruct((3 * half, toks), BF16),
            jax.ShapeDtypeStruct(gshape, dtype),
        ],
        in_specs=[
            whole_spec(na.shape),
            part,
            part,
            part,
            part,
            pl.BlockSpec((PAIR, heads // 2, slots, slots), lambda i: (i, which, 0, 0)),
        ],
        out_specs=[whole_spec((3 * half, toks)), whole_spec(gshape)],
        compiler_params=pltpu.CompilerParams(vmem_limit_bytes=VMEM_BYTES),
        cost_estimate=pl.CostEstimate(
            flops=2 * toks * width * width * 5, bytes_accessed=12_000_000, transcendentals=0
        ),
        name="middle",
    )(na, q, k, v, do, e)


def back(dxo, dxp, qkv_o, qkv_p, h0, gh1, fs, gain, mols):
    width, toks = h0.shape
    slots = toks // mols
    col = lambda rows: pl.BlockSpec((rows, PAIR * slots), lambda i: (0, i))
    return pl.pallas_call(
        back_kernel,
        grid=(mols // PAIR,),
        out_shape=[
            jax.ShapeDtypeStruct((mols, slots, width), F32),
            jax.ShapeDtypeStruct((2, width, slots), F32),
            jax.ShapeDtypeStruct((width, 256), F32),
        ],
        in_specs=[
            col(dxo.shape[0]),
            col(dxo.shape[0]),
            whole_spec(qkv_o.shape),
            whole_spec(qkv_p.shape),
            col(width),
            col(width),
            col(256),
            whole_spec(gain.shape),
        ],
        out_specs=[
            pl.BlockSpec((PAIR, slots, width), lambda i: (i, 0, 0)),
            whole_spec((2, width, slots)),
            whole_spec((width, 256)),
        ],
        scratch_shapes=[pltpu.VMEM((width, slots), F32)],
        compiler_params=pltpu.CompilerParams(vmem_limit_bytes=VMEM_BYTES),
        cost_estimate=pl.CostEstimate(
            flops=2 * toks * width * width * 4, bytes_accessed=15_000_000, transcendentals=0
        ),
        name="back",
    )(dxo, dxp, qkv_o, qkv_p, h0, gh1, fs, gain)


def swap(value):
    return lax.ppermute(value, "mp", [(0, 1), (1, 0)])


def hop(value, flip):
    size = lax.axis_size("dp")
    return lax.ppermute(value, "dp", [(i, i ^ flip) for i in range(size)])


def take(value, index, axis=0):
    return lax.dynamic_index_in_dim(value, index, axis, keepdims=False)


def exchange(value, mine, count, stride):
    total = take(value, mine).astype(F32)
    for k in range(1, count):
        total = total + hop(take(value, mine ^ k), k * stride).astype(F32)
    return total


def reduce_owned(value):
    index = lax.axis_index("dp")
    plane, line = index & 3, index >> 2
    rows, columns = value.shape[1:]
    cut = columns * 7 // 9 // 128 * 128
    first = value[:, :, :cut].reshape(4, 4, rows, cut).swapaxes(0, 1)
    first = exchange(first, plane, 4, 1).astype(BF16)
    first = exchange(first, line, 4, 4)
    second = value[:, :, cut:].reshape(4, 4, rows, columns - cut)
    second = exchange(second, line, 4, 4).astype(BF16)
    second = exchange(second, plane, 4, 1)
    return jnp.concatenate([first, second], axis=1)


def adam_step(master, mean_old, square_old, gradient, rate, decay, clip_scale):
    clipped = gradient * clip_scale
    mean_new = BETA_FIRST * mean_old + (1.0 - BETA_FIRST) * clipped
    square_new = BETA_SECOND * square_old + (1.0 - BETA_SECOND) * clipped * clipped
    mean_hat = mean_new / (1.0 - BETA_FIRST**STEP)
    square_hat = square_new / (1.0 - BETA_SECOND**STEP)
    updated = master - rate * (mean_hat / (jnp.sqrt(square_hat) + ADAM_EPS) + decay * master)
    return (updated, mean_new, square_new)


def on_device(
    tokens,
    cotangent,
    lengths,
    token_types,
    node_pairs,
    laplacian,
    qkv_weight,
    out_weight,
    up_weight,
    down_weight,
    qkv_master,
    qkv_mean,
    qkv_square,
    out_master,
    out_mean,
    out_square,
    up_master,
    up_mean,
    up_square,
    down_master,
    down_mean,
    down_square,
    norm_params,
    norm_mean,
    norm_square,
    embed_weight,
    embed_mean,
    embed_square,
):
    mols, slots, width = tokens.shape
    half = width // 2
    dp_size = lax.axis_size("dp")
    mp_size = lax.axis_size("mp")
    idents = embed_weight.shape[0]

    own = (qkv_weight.transpose(1, 0, 2), out_weight, up_weight, down_weight)
    peer = tuple(swap(w) for w in own)

    embed_rows = jnp.pad(embed_weight, ((0, IDENT_ROWS - idents), (0, 0)))
    e1 = lax.reduce_precision(embed_rows, 8, 7)
    e2 = lax.reduce_precision(embed_rows - e1, 8, 7)
    e3 = embed_rows - e1 - e2
    blank = jnp.zeros((256 - 6 * IDENT_ROWS, width), F32)
    est = jnp.concatenate([e1, e2, e3, e1, e2, e1, blank], axis=0).astype(BF16).T
    norm_t = norm_params.T

    (output, h0, gh1, na, fs, q, k, v, do, e, gown1, gpeer1, lnacc_b) = front(
        lengths,
        tokens,
        cotangent,
        token_types,
        node_pairs.transpose(0, 2, 1),
        laplacian.transpose(0, 2, 1),
        est,
        norm_t,
        own,
        peer,
    )
    sum1 = gown1 + swap(gpeer1).astype(F32)
    dxp, gpeer2 = middle(1, BF16, na, q, k, v, do, e)
    got2 = swap(gpeer2)
    dxo, gown2 = middle(0, F32, na, q, k, v, do, e)
    sum2 = gown2 + got2.astype(F32)
    input_grad, lnacc_a, gembed = back(
        dxo, dxp, own[0], peer[0], h0, gh1, fs, norm_t, mols
    )

    if dp_size == 16:
        red1 = reduce_owned(sum1.astype(BF16))
        red2 = reduce_owned(sum2.astype(BF16))
        some = half // dp_size
        reduced_down = red1[0:some, 0:width]
        reduced_out = red1[some:, 0:width]
        reduced_up = red1[:, width:]
        reduced_qkv = red2.reshape(2 * some, 3, half)
    else:
        some = half // 16
        scatter = partial(lax.psum_scatter, axis_name="dp", scatter_dimension=0, tiled=True)
        reduced_down = scatter(sum1[:, 0:some, 0:width].reshape(half, width))
        reduced_out = scatter(sum1[:, some:, 0:width].reshape(half, width))
        reduced_up = scatter(sum1[:, :, width:].reshape(width, half))
        reduced_qkv = scatter(sum2.reshape(width, 3, half))

    i1, i2, i3 = 0, 3 * IDENT_ROWS, 5 * IDENT_ROWS
    grad_embed = (
        gembed[:, i1 : i1 + idents] + gembed[:, i2 : i2 + idents] + gembed[:, i3 : i3 + idents]
    )
    small = jnp.concatenate(
        [jnp.sum(lnacc_a, axis=2).T, jnp.sum(lnacc_b, axis=2).T, grad_embed], axis=1
    )
    world = dp_size * mp_size
    shard_width = width // world
    small = small.reshape(world, shard_width, small.shape[1])
    got = lax.all_to_all(small, ("dp", "mp"), 0, 0, tiled=True)
    small_own = jnp.sum(got, axis=0).T
    reduced_norm = small_own[0:4]
    reduced_embed = small_own[4:]

    own_square = (
        jnp.sum(reduced_qkv * reduced_qkv)
        + jnp.sum(reduced_out * reduced_out)
        + jnp.sum(reduced_up * reduced_up)
        + jnp.sum(reduced_down * reduced_down)
        + jnp.sum(small_own * small_own)
    )
    squares = jnp.broadcast_to(own_square, (world, 1))
    total_square = jnp.sum(lax.all_to_all(squares, ("dp", "mp"), 0, 0, tiled=True))
    clip_norm = jnp.sqrt(total_square)
    clip_scale = jnp.minimum(1.0, CLIP_LIMIT / (clip_norm + 1e-06))
    shard_index = lax.axis_index("dp") * mp_size + lax.axis_index("mp")
    norm_own = lax.dynamic_slice_in_dim(norm_params, shard_index * shard_width, shard_width, 1)
    embed_own = lax.dynamic_slice_in_dim(embed_weight, shard_index * shard_width, shard_width, 1)
    qkv_new = adam_step(
        qkv_master, qkv_mean, qkv_square, reduced_qkv, MATRIX_RATE, MATRIX_DECAY, clip_scale
    )
    out_new = adam_step(
        out_master, out_mean, out_square, reduced_out, MATRIX_RATE, MATRIX_DECAY, clip_scale
    )
    up_new = adam_step(
        up_master, up_mean, up_square, reduced_up, MATRIX_RATE, MATRIX_DECAY, clip_scale
    )
    down_new = adam_step(
        down_master, down_mean, down_square, reduced_down, MATRIX_RATE, MATRIX_DECAY, clip_scale
    )
    norm_new = adam_step(norm_own, norm_mean, norm_square, reduced_norm, NORM_RATE, 0.0, clip_scale)
    embed_new = adam_step(
        embed_own, embed_mean, embed_square, reduced_embed, EMBED_RATE, 0.0, clip_scale
    )
    return (output, input_grad, clip_norm) + (
        qkv_new + out_new + up_new + down_new + norm_new + embed_new
    )


def solution(mesh):
    tokens = P(("dp", "mp"), None, None)
    qkv = P("dp", None, "mp")
    rows = P(("mp", "dp"), None)
    both = P("dp", "mp")
    small = P(None, ("dp", "mp"))
    return jax.shard_map(
        on_device,
        mesh=mesh,
        in_specs=(
            tokens,
            tokens,
            P(("dp", "mp")),
            P(("dp", "mp"), None),
            tokens,
            tokens,
            P(None, None, "mp"),
            P("mp", None),
            P(None, "mp"),
            P("mp", None),
        )
        + (qkv,) * 3
        + (rows,) * 3
        + (both,) * 3
        + (rows,) * 3
        + (P(), small, small) * 2,
        out_specs=(tokens, tokens, P())
        + (qkv,) * 3
        + (rows,) * 3
        + (both,) * 3
        + (rows,) * 3
        + (small,) * 6,
        check_vma=False,
    )
```

time: 1030 us -> 276 us (0.27)
  waiting for transfers between devices: 614 us -> 52.8 us
  matrix products: 198 us -> 0 us
  Pallas kernels: 0 us -> 131 us
  blocking collectives: 82.2 us -> 0 us
  starting transfers between devices: 1.58 us -> 43.2 us
  other arithmetic: 58.3 us -> 22.2 us
  local copies, waits for them, and re-layouts: 49.3 us -> 19.6 us
  between operations: 21.3 us -> 6.23 us
    reduce_scatter x8 -> x0, waiting for transfers between devices: 520 us -> none  [the longest x1 137 us: on_device(): lax.psum_scatter(grad_qkv, 'dp', scatter_dimension=0, tiled=True)]
    dot_general x44 -> x0, matrix products: 198 us -> none  [the longest x4 31.8 us: attention_backward(): jnp.einsum('mhqk,mqhe->mkhe', grad_scores, query_rows, preferred_element_...]
    pallas_call x0 -> x4, Pallas kernels: none -> 131 us  [the longest x1 66.9 us: front(): pl.pallas_call(front_kernel, grid=(steps,), out_shape=[o[0] for o in outs...]
    unnamed x14 -> x0, waiting for transfers between devices: 57 us -> none
    unnamed x2 -> x0, blocking collectives: 42.2 us -> none
    psum x1 -> x0, blocking collectives: 40 us -> none  [on_device(): total_square = lax.psum(own_square, ('dp', 'mp'))]
    ppermute x0 -> x30, waiting for transfers between devices: none -> 38 us  [the longest x24 36.6 us: hop(): return lax.ppermute(value, 'dp', [(i, i ^ flip) for i in range(size)])]
    all_gather x4 -> x0, waiting for transfers between devices: 37.8 us -> none  [the longest x1 13.2 us: on_device(): lax.all_gather(grad_h1.astype(jnp.bfloat16), 'mp', axis=0, tiled=True)]
  transfers between devices with their start and end apart: 13 -> 32, of which waited for: 11 -> 15; matrix products, arithmetic and copies ran while one was open for 7% -> 10% of each run, Pallas kernels for 0% -> 23%
where the time goes in v1:
time: 276 us; the launch traced here: 275 us
  Pallas kernels  131 us (47%)
  waiting for transfers between devices  52.8 us (19%)
  starting transfers between devices  43.2 us (16%)
  other arithmetic  22.2 us (8%)
  local copies, waits for them, and re-layouts  19.6 us (7%)
  between operations  6.23 us (2%)
    pallas_call x1, Pallas kernels, front(): pl.pallas_call(front_kernel, grid=(steps,), out_shape=[o[0] for o in outs...  66.9 us
    pallas_call x2, Pallas kernels, middle(): pl.pallas_call(middle_kernel, grid=(mols // PAIR,), out_shape=[jax.ShapeD...  45.4 us
    ppermute x24, waiting for transfers between devices, hop(): return lax.ppermute(value, 'dp', [(i, i ^ flip) for i in range(size)])  36.6 us
    ppermute x24, starting transfers between devices, hop(): return lax.ppermute(value, 'dp', [(i, i ^ flip) for i in range(size)])  30.4 us
    pallas_call x1, Pallas kernels, back(): pl.pallas_call(back_kernel, grid=(mols // PAIR,), out_shape=[jax.ShapeDty...  18.9 us
    unnamed x54, local copies, waits for them, and re-layouts  12.9 us
    all_to_all x1, waiting for transfers between devices, on_device(): got = lax.all_to_all(small, ('dp', 'mp'), 0, 0, tiled=True)  7.94 us
    all_to_all x1, starting transfers between devices, on_device(): got = lax.all_to_all(small, ('dp', 'mp'), 0, 0, tiled=True)  7.45 us
  transfers between devices with their start and end apart: 32, of which 15 were waited for; matrix products, arithmetic and copies ran while one was open for 10% of the time, Pallas kernels for 23%

profile of v1, /device:TPU:0, one launch (start us, length us, event | category | flops | bytes accessed | tf_op | source)
XLA Modules:
  0.0 275.3 jit_solution(342486223539213820)
XLA Ops:
  8.6 66.9 %front.1 = (bf16[8,128,768]{2,1,0:T(8,128)(2,1)}, f32[768,1024]{1,0:T(8,128)}, f32[768,1024]{1,0:T(8,128)}, bf16[768,1024]{1,0:T(8,128)(2,1)}, bf16[256,1024]{1,...) custom-call(s32[8]{0:T(128)} %len_ref.1, ...), custom_call_target="tpu_custom_call" | custom-call | flops 18119393280 | bytes 50000000 | tf_op jit(solution)/shard_map/front/pallas_call | solution.py:425
  76.0 22.5 %middle.3 = (bf16[1152,1024]{1,0:T(8,128)(2,1)}, bf16[16,48,1152]{2,1,0:T(8,128)(2,1)}) custom-call(bf16[768,1024]{1,0:T(8,128)(2,1)} %get-tuple-element.42.na_ref, bf16[8,1024,128]{2,1,0:T(8,128)(2,1)} %get-tuple-element.43.q_ref, bf16[8,1024,128]{2,1,0:T(8,128)(2,1)} %get-tuple-element.44.k_ref, bf16[8,1024,128]{2,1,0:T(8,128)(2,1)} %get-tuple-element.45.v_ref, ...), custom_call_target="tpu_custom_call" | custom-call | flops 6039797760 | bytes 12000000 | tf_op jit(solution)/shard_map/middle/pallas_call | solution.py:476
  99.0 23.0 %middle.2 = (bf16[1152,1024]{1,0:T(8,128)(2,1)}, f32[16,48,1152]{2,1,0:T(8,128)}) custom-call(bf16[768,1024]{1,0:T(8,128)(2,1)} %get-tuple-element.42.na_ref, bf16[8,1024,128]{2,1,0:T(8,128)(2,1)} %get-tuple-element.43.q_ref, bf16[8,1024,128]{2,1,0:T(8,128)(2,1)} %get-tuple-element.44.k_ref, bf16[8,1024,128]{2,1,0:T(8,128)(2,1)} %get-tuple-element.45.v_ref, ...), custom_call_target="tpu_custom_call" | custom-call | flops 6039797760 | bytes 12000000 | tf_op jit(solution)/shard_map/middle/pallas_call | solution.py:476
  122.0 18.9 %back.1 = (f32[8,128,768]{2,1,0:T(8,128)}, f32[2,768,128]{2,1,0:T(8,128)}, f32[768,256]{1,0:T(8,128)}) custom-call(bf16[1152,1024]{1,0:T(8,128)(2,1)} %get-tuple-element.48.dxo_ref, bf16[1152,1024]{1,0:T(8,128)(2,1)} %get-tuple-element.49.dxp_ref, bf16[3,768,384]{2,1,0:T(8,128)(2,1)} %bitcast.118, bf16[3,768,384]{2,1,0:T(8,128)(2,1)} %copy-done.20, ...), custom_call_target="tpu_custom_call" | custom-call | flops 4831838208 | bytes 15000000 | tf_op jit(solution)/shard_map/back/pallas_call | solution.py:504
  142.3 2.5 slice_add_fusion
  148.2 1.8 copy.197
  150.0 2.2 reshape.112
  152.2 7.5 %all-to-all-start = ((f32[32,1,912]{2,1,0:T(1,128)}), f32[32,1,912]{2,1,0:T(1,128)}, u32[]{:S(2)}, u32[]{:S(2)}) async-start(f32[32,1,912]{2,1,0:T(1,128)} %reshape.112), calls=%async_computation | async-start | bytes 262144 | tf_op jit(solution)/shard_map/all_to_all | solution.py:674
  159.7 7.9 %all-to-all-done = f32[32,1,912]{2,1,0:T(1,128)} async-done(((f32[32,1,912]{2,1,0:T(1,128)}), f32[32,1,912]{2,1,0:T(1,128)}, u32[]{:S(2)}, u32[]{:S(2)}) %all-to-all-start) | async-done | bytes 116768 | tf_op jit(solution)/shard_map/all_to_all | solution.py:674
  168.2 2.5 reduce.3
  170.7 1.8 reshape.113
  177.6 1.8 copy-done.1
  189.6 3.3 %collective-permute-start.12 = (bf16[4,48,256]{2,1,0:T(8,128)(2,1)S(1)}, bf16[4,48,256]{2,1,0:T(8,128)(2,1)S(1)}, u32[]{:S(2)}, u32[]{:S(2)}) collective-permute-start(bf16[4,48,256]{2,1,0:T(8,128)(2,1)S(1)} %get-tuple-element.262), channel_id=1, source_target_pairs={{0,16},{2,18},{4,20},{6,22},{8,24},{10,26},{12,28},{14,30},{16,0},... | collective-permute-start | bytes 294920 | tf_op jit(solution)/shard_map/ppermute | solution.py:542
  192.9 5.0 %collective-permute-done.25 = bf16[4,48,256]{2,1,0:T(8,128)(2,1)S(1)} collective-permute-done((bf16[4,48,256]{2,1,0:T(8,128)(2,1)S(1)}, bf16[4,48,256]{2,1,0:T(8,128)(2,1)S(1)}, u32[]{:S(2)}, u32[]{:S(2)}) %collective-permute-start.25) | collective-permute-done | bytes 98336 | tf_op jit(solution)/shard_map/ppermute | solution.py:542
  208.4 5.3 %collective-permute-done.16 = bf16[48,256]{1,0:T(8,128)(2,1)S(1)} collective-permute-done((bf16[48,256]{1,0:T(8,128)(2,1)S(1)}, bf16[48,256]{1,0:T(8,128)(2,1)S(1)}, u32[]{:S(2)}, u32[]{:S(2)}) %collective-permute-start.16) | collective-permute-done | bytes 24608 | tf_op jit(solution)/shard_map/ppermute | solution.py:542
  215.2 6.1 %collective-permute-done.15 = bf16[48,256]{1,0:T(8,128)(2,1)S(1)} collective-permute-done((bf16[48,256]{1,0:T(8,128)(2,1)S(1)}, bf16[48,256]{1,0:T(8,128)(2,1)S(1)}, u32[]{:S(2)}, u32[]{:S(2)}) %collective-permute-start.15) | collective-permute-done | bytes 24608 | tf_op jit(solution)/shard_map/ppermute | solution.py:542
  224.0 2.0 collective-permute-start.23
  227.5 4.5 %collective-permute-done.7 = bf16[4,48,896]{2,1,0:T(8,128)(2,1)S(1)} collective-permute-done((bf16[4,48,896]{2,1,0:T(8,128)(2,1)S(1)}, bf16[4,48,896]{2,1,0:T(8,128)(2,1)S(1)}, u32[]{:S(2)}, u32[]{:S(2)}) %collective-permute-start.7) | collective-permute-done | bytes 344096 | tf_op jit(solution)/shard_map/ppermute | solution.py:542
  232.0 7.3 %collective-permute-done.6 = bf16[4,48,896]{2,1,0:T(8,128)(2,1)S(1)} collective-permute-done((bf16[4,48,896]{2,1,0:T(8,128)(2,1)S(1)}, bf16[4,48,896]{2,1,0:T(8,128)(2,1)S(1)}, u32[]{:S(2)}, u32[]{:S(2)}) %collective-permute-start.6) | collective-permute-done | bytes 344096 | tf_op jit(solution)/shard_map/ppermute | solution.py:542
  239.7 2.4 collective-permute-start.10
  244.5 2.6 collective-permute-done.10
  247.1 3.8 %collective-permute-done.9 = bf16[48,896]{1,0:T(8,128)(2,1)S(1)} collective-permute-done((bf16[48,896]{1,0:T(8,128)(2,1)S(1)}, bf16[48,896]{1,0:T(8,128)(2,1)S(1)}, u32[]{:S(2)}, u32[]{:S(2)}) %collective-permute-start.9) | collective-permute-done | bytes 86048 | tf_op jit(solution)/shard_map/ppermute | solution.py:542
  255.4 3.5 %all-to-all-start.1 = ((f32[32,1,1]{2,1,0:T(1,128)}), f32[32,1,1]{2,1,0:T(1,128)S(1)}, u32[]{:S(2)}, u32[]{:S(2)}) async-start(f32[32,1,1]{2,1,0:T(1,128)} %broadcast_in_dim.7), calls=%async_computation.1 | async-start | bytes 32768 | tf_op jit(solution)/shard_map/all_to_all | solution.py:687
  259.1 6.9 %all-to-all-done.1 = f32[32,1,1]{2,1,0:T(1,128)S(1)} async-done(((f32[32,1,1]{2,1,0:T(1,128)}), f32[32,1,1]{2,1,0:T(1,128)S(1)}, u32[]{:S(2)}, u32[]{:S(2)}) %all-to-all-start.1) | async-done | bytes 160 | tf_op jit(solution)/shard_map/all_to_all | solution.py:687
  (144 shorter events, 57.3 us)
Async XLA Ops:
  0.7 6.7 %collective-permute-start = (bf16[3,768,384]{2,1,0:T(8,128)(2,1)}, bf16[3,768,384]{2,1,0:T(8,128)(2,1)S(1)}, u32[]{:S(2)}, u32[]{:S(2)}) collective-permute-start(bf16[3,768,384]{2,1,0:T(8,128)(2,1)} %bitcast.116), channel_id=1, source_target_pairs={{0,1},{1,0},{2,3},{3,2},{4,5},{5,4},{6,7},{7,6},{8,9},{9,8},{10,11... | collective-permute-start | bytes 5308424 | tf_op jit(solution)/shard_map/ppermute | solution.py:537
  75.6 100.0 %collective-permute-start.17 = (bf16[16,48,1152]{2,1,0:T(8,128)(2,1)}, bf16[16,48,1152]{2,1,0:T(8,128)(2,1)}, u32[]{:S(2)}, u32[]{:S(2)}) collective-permute-start(bf16[16,48,1152]{2,1,0:T(8,128)(2,1)} %get-tuple-element.57), channel_id=1, source_target_pairs={{0,1},{1,0},{2,3},{3,2},{4,5},{5,4},{6,7},{7,6},{8,9},{9,8},{10,11... | collective-permute-start | bytes 5308424 | tf_op jit(solution)/shard_map/ppermute | solution.py:537
  98.5 79.1 %collective-permute-start.4 = (bf16[16,48,1152]{2,1,0:T(8,128)(2,1)}, bf16[16,48,1152]{2,1,0:T(8,128)(2,1)}, u32[]{:S(2)}, u32[]{:S(2)}) collective-permute-start(bf16[16,48,1152]{2,1,0:T(8,128)(2,1)} %get-tuple-element.55), channel_id=1, source_target_pairs={{0,1},{1,0},{2,3},{3,2},{4,5},{5,4},{6,7},{7,6},{8,9},{9,8},{10,11... | collective-permute-start | bytes 5308424 | tf_op jit(solution)/shard_map/ppermute | solution.py:537
  152.2 15.4 %all-to-all-start = ((f32[32,1,912]{2,1,0:T(1,128)}), f32[32,1,912]{2,1,0:T(1,128)}, u32[]{:S(2)}, u32[]{:S(2)}) async-start(f32[32,1,912]{2,1,0:T(1,128)} %reshape.112), calls=%async_computation | async-start | bytes 262144 | tf_op jit(solution)/shard_map/all_to_all | solution.py:674
  182.1 7.5 %collective-permute-start.26 = (bf16[4,48,256]{2,1,0:T(8,128)(2,1)S(1)}, bf16[4,48,256]{2,1,0:T(8,128)(2,1)S(1)}, u32[]{:S(2)}, u32[]{:S(2)}) collective-permute-start(bf16[4,48,256]{2,1,0:T(8,128)(2,1)S(1)} %get-tuple-element.258), channel_id=1, source_target_pairs={{0,24},{2,26},{4,28},{6,30},{8,16},{10,18},{12,20},{14,22},{16,8},... | collective-permute-start | bytes 294920 | tf_op jit(solution)/shard_map/ppermute | solution.py:542
  183.7 14.2 %collective-permute-start.25 = (bf16[4,48,256]{2,1,0:T(8,128)(2,1)S(1)}, bf16[4,48,256]{2,1,0:T(8,128)(2,1)S(1)}, u32[]{:S(2)}, u32[]{:S(2)}) collective-permute-start(bf16[4,48,256]{2,1,0:T(8,128)(2,1)S(1)} %get-tuple-element.259), channel_id=1, source_target_pairs={{0,16},{2,18},{4,20},{6,22},{8,24},{10,26},{12,28},{14,30},{16,0},... | collective-permute-start | bytes 294920 | tf_op jit(solution)/shard_map/ppermute | solution.py:542
  185.1 37.3 %collective-permute-start.18 = (bf16[4,48,896]{2,1,0:T(8,128)(2,1)S(1)}, bf16[4,48,896]{2,1,0:T(8,128)(2,1)S(1)}, u32[]{:S(2)}, u32[]{:S(2)}) collective-permute-start(bf16[4,48,896]{2,1,0:T(8,128)(2,1)S(1)} %get-tuple-element.251), channel_id=1, source_target_pairs={{0,2},{2,0},{4,6},{6,4},{8,10},{10,8},{12,14},{14,12},{16,18},{18,... | collective-permute-start | bytes 1032200 | tf_op jit(solution)/shard_map/ppermute | solution.py:542
  185.6 14.0 %collective-permute-start.11 = (bf16[4,48,256]{2,1,0:T(8,128)(2,1)S(1)}, bf16[4,48,256]{2,1,0:T(8,128)(2,1)S(1)}, u32[]{:S(2)}, u32[]{:S(2)}) collective-permute-start(bf16[4,48,256]{2,1,0:T(8,128)(2,1)S(1)} %get-tuple-element.260), channel_id=1, source_target_pairs={{0,8},{2,10},{4,12},{6,14},{8,0},{10,2},{12,4},{14,6},{16,24},{18,... | collective-permute-start | bytes 294920 | tf_op jit(solution)/shard_map/ppermute | solution.py:542
  187.3 12.9 %collective-permute-start.13 = (bf16[4,48,256]{2,1,0:T(8,128)(2,1)S(1)}, bf16[4,48,256]{2,1,0:T(8,128)(2,1)S(1)}, u32[]{:S(2)}, u32[]{:S(2)}) collective-permute-start(bf16[4,48,256]{2,1,0:T(8,128)(2,1)S(1)} %get-tuple-element.261), channel_id=1, source_target_pairs={{0,24},{2,26},{4,28},{6,30},{8,16},{10,18},{12,20},{14,22},{16,8},... | collective-permute-start | bytes 294920 | tf_op jit(solution)/shard_map/ppermute | solution.py:542
  189.6 12.7 %collective-permute-start.12 = (bf16[4,48,256]{2,1,0:T(8,128)(2,1)S(1)}, bf16[4,48,256]{2,1,0:T(8,128)(2,1)S(1)}, u32[]{:S(2)}, u32[]{:S(2)}) collective-permute-start(bf16[4,48,256]{2,1,0:T(8,128)(2,1)S(1)} %get-tuple-element.262), channel_id=1, source_target_pairs={{0,16},{2,18},{4,20},{6,22},{8,24},{10,26},{12,28},{14,30},{16,0},... | collective-permute-start | bytes 294920 | tf_op jit(solution)/shard_map/ppermute | solution.py:542
  200.2 5.9 %collective-permute-start.28 = (bf16[48,256]{1,0:T(8,128)(2,1)S(1)}, bf16[48,256]{1,0:T(8,128)(2,1)S(1)}, u32[]{:S(2)}, u32[]{:S(2)}) collective-permute-start(bf16[48,256]{1,0:T(8,128)(2,1)S(1)} %get-tuple-element.277), channel_id=1, source_target_pairs={{0,4},{2,6},{4,0},{6,2},{8,12},{10,14},{12,8},{14,10},{16,20},{18,... | collective-permute-start | bytes 73736 | tf_op jit(solution)/shard_map/ppermute | solution.py:542
  203.4 20.3 %collective-permute-start.20 = (bf16[4,48,896]{2,1,0:T(8,128)(2,1)S(1)}, bf16[4,48,896]{2,1,0:T(8,128)(2,1)S(1)}, u32[]{:S(2)}, u32[]{:S(2)}) collective-permute-start(bf16[4,48,896]{2,1,0:T(8,128)(2,1)S(1)} %get-tuple-element.252), channel_id=1, source_target_pairs={{0,6},{2,4},{4,2},{6,0},{8,14},{10,12},{12,10},{14,8},{16,22},{18,... | collective-permute-start | bytes 1032200 | tf_op jit(solution)/shard_map/ppermute | solution.py:542
  204.6 19.1 %collective-permute-start.19 = (bf16[4,48,896]{2,1,0:T(8,128)(2,1)S(1)}, bf16[4,48,896]{2,1,0:T(8,128)(2,1)S(1)}, u32[]{:S(2)}, u32[]{:S(2)}) collective-permute-start(bf16[4,48,896]{2,1,0:T(8,128)(2,1)S(1)} %get-tuple-element.253), channel_id=1, source_target_pairs={{0,4},{2,6},{4,0},{6,2},{8,12},{10,14},{12,8},{14,10},{16,20},{18,... | collective-permute-start | bytes 1032200 | tf_op jit(solution)/shard_map/ppermute | solution.py:542
  206.1 7.5 %collective-permute-start.16 = (bf16[48,256]{1,0:T(8,128)(2,1)S(1)}, bf16[48,256]{1,0:T(8,128)(2,1)S(1)}, u32[]{:S(2)}, u32[]{:S(2)}) collective-permute-start(bf16[48,256]{1,0:T(8,128)(2,1)S(1)} %get-tuple-element.279), channel_id=1, source_target_pairs={{0,6},{2,4},{4,2},{6,0},{8,14},{10,12},{12,10},{14,8},{16,22},{18,... | collective-permute-start | bytes 73736 | tf_op jit(solution)/shard_map/ppermute | solution.py:542
  206.7 14.6 %collective-permute-start.15 = (bf16[48,256]{1,0:T(8,128)(2,1)S(1)}, bf16[48,256]{1,0:T(8,128)(2,1)S(1)}, u32[]{:S(2)}, u32[]{:S(2)}) collective-permute-start(bf16[48,256]{1,0:T(8,128)(2,1)S(1)} %get-tuple-element.280), channel_id=1, source_target_pairs={{0,4},{2,6},{4,0},{6,2},{8,12},{10,14},{12,8},{14,10},{16,20},{18,... | collective-permute-start | bytes 73736 | tf_op jit(solution)/shard_map/ppermute | solution.py:542
  213.7 12.3 %collective-permute-start.5 = (bf16[4,48,896]{2,1,0:T(8,128)(2,1)S(1)}, bf16[4,48,896]{2,1,0:T(8,128)(2,1)S(1)}, u32[]{:S(2)}, u32[]{:S(2)}) collective-permute-start(bf16[4,48,896]{2,1,0:T(8,128)(2,1)S(1)} %get-tuple-element.254), channel_id=1, source_target_pairs={{0,2},{2,0},{4,6},{6,4},{8,10},{10,8},{12,14},{14,12},{16,18},{18,... | collective-permute-start | bytes 1032200 | tf_op jit(solution)/shard_map/ppermute | solution.py:542
  221.3 10.8 %collective-permute-start.7 = (bf16[4,48,896]{2,1,0:T(8,128)(2,1)S(1)}, bf16[4,48,896]{2,1,0:T(8,128)(2,1)S(1)}, u32[]{:S(2)}, u32[]{:S(2)}) collective-permute-start(bf16[4,48,896]{2,1,0:T(8,128)(2,1)S(1)} %get-tuple-element.255), channel_id=1, source_target_pairs={{0,6},{2,4},{4,2},{6,0},{8,14},{10,12},{12,10},{14,8},{16,22},{18,... | collective-permute-start | bytes 1032200 | tf_op jit(solution)/shard_map/ppermute | solution.py:542
  222.4 16.9 %collective-permute-start.6 = (bf16[4,48,896]{2,1,0:T(8,128)(2,1)S(1)}, bf16[4,48,896]{2,1,0:T(8,128)(2,1)S(1)}, u32[]{:S(2)}, u32[]{:S(2)}) collective-permute-start(bf16[4,48,896]{2,1,0:T(8,128)(2,1)S(1)} %get-tuple-element.256), channel_id=1, source_target_pairs={{0,4},{2,6},{4,0},{6,2},{8,12},{10,14},{12,8},{14,10},{16,20},{18,... | collective-permute-start | bytes 1032200 | tf_op jit(solution)/shard_map/ppermute | solution.py:542
  223.9 18.1 %collective-permute-start.21 = (bf16[48,896]{1,0:T(8,128)(2,1)S(1)}, bf16[48,896]{1,0:T(8,128)(2,1)S(1)}, u32[]{:S(2)}, u32[]{:S(2)}) collective-permute-start(bf16[48,896]{1,0:T(8,128)(2,1)S(1)} %get-tuple-element.266), channel_id=1, source_target_pairs={{0,8},{2,10},{4,12},{6,14},{8,0},{10,2},{12,4},{14,6},{16,24},{18,... | collective-permute-start | bytes 258056 | tf_op jit(solution)/shard_map/ppermute | solution.py:542
  224.0 19.2 %collective-permute-start.23 = (bf16[48,896]{1,0:T(8,128)(2,1)S(1)}, bf16[48,896]{1,0:T(8,128)(2,1)S(1)}, u32[]{:S(2)}, u32[]{:S(2)}) collective-permute-start(bf16[48,896]{1,0:T(8,128)(2,1)S(1)} %get-tuple-element.267), channel_id=1, source_target_pairs={{0,24},{2,26},{4,28},{6,30},{8,16},{10,18},{12,20},{14,22},{16,8},... | collective-permute-start | bytes 258056 | tf_op jit(solution)/shard_map/ppermute | solution.py:542
  226.0 17.2 %collective-permute-start.22 = (bf16[48,896]{1,0:T(8,128)(2,1)S(1)}, bf16[48,896]{1,0:T(8,128)(2,1)S(1)}, u32[]{:S(2)}, u32[]{:S(2)}) collective-permute-start(bf16[48,896]{1,0:T(8,128)(2,1)S(1)} %get-tuple-element.268), channel_id=1, source_target_pairs={{0,16},{2,18},{4,20},{6,22},{8,24},{10,26},{12,28},{14,30},{16,0},... | collective-permute-start | bytes 258056 | tf_op jit(solution)/shard_map/ppermute | solution.py:542
  239.7 7.4 %collective-permute-start.10 = (bf16[48,896]{1,0:T(8,128)(2,1)S(1)}, bf16[48,896]{1,0:T(8,128)(2,1)S(1)}, u32[]{:S(2)}, u32[]{:S(2)}) collective-permute-start(bf16[48,896]{1,0:T(8,128)(2,1)S(1)} %get-tuple-element.270), channel_id=1, source_target_pairs={{0,24},{2,26},{4,28},{6,30},{8,16},{10,18},{12,20},{14,22},{16,8},... | collective-permute-start | bytes 258056 | tf_op jit(solution)/shard_map/ppermute | solution.py:542
  242.1 8.8 %collective-permute-start.9 = (bf16[48,896]{1,0:T(8,128)(2,1)S(1)}, bf16[48,896]{1,0:T(8,128)(2,1)S(1)}, u32[]{:S(2)}, u32[]{:S(2)}) collective-permute-start(bf16[48,896]{1,0:T(8,128)(2,1)S(1)} %get-tuple-element.271), channel_id=1, source_target_pairs={{0,16},{2,18},{4,20},{6,22},{8,24},{10,26},{12,28},{14,30},{16,0},... | collective-permute-start | bytes 258056 | tf_op jit(solution)/shard_map/ppermute | solution.py:542
  255.4 10.5 %all-to-all-start.1 = ((f32[32,1,1]{2,1,0:T(1,128)}), f32[32,1,1]{2,1,0:T(1,128)S(1)}, u32[]{:S(2)}, u32[]{:S(2)}) async-start(f32[32,1,1]{2,1,0:T(1,128)} %broadcast_in_dim.7), calls=%async_computation.1 | async-start | bytes 32768 | tf_op jit(solution)/shard_map/all_to_all | solution.py:687
  (30 other events, 625.0 us)

commit v2 on v1

--- a/solution.py
+++ b/solution.py
@@ -25,6 +25,7 @@
 LOG2E = 1.4426950408889634
 LN2 = 0.6931471805599453
 IDENT_ROWS = 40
+IDENT_USED = 34
 PAIR = 2
 VMEM_BYTES = 60 * 1024 * 1024
 
@@ -81,79 +82,45 @@
     return jnp.concatenate(columns, axis=1)
 
 
-def front_kernel(
-    len_ref,
+def lane_columns(row, slots):
+    return jnp.broadcast_to(row, (slots, row.shape[1])).T
+
+
+def embed_kernel(
     tok_ref,
     cot_ref,
     typ_ref,
     pair_ref,
     lap_ref,
-    est_ref,
+    embed_ref,
     norm_ref,
-    qkv_o,
-    qkv_p,
-    out_o,
-    out_p,
-    up_o,
-    up_p,
-    down_o,
-    down_p,
-    output_ref,
     h0_ref,
-    gh1_ref,
     na_ref,
     fs_ref,
-    q_ref,
-    k_ref,
-    v_ref,
-    do_ref,
-    e_ref,
-    gown_ref,
-    gpeer_ref,
-    lnacc_ref,
-    qkvt,
-    outt,
-    upt,
-    downt,
+    ct_ref,
     nb,
-    act_s,
-    cot_s,
-    nbt_s,
-    gp_s,
-    mix_s,
-    ga_s,
-    mixf,
-    h1_s,
-    nrm_s,
-    dgel_s,
-    rec_s,
+    rows,
+    est,
 ):
-    step = pl.program_id(0)
-    steps = pl.num_programs(0)
     slots = tok_ref.shape[1]
     width = tok_ref.shape[2]
-    half = width // 2
-    halves = ((qkv_o, out_o, up_o, down_o), (qkv_p, out_p, up_p, down_p))
-
-    @pl.when(step == 0)
+
+    @pl.when(pl.program_id(0) == 0)
     def _():
-        for h, (qkv, out, up, down) in enumerate(halves):
-            for c in range(3):
-                qkvt[h, c * half : (c + 1) * half, :] = qkv[c].T
-            outt[h] = out[...].T
-            upt[h] = up[...].T
-            downt[h] = down[...].T
-        for row in range(4):
-            nb[row] = jnp.broadcast_to(norm_ref[:, row : row + 1], (width, slots))
-        lnacc_ref[...] = jnp.zeros_like(lnacc_ref)
-
-    base = pl.multiple_of(step * PAIR * slots, PAIR * slots)
-    span = pl.ds(base, PAIR * slots)
+        for row in range(2):
+            nb[row] = lane_columns(norm_ref[row : row + 1, :], slots)
+        rows[...] = jnp.zeros_like(rows)
+        rows[0 : embed_ref.shape[0], :] = embed_ref[...]
+        whole = rows[...]
+        e1 = whole.astype(BF16).astype(F32)
+        e2 = (whole - e1).astype(BF16).astype(F32)
+        e3 = whole - e1 - e2
+        blank = jnp.zeros((8, width), F32)
+        stacked = jnp.concatenate([e1, e2, e3, blank, e1, e2, e1, blank], axis=0)
+        est[...] = stacked.T.astype(BF16)
 
     node_iota = lax.broadcasted_iota(jnp.int32, (lap_ref.shape[2], slots), 0)
     row_iota = lax.broadcasted_iota(jnp.int32, (8, slots), 0)
-    lane_iota = lax.broadcasted_iota(jnp.int32, (1, slots), 1)
-
     for j in range(PAIR):
         lanes = slice(j * slots, (j + 1) * slots)
         lap = lap_ref[j]
@@ -174,13 +141,79 @@
         f1 = jnp.concatenate([lf[0:ident], rf[0:ident], kinds], axis=0)
         f2 = jnp.concatenate([lf[ident : 2 * ident], rf[ident : 2 * ident], none], axis=0)
         f3 = jnp.concatenate([lf[2 * ident :], rf[2 * ident :], none], axis=0)
-        stack = jnp.concatenate([f1, f1, f1, f2, f2, f3, none, none], axis=0).astype(BF16)
+        stack = jnp.concatenate([f1, f1, f1, none, f2, f2, f3, none], axis=0).astype(BF16)
         fs_ref[:, lanes] = stack
-        h0 = tok_ref[j].T.astype(F32) + dot_nn(est_ref[...], stack)
+        h0 = tok_ref[j].T.astype(F32) + dot_nn(est[...], stack)
         h0_ref[:, lanes] = h0
         centred, rec = norm_parts(h0)
         na_ref[:, lanes] = (centred * rec * nb[0] + nb[1]).astype(BF16)
-        cot_s[:, pl.ds(pl.multiple_of(base + j * slots, slots), slots)] = cot_ref[j].T
+        ct_ref[:, lanes] = cot_ref[j].T
+
+
+def front_kernel(
+    len_ref,
+    h0_ref,
+    na_ref,
+    cot_s,
+    norm_ref,
+    qkv_o,
+    qkv_p,
+    out_o,
+    out_p,
+    up_o,
+    up_p,
+    down_o,
+    down_p,
+    output_ref,
+    gh1_ref,
+    q_ref,
+    k_ref,
+    v_ref,
+    do_ref,
+    e_ref,
+    gown_ref,
+    gpeer_ref,
+    lnacc_ref,
+    qkvt,
+    outt,
+    upt,
+    downt,
+    nb,
+    act_s,
+    nbt_s,
+    gp_s,
+    mix_s,
+    ga_s,
+    mixf,
+    h1_s,
+    nrm_s,
+    dgel_s,
+    rec_s,
+):
+    step = pl.program_id(0)
+    steps = pl.num_programs(0)
+    slots = output_ref.shape[1]
+    width = output_ref.shape[2]
+    half = width // 2
+    halves = ((qkv_o, out_o, up_o, down_o), (qkv_p, out_p, up_p, down_p))
+
+    @pl.when(step == 0)
+    def _():
+        for h, (qkv, out, up, down) in enumerate(halves):
+            for c in range(3):
+                qkvt[h, c * half : (c + 1) * half, :] = qkv[c].T
+            outt[h] = out[...].T
+            upt[h] = up[...].T
+            downt[h] = down[...].T
+        for row in range(2):
+            nb[row] = lane_columns(norm_ref[row + 2 : row + 3, :], slots)
+        lnacc_ref[...] = jnp.zeros_like(lnacc_ref)
+
+    base = pl.multiple_of(step * PAIR * slots, PAIR * slots)
+    span = pl.ds(base, PAIR * slots)
+
+    row_iota = lax.broadcasted_iota(jnp.int32, (8, slots), 0)
+    lane_iota = lax.broadcasted_iota(jnp.int32, (1, slots), 1)
 
     one_row = jnp.where(row_iota == 0, 1.0, 0.0)
     two_rows = jnp.where(row_iota < 2, 1.0, 0.0)
@@ -220,7 +253,7 @@
             mixf[out_rows, lanes] = jnp.concatenate(mixes, axis=0)
             return carry
 
-        lax.fori_loop(0, groups, attend, 0)
+        lax.fori_loop(0, groups, attend, 0, unroll=4)
 
     mix = mixf[...].astype(BF16)
     mix_s[:, span] = mix
@@ -234,7 +267,7 @@
         nrm_s[:, lanes] = unit
         rec_s[j, groups, 0:1, :] = rec
         nbt_s[:, pl.ds(pl.multiple_of(base + j * slots, slots), slots)] = (
-            unit * nb[2] + nb[3]
+            unit * nb[0] + nb[1]
         ).astype(BF16)
 
     for h in range(2):
@@ -260,7 +293,7 @@
         unit = nrm_s[:, lanes]
         lnacc_ref[0] += gb * unit
         lnacc_ref[1] += gb
-        f = gb * nb[2]
+        f = gb * nb[0]
         f_mean = jnp.sum(f, axis=0, keepdims=True) * inv
         fn_mean = jnp.sum(f * unit, axis=0, keepdims=True) * inv
         gh1 = cot_s[:, cols].astype(F32) + rec_s[j, groups, 0:1, :] * (
@@ -338,7 +371,7 @@
                 dx_ref[at, cols] = whole.astype(BF16)
             return carry
 
-        lax.fori_loop(0, groups, attend, 0)
+        lax.fori_loop(0, groups, attend, 0, unroll=4)
 
     @pl.when(step == steps - 1)
     def _():
@@ -350,7 +383,7 @@
 
 
 def back_kernel(
-    dxo_ref, dxp_ref, qkv_o, qkv_p, h0_ref, gh1_ref, fs_ref, gain_ref, ig_ref, lnacc_ref, ge_ref, nb
+    dxo_ref, dxp_ref, qkv_o, qkv_p, h0_ref, gh1_ref, fs_ref, gain_ref, lnb_ref, ig_ref, small_ref, nb, lnacc, ge
 ):
     step = pl.program_id(0)
     slots = ig_ref.shape[1]
@@ -360,33 +393,115 @@
 
     @pl.when(step == 0)
     def _():
-        lnacc_ref[...] = jnp.zeros_like(lnacc_ref)
-        ge_ref[...] = jnp.zeros_like(ge_ref)
-        nb[...] = jnp.broadcast_to(gain_ref[:, 0:1], (width, slots))
+        lnacc[...] = jnp.zeros_like(lnacc)
+        ge[...] = jnp.zeros_like(ge)
+        nb[...] = lane_columns(gain_ref[0:1, :], slots)
 
     total = None
     for qkv, dx in ((qkv_o, dxo_ref), (qkv_p, dxp_ref)):
         for c in range(3):
             part = dot_nn(qkv[c], dx[c * half : (c + 1) * half, :])
             total = part if total is None else total + part
+    highs, lows = [], []
     for j in range(PAIR):
         lanes = slice(j * slots, (j + 1) * slots)
         ga = total[:, lanes]
         centred, rec = norm_parts(h0_ref[:, lanes])
         unit = centred * rec
-        lnacc_ref[0] += ga * unit
-        lnacc_ref[1] += ga
+        lnacc[0] += ga * unit
+        lnacc[1] += ga
         f = ga * nb[...]
         f_mean = jnp.sum(f, axis=0, keepdims=True) * inv
         fn_mean = jnp.sum(f * unit, axis=0, keepdims=True) * inv
         ig = gh1_ref[:, lanes] + rec * (f - f_mean - unit * fn_mean)
         ig_ref[j] = ig.T
         high = ig.astype(BF16)
-        rest = ig - high.astype(F32)
-        low = rest.astype(BF16)
-        least = (rest - low.astype(F32)).astype(BF16)
-        fs = fs_ref[:, lanes]
-        ge_ref[...] += dot_nt(high, fs) + dot_nt(low, fs) + dot_nt(least, fs)
+        highs.append(high)
+        lows.append((ig - high.astype(F32)).astype(BF16))
+    fs = fs_ref[...]
+    ge[...] += dot_nt(jnp.concatenate(highs, axis=1), fs) + dot_nt(
+        jnp.concatenate(lows, axis=1), fs
+    )
+
+    @pl.when(step == pl.num_programs(0) - 1)
+    def _():
+        lane = lax.broadcasted_iota(jnp.int32, (width, slots), 1)
+        rows = ge[:, 0:slots] + ge[:, slots:]
+        sums = (lnacc[0], lnacc[1], lnb_ref[0], lnb_ref[1])
+        for at, part in enumerate(sums):
+            rows = jnp.where(lane == IDENT_USED + at, jnp.sum(part, axis=1, keepdims=True), rows)
+        rows = jnp.where(lane < IDENT_ROWS, rows, 0.0)
+        if small_ref.shape[0] == width:
+            small_ref[...] = rows
+        else:
+            cut = rows.reshape(small_ref.shape[0], 3, 8, slots)
+            flat = (small_ref.shape[0] * 8, slots)
+            packed = cut[:, 0].reshape(flat)
+            packed = packed + pltpu.roll(cut[:, 1].reshape(flat), IDENT_ROWS, 1)
+            packed = packed + pltpu.roll(cut[:, 2].reshape(flat), 2 * IDENT_ROWS, 1)
+            small_ref[...] = packed.reshape(small_ref.shape)
+
+
+def gather_kernel(got1_ref, own_ref, a_ref, b_ref, c_ref, got_ref, red1_ref, red2_ref, small_ref, sq_ref):
+    red1 = got1_ref[0].astype(F32)
+    for o in range(1, got1_ref.shape[0]):
+        red1 = red1 + got1_ref[o].astype(F32)
+    red2 = own_ref[...].astype(F32) + a_ref[...].astype(F32)
+    red2 = red2 + b_ref[...].astype(F32) + c_ref[...].astype(F32)
+    small = got_ref[0]
+    for o in range(1, got_ref.shape[0]):
+        small = small + got_ref[o]
+    red1_ref[...] = red1
+    red2_ref[...] = red2
+    small_ref[...] = small
+    both = red1 * red1 + red2 * red2
+    lanes = sq_ref.shape[1]
+    folded = both[:, 0:lanes]
+    for c in range(1, both.shape[1] // lanes):
+        folded = folded + both[:, c * lanes : (c + 1) * lanes]
+    total = jnp.sum(folded) + jnp.sum(small * small)
+    sq_ref[...] = jnp.full(sq_ref.shape, total, F32)
+
+
+def adam_kernel(*refs):
+    sq_ref, red1_ref, red2_ref, small_ref = refs[0:4]
+    ins, clip_ref, outs = refs[4:22], refs[22], refs[23:41]
+    total = jnp.sum(sq_ref[...], axis=0, keepdims=True)
+    clip = jnp.sqrt(total)
+    clip_ref[...] = clip
+    scale = jnp.max(jnp.minimum(1.0, CLIP_LIMIT / (clip + 1e-06)))
+    half = red2_ref.shape[1] // 3
+    some = red1_ref.shape[0] // 2
+    lanes = small_ref.shape[1]
+    small = small_ref[...]
+    table = jnp.concatenate(
+        [
+            small,
+            pltpu.roll(small, lanes - IDENT_ROWS, 1),
+            pltpu.roll(small, lanes - 2 * IDENT_ROWS, 1),
+        ],
+        axis=0,
+    )
+    norm_grad = table.T[IDENT_USED : IDENT_USED + 4]
+    matrix = (MATRIX_RATE, MATRIX_DECAY)
+    for c in range(3):
+        step = adam_step(
+            ins[0][c], ins[1][c], ins[2][c], red2_ref[:, c * half : (c + 1) * half], *matrix, scale
+        )
+        for out, value in zip(outs[0:3], step):
+            out[c] = value
+    jobs = (
+        (red1_ref[some:, 0 : 2 * half], matrix),
+        (red1_ref[:, 2 * half :], matrix),
+        (red1_ref[0:some, 0 : 2 * half], matrix),
+        (norm_grad, (NORM_RATE, 0.0)),
+        (table[:, 0:IDENT_USED], (EMBED_RATE, 0.0)),
+    )
+    for at, (grad, rates) in enumerate(jobs):
+        i = 3 * (at + 1)
+        step = adam_step(ins[i][...], ins[i + 1][...], ins[i + 2][...], grad, *rates, scale)
+        for out, value in zip(outs[i : i + 3], step):
+            out[...] = value
 
 
 def whole_spec(shape):
@@ -394,48 +509,83 @@
     return pl.BlockSpec(shape, lambda i: zeros, pipeline_mode=pl.Buffered(1))
 
 
-def front(lengths, tokens, cotangent, token_types, pairs_t, lap_t, est, norm_t, own, peer):
+def lead_spec(*rest):
+    return pl.BlockSpec((PAIR,) + rest, lambda i: (i,) + (0,) * len(rest))
+
+
+def column_spec(rows, slots):
+    return pl.BlockSpec((rows, PAIR * slots), lambda i: (0, i))
+
+
+def costs(flops, moved):
+    return pl.CostEstimate(flops=flops, bytes_accessed=moved, transcendentals=0)
+
+
+def embed(tokens, cotangent, token_types, pairs_t, lap_t, embed_weight, norm_params):
     mols, slots, width = tokens.shape
+    toks = mols * slots
+    rows = (width, width, 256, width)
+    types = (F32, BF16, BF16, BF16)
+    return pl.pallas_call(
+        embed_kernel,
+        grid=(mols // PAIR,),
+        out_shape=[jax.ShapeDtypeStruct((r, toks), t) for r, t in zip(rows, types)],
+        out_specs=[column_spec(r, slots) for r in rows],
+        in_specs=[
+            lead_spec(slots, width),
+            lead_spec(slots, width),
+            lead_spec(1, slots),
+            lead_spec(2, slots),
+            lead_spec(lap_t.shape[1], lap_t.shape[2]),
+            whole_spec(embed_weight.shape),
+            whole_spec(norm_params.shape),
+        ],
+        scratch_shapes=[
+            pltpu.VMEM((2, width, slots), F32),
+            pltpu.VMEM((IDENT_ROWS, width), F32),
+            pltpu.VMEM((width, 256), BF16),
+        ],
+        compiler_params=pltpu.CompilerParams(vmem_limit_bytes=VMEM_BYTES),
+        cost_estimate=costs(8_000_000_000, 10_000_000),
+        name="embed",
+    )(tokens, cotangent, token_types.reshape(mols, 1, slots), pairs_t, lap_t, embed_weight, norm_params)
+
+
+def front(lengths, h0, na, cot, norm_params, own, peer, mols):
+    width, toks = h0.shape
+    slots = toks // mols
     half = width // 2
     heads = width // HEAD_DIM
-    toks = mols * slots
-    steps = mols // PAIR
     owners = 16
-    lead = lambda *rest: pl.BlockSpec((PAIR,) + rest, lambda i: (i,) + (0,) * len(rest))
-    col = lambda rows: pl.BlockSpec((rows, PAIR * slots), lambda i: (0, i))
+    col = column_spec(width, slots)
     weights = []
     for pair in zip(own, peer):
         weights += list(pair)
     gshape = (owners, 2 * half // owners, 3 * half)
+    padded = jax.ShapeDtypeStruct((mols, heads * PAD_DIM, slots), BF16)
     outs = [
-        (jax.ShapeDtypeStruct((mols, slots, width), BF16), lead(slots, width)),
-        (jax.ShapeDtypeStruct((width, toks), F32), col(width)),
-        (jax.ShapeDtypeStruct((width, toks), F32), col(width)),
-        (jax.ShapeDtypeStruct((width, toks), BF16), col(width)),
-        (jax.ShapeDtypeStruct((256, toks), BF16), col(256)),
-        (jax.ShapeDtypeStruct((mols, heads * PAD_DIM, slots), BF16), lead(heads * PAD_DIM, slots)),
-        (jax.ShapeDtypeStruct((mols, heads * PAD_DIM, slots), BF16), lead(heads * PAD_DIM, slots)),
-        (jax.ShapeDtypeStruct((mols, heads * PAD_DIM, slots), BF16), lead(heads * PAD_DIM, slots)),
-        (jax.ShapeDtypeStruct((mols, heads * PAD_DIM, slots), BF16), lead(heads * PAD_DIM, slots)),
-        (jax.ShapeDtypeStruct((mols, heads, slots, slots), BF16), lead(heads, slots, slots)),
-        (jax.ShapeDtypeStruct(gshape, F32), whole_spec(gshape)),
+        (jax.ShapeDtypeStruct((mols, slots, width), BF16), lead_spec(slots, width)),
+        (jax.ShapeDtypeStruct((width, toks), F32), col),
+        (padded, lead_spec(heads * PAD_DIM, slots)),
+        (padded, lead_spec(heads * PAD_DIM, slots)),
+        (padded, lead_spec(heads * PAD_DIM, slots)),
+        (padded, lead_spec(heads * PAD_DIM, slots)),
+        (jax.ShapeDtypeStruct((mols, heads, slots, slots), BF16), lead_spec(heads, slots, slots)),
+        (jax.ShapeDtypeStruct(gshape, BF16), whole_spec(gshape)),
         (jax.ShapeDtypeStruct(gshape, BF16), whole_spec(gshape)),
         (jax.ShapeDtypeStruct((2, width, slots), F32), whole_spec((2, width, slots))),
     ]
     return pl.pallas_call(
         front_kernel,
-        grid=(steps,),
+        grid=(mols // PAIR,),
         out_shape=[o[0] for o in outs],
         out_specs=[o[1] for o in outs],
         in_specs=[
             pl.BlockSpec(memory_space=pltpu.SMEM),
-            lead(slots, width),
-            lead(slots, width),
-            lead(1, slots),
-            lead(2, slots),
-            lead(lap_t.shape[1], lap_t.shape[2]),
-            whole_spec(est.shape),
-            whole_spec(norm_t.shape),
+            col,
+            col,
+            whole_spec(cot.shape),
+            whole_spec(norm_params.shape),
         ]
         + [whole_spec(w.shape) for w in weights],
         scratch_shapes=[
@@ -443,30 +593,18 @@
             pltpu.VMEM((2, width, half), BF16),
             pltpu.VMEM((2, half, width), BF16),
             pltpu.VMEM((2, width, half), BF16),
-            pltpu.VMEM((4, width, slots), F32),
+            pltpu.VMEM((2, width, slots), F32),
         ]
-        + [pltpu.VMEM((width, toks), BF16)] * 6
+        + [pltpu.VMEM((width, toks), BF16)] * 5
         + [pltpu.VMEM((width, PAIR * slots), F32)] * 4
         + [pltpu.VMEM((PAIR, heads // 4 + 1, 8, slots), F32)],
         compiler_params=pltpu.CompilerParams(vmem_limit_bytes=VMEM_BYTES),
-        cost_estimate=pl.CostEstimate(
-            flops=2 * toks * width * width * 15, bytes_accessed=50_000_000, transcendentals=0
-        ),
+        cost_estimate=costs(60_000_000_000, 50_000_000),
         name="front",
-    )(
-        lengths,
-        tokens,
-        cotangent,
-        token_types.reshape(mols, 1, slots),
-        pairs_t,
-        lap_t,
-        est,
-        norm_t,
-        *weights,
-    )
-
-
-def middle(which, dtype, na, q, k, v, do, e):
+    )(lengths, h0, na, cot, norm_params, *weights)
+
+
+def middle(which, na, q, k, v, do, e):
     mols, heads, slots, _ = e.shape
     width, toks = na.shape
     half = width // 2
@@ -478,7 +616,7 @@
         grid=(mols // PAIR,),
         out_shape=[
             jax.ShapeDtypeStruct((3 * half, toks), BF16),
-            jax.ShapeDtypeStruct(gshape, dtype),
+            jax.ShapeDtypeStruct(gshape, BF16),
         ],
         in_specs=[
             whole_spec(na.shape),
@@ -490,47 +628,71 @@
         ],
         out_specs=[whole_spec((3 * half, toks)), whole_spec(gshape)],
         compiler_params=pltpu.CompilerParams(vmem_limit_bytes=VMEM_BYTES),
-        cost_estimate=pl.CostEstimate(
-            flops=2 * toks * width * width * 5, bytes_accessed=12_000_000, transcendentals=0
-        ),
+        cost_estimate=costs(20_000_000_000, 12_000_000),
         name="middle",
     )(na, q, k, v, do, e)
 
 
-def back(dxo, dxp, qkv_o, qkv_p, h0, gh1, fs, gain, mols):
+def back(dxo, dxp, qkv_o, qkv_p, h0, gh1, fs, gain, lnb, mols, packed):
     width, toks = h0.shape
     slots = toks // mols
-    col = lambda rows: pl.BlockSpec((rows, PAIR * slots), lambda i: (0, i))
+    col = column_spec(width, slots)
+    dxs = column_spec(dxo.shape[0], slots)
+    small = (width // 24, 8, slots) if packed else (width, slots)
     return pl.pallas_call(
         back_kernel,
         grid=(mols // PAIR,),
         out_shape=[
             jax.ShapeDtypeStruct((mols, slots, width), F32),
-            jax.ShapeDtypeStruct((2, width, slots), F32),
-            jax.ShapeDtypeStruct((width, 256), F32),
+            jax.ShapeDtypeStruct(small, F32),
         ],
         in_specs=[
-            col(dxo.shape[0]),
-            col(dxo.shape[0]),
+            dxs,
+            dxs,
             whole_spec(qkv_o.shape),
             whole_spec(qkv_p.shape),
-            col(width),
-            col(width),
-            col(256),
+            col,
+            col,
+            column_spec(fs.shape[0], slots),
             whole_spec(gain.shape),
+            whole_spec(lnb.shape),
         ],
-        out_specs=[
-            pl.BlockSpec((PAIR, slots, width), lambda i: (i, 0, 0)),
-            whole_spec((2, width, slots)),
-            whole_spec((width, 256)),
+        out_specs=[lead_spec(slots, width), whole_spec(small)],
+        scratch_shapes=[
+            pltpu.VMEM((width, slots), F32),
+            pltpu.VMEM((2, width, slots), F32),
+            pltpu.VMEM((width, fs.shape[0]), F32),
         ],
-        scratch_shapes=[pltpu.VMEM((width, slots), F32)],
         compiler_params=pltpu.CompilerParams(vmem_limit_bytes=VMEM_BYTES),
-        cost_estimate=pl.CostEstimate(
-            flops=2 * toks * width * width * 4, bytes_accessed=15_000_000, transcendentals=0
-        ),
+        cost_estimate=costs(18_000_000_000, 15_000_000),
         name="back",
-    )(dxo, dxp, qkv_o, qkv_p, h0, gh1, fs, gain)
+    )(dxo, dxp, qkv_o, qkv_p, h0, gh1, fs, gain, lnb)
+
+
+def gather(got1, own2, others2, got):
+    rows, columns = got1.shape[1:]
+    lanes = got.shape[2]
+    return pl.pallas_call(
+        gather_kernel,
+        out_shape=[
+            jax.ShapeDtypeStruct((rows, columns), F32),
+            jax.ShapeDtypeStruct((rows, columns), F32),
+            jax.ShapeDtypeStruct(got.shape[1:], F32),
+            jax.ShapeDtypeStruct((got.shape[0], lanes), F32),
+        ],
+        compiler_params=pltpu.CompilerParams(vmem_limit_bytes=VMEM_BYTES),
+        name="gather",
+    )(got1, own2, *others2, got)
+
+
+def adam_all(squares, red1, red2, small, state):
+    return pl.pallas_call(
+        adam_kernel,
+        out_shape=[jax.ShapeDtypeStruct((1, squares.shape[1]), F32)]
+        + [jax.ShapeDtypeStruct(a.shape, F32) for a in state],
+        compiler_params=pltpu.CompilerParams(vmem_limit_bytes=VMEM_BYTES),
+        name="adam",
+    )(squares, red1, red2, small, *state)
 
 
 def swap(value):
@@ -544,27 +706,6 @@
 
 def take(value, index, axis=0):
     return lax.dynamic_index_in_dim(value, index, axis, keepdims=False)
-
-
-def exchange(value, mine, count, stride):
-    total = take(value, mine).astype(F32)
-    for k in range(1, count):
-        total = total + hop(take(value, mine ^ k), k * stride).astype(F32)
-    return total
-
-
-def reduce_owned(value):
-    index = lax.axis_index("dp")
-    plane, line = index & 3, index >> 2
-    rows, columns = value.shape[1:]
-    cut = columns * 7 // 9 // 128 * 128
-    first = value[:, :, :cut].reshape(4, 4, rows, cut).swapaxes(0, 1)
-    first = exchange(first, plane, 4, 1).astype(BF16)
-    first = exchange(first, line, 4, 4)
-    second = value[:, :, cut:].reshape(4, 4, rows, columns - cut)
-    second = exchange(second, line, 4, 4).astype(BF16)
-    second = exchange(second, plane, 4, 1)
-    return jnp.concatenate([first, second], axis=1)
 
 
 def adam_step(master, mean_old, square_old, gradient, rate, decay, clip_scale):
@@ -616,99 +757,92 @@
     own = (qkv_weight.transpose(1, 0, 2), out_weight, up_weight, down_weight)
     peer = tuple(swap(w) for w in own)
 
-    embed_rows = jnp.pad(embed_weight, ((0, IDENT_ROWS - idents), (0, 0)))
-    e1 = lax.reduce_precision(embed_rows, 8, 7)
-    e2 = lax.reduce_precision(embed_rows - e1, 8, 7)
-    e3 = embed_rows - e1 - e2
-    blank = jnp.zeros((256 - 6 * IDENT_ROWS, width), F32)
-    est = jnp.concatenate([e1, e2, e3, e1, e2, e1, blank], axis=0).astype(BF16).T
-    norm_t = norm_params.T
-
-    (output, h0, gh1, na, fs, q, k, v, do, e, gown1, gpeer1, lnacc_b) = front(
-        lengths,
+    world = dp_size * mp_size
+    shard_width = width // world
+    fits = dp_size == 16 and shard_width == 24
+
+    h0, na, fs, cot = embed(
         tokens,
         cotangent,
         token_types,
         node_pairs.transpose(0, 2, 1),
         laplacian.transpose(0, 2, 1),
-        est,
-        norm_t,
-        own,
-        peer,
+        embed_weight,
+        norm_params,
     )
-    sum1 = gown1 + swap(gpeer1).astype(F32)
-    dxp, gpeer2 = middle(1, BF16, na, q, k, v, do, e)
+    (output, gh1, q, k, v, do, e, gown1, gpeer1, lnb) = front(
+        lengths, h0, na, cot, norm_params, own, peer, mols
+    )
+    sum1 = (gown1.astype(F32) + swap(gpeer1).astype(F32)).astype(BF16)
+    sum1, do = lax.optimization_barrier((sum1, do))
+    if fits:
+        got1 = lax.all_to_all(sum1, "dp", 0, 0, tiled=True)
+    dxp, gpeer2 = middle(1, na, q, k, v, do, e)
     got2 = swap(gpeer2)
-    dxo, gown2 = middle(0, F32, na, q, k, v, do, e)
-    sum2 = gown2 + got2.astype(F32)
-    input_grad, lnacc_a, gembed = back(
-        dxo, dxp, own[0], peer[0], h0, gh1, fs, norm_t, mols
-    )
-
-    if dp_size == 16:
-        red1 = reduce_owned(sum1.astype(BF16))
-        red2 = reduce_owned(sum2.astype(BF16))
-        some = half // dp_size
-        reduced_down = red1[0:some, 0:width]
-        reduced_out = red1[some:, 0:width]
-        reduced_up = red1[:, width:]
-        reduced_qkv = red2.reshape(2 * some, 3, half)
-    else:
-        some = half // 16
-        scatter = partial(lax.psum_scatter, axis_name="dp", scatter_dimension=0, tiled=True)
-        reduced_down = scatter(sum1[:, 0:some, 0:width].reshape(half, width))
-        reduced_out = scatter(sum1[:, some:, 0:width].reshape(half, width))
-        reduced_up = scatter(sum1[:, :, width:].reshape(width, half))
-        reduced_qkv = scatter(sum2.reshape(width, 3, half))
-
-    i1, i2, i3 = 0, 3 * IDENT_ROWS, 5 * IDENT_ROWS
-    grad_embed = (
-        gembed[:, i1 : i1 + idents] + gembed[:, i2 : i2 + idents] + gembed[:, i3 : i3 + idents]
-    )
-    small = jnp.concatenate(
-        [jnp.sum(lnacc_a, axis=2).T, jnp.sum(lnacc_b, axis=2).T, grad_embed], axis=1
-    )
-    world = dp_size * mp_size
-    shard_width = width // world
-    small = small.reshape(world, shard_width, small.shape[1])
-    got = lax.all_to_all(small, ("dp", "mp"), 0, 0, tiled=True)
-    small_own = jnp.sum(got, axis=0).T
-    reduced_norm = small_own[0:4]
-    reduced_embed = small_own[4:]
-
-    own_square = (
-        jnp.sum(reduced_qkv * reduced_qkv)
-        + jnp.sum(reduced_out * reduced_out)
-        + jnp.sum(reduced_up * reduced_up)
-        + jnp.sum(reduced_down * reduced_down)
-        + jnp.sum(small_own * small_own)
-    )
-    squares = jnp.broadcast_to(own_square, (world, 1))
-    total_square = jnp.sum(lax.all_to_all(squares, ("dp", "mp"), 0, 0, tiled=True))
-    clip_norm = jnp.sqrt(total_square)
-    clip_scale = jnp.minimum(1.0, CLIP_LIMIT / (clip_norm + 1e-06))
-    shard_index = lax.axis_index("dp") * mp_size + lax.axis_index("mp")
+    dxo, gown2 = middle(0, na, q, k, v, do, e)
+    sum2 = (gown2.astype(F32) + got2.astype(F32)).astype(BF16)
+    index = lax.axis_index("dp")
+    if fits:
+        plane, line = index & 3, index >> 2
+        grid = sum2.reshape((4, 4) + sum2.shape[1:]).swapaxes(0, 1)
+        own2 = take(grid, plane)
+        sends = [take(grid, plane ^ k) for k in (1, 2, 3)]
+        sends, dxo = lax.optimization_barrier((sends, dxo))
+        near = [hop(piece, k) for piece, k in zip(sends, (1, 2, 3))]
+    input_grad, small = back(dxo, dxp, own[0], peer[0], h0, gh1, fs, norm_params, lnb, mols, fits)
+
+    shard_index = index * mp_size + lax.axis_index("mp")
     norm_own = lax.dynamic_slice_in_dim(norm_params, shard_index * shard_width, shard_width, 1)
     embed_own = lax.dynamic_slice_in_dim(embed_weight, shard_index * shard_width, shard_width, 1)
-    qkv_new = adam_step(
-        qkv_master, qkv_mean, qkv_square, reduced_qkv, MATRIX_RATE, MATRIX_DECAY, clip_scale
+    flip = lambda a: a.transpose(1, 0, 2)
+    if fits:
+        plane_sum = own2.astype(F32)
+        for piece in near:
+            plane_sum = plane_sum + piece.astype(F32)
+        plane_sum = plane_sum.astype(BF16)
+        small, got1, plane_sum = lax.optimization_barrier((small, got1, plane_sum))
+        got = lax.all_to_all(small, ("dp", "mp"), 0, 0, tiled=True)
+        far = [hop(take(plane_sum, line ^ k), 4 * k) for k in (1, 2, 3)]
+        red1, red2, small_own, squares = gather(got1, take(plane_sum, line), far, got)
+        lanes = squares.shape[1]
+        squares = lax.all_to_all(squares.reshape(world, 1, lanes), ("dp", "mp"), 0, 0, tiled=True)
+        state = (
+            (flip(qkv_master), flip(qkv_mean), flip(qkv_square))
+            + (out_master, out_mean, out_square)
+            + (up_master, up_mean, up_square)
+            + (down_master, down_mean, down_square)
+            + (norm_own, norm_mean, norm_square)
+            + (embed_own.T, embed_mean.T, embed_square.T)
+        )
+        clip, *new = adam_all(squares.reshape(world, lanes), red1, red2, small_own, state)
+        new = [flip(a) for a in new[0:3]] + list(new[3:15]) + [a.T for a in new[15:18]]
+        return (output, input_grad, clip[0, 0]) + tuple(new)
+
+    some = half // 16
+    scatter = partial(lax.psum_scatter, axis_name="dp", scatter_dimension=0, tiled=True)
+    sum1, sum2 = sum1.astype(F32), sum2.astype(F32)
+    reduced_down = scatter(sum1[:, 0:some, 0:width].reshape(half, width))
+    reduced_out = scatter(sum1[:, some:, 0:width].reshape(half, width))
+    reduced_up = scatter(sum1[:, :, width:].reshape(width, half))
+    reduced_qkv = scatter(sum2.reshape(width, 3, half))
+    small = small[:, : idents + 4].reshape(world, shard_width, idents + 4)
+    small_own = jnp.sum(lax.all_to_all(small, ("dp", "mp"), 0, 0, tiled=True), axis=0).T
+    reduced = (reduced_qkv, reduced_out, reduced_up, reduced_down, small_own[idents:], small_own[:idents])
+    own_square = sum(jnp.sum(piece * piece) for piece in reduced)
+    clip_norm = jnp.sqrt(lax.psum(own_square, ("dp", "mp")))
+    clip_scale = jnp.minimum(1.0, CLIP_LIMIT / (clip_norm + 1e-06))
+    state = (
+        (qkv_master, qkv_mean, qkv_square, MATRIX_RATE, MATRIX_DECAY),
+        (out_master, out_mean, out_square, MATRIX_RATE, MATRIX_DECAY),
+        (up_master, up_mean, up_square, MATRIX_RATE, MATRIX_DECAY),
+        (down_master, down_mean, down_square, MATRIX_RATE, MATRIX_DECAY),
+        (norm_own, norm_mean, norm_square, NORM_RATE, 0.0),
+        (embed_own, embed_mean, embed_square, EMBED_RATE, 0.0),
     )
-    out_new = adam_step(
-        out_master, out_mean, out_square, reduced_out, MATRIX_RATE, MATRIX_DECAY, clip_scale
-    )
-    up_new = adam_step(
-        up_master, up_mean, up_square, reduced_up, MATRIX_RATE, MATRIX_DECAY, clip_scale
-    )
-    down_new = adam_step(
-        down_master, down_mean, down_square, reduced_down, MATRIX_RATE, MATRIX_DECAY, clip_scale
-    )
-    norm_new = adam_step(norm_own, norm_mean, norm_square, reduced_norm, NORM_RATE, 0.0, clip_scale)
-    embed_new = adam_step(
-        embed_own, embed_mean, embed_square, reduced_embed, EMBED_RATE, 0.0, clip_scale
-    )
-    return (output, input_grad, clip_norm) + (
-        qkv_new + out_new + up_new + down_new + norm_new + embed_new
-    )
+    new = ()
+    for (master, mean, square, rate, decay), grad in zip(state, reduced):
+        new += adam_step(master, mean, square, grad, rate, decay, clip_scale)
+    return (output, input_grad, clip_norm) + new
 
 
 def solution(mesh):

time: 276 us -> 194 us (0.70)
  waiting for transfers between devices: 52.8 us -> 26.6 us
  Pallas kernels: 131 us -> 116 us
  other arithmetic: 22.2 us -> 7.72 us
  starting transfers between devices: 43.2 us -> 31.6 us
  local copies, waits for them, and re-layouts: 19.6 us -> 9.94 us
  between operations: 6.23 us -> 0.96 us
    ppermute x24 -> x6, starting transfers between devices: 30.4 us -> 7.67 us  [hop(): return lax.ppermute(value, 'dp', [(i, i ^ flip) for i in range(size)])]
    ppermute x24 -> x6, waiting for transfers between devices: 36.6 us -> 18 us  [hop(): return lax.ppermute(value, 'dp', [(i, i ^ flip) for i in range(size)])]
    pallas_call x2, Pallas kernels: 45.4 us -> 34.5 us  [middle(): pl.pallas_call(middle_kernel, grid=(mols // PAIR,), out_shape=[jax.ShapeD...]
    all_to_all x1 -> x2, starting transfers between devices: 3.46 us -> 12.9 us  [the longest x1 8.02 us: on_device(): got1 = lax.all_to_all(sum1, 'dp', 0, 0, tiled=True)]
    unnamed x54 -> x23, local copies, waits for them, and re-layouts: 12.9 us -> 4.85 us
    all_to_all x1, waiting for transfers between devices: 7.94 us -> 0.01 us  [on_device(): got = lax.all_to_all(small, ('dp', 'mp'), 0, 0, tiled=True)]
    reduce_sum x8 -> x0, other arithmetic: 6.6 us -> none  [the longest x1 1.41 us: on_device(): jnp.sum(lnacc_a, axis=2)]
    sub x5 -> x0, other arithmetic: 4.69 us -> none  [adam_step(): master - rate * (mean_hat / (jnp.sqrt(square_hat) + ADAM_EPS) + decay * m...]
  transfers between devices with their start and end apart: 32 -> 15, of which waited for: 15 -> 6; matrix products, arithmetic and copies ran while one was open for 10% -> 5% of each run, Pallas kernels for 23% -> 20%
where the time goes in v2:
time: 194 us; the launch traced here: 193 us
  Pallas kernels  116 us (60%)
  starting transfers between devices  31.6 us (16%)
  waiting for transfers between devices  26.6 us (14%)
  local copies, waits for them, and re-layouts  9.94 us (5%)
  other arithmetic  7.72 us (4%)
    pallas_call x1, Pallas kernels, front(): pl.pallas_call(front_kernel, grid=(mols // PAIR,), out_shape=[o[0] for o...  54.2 us
    pallas_call x2, Pallas kernels, middle(): pl.pallas_call(middle_kernel, grid=(mols // PAIR,), out_shape=[jax.ShapeD...  34.5 us
    ppermute x6, waiting for transfers between devices, hop(): return lax.ppermute(value, 'dp', [(i, i ^ flip) for i in range(size)])  18 us
    pallas_call x1, Pallas kernels, back(): pl.pallas_call(back_kernel, grid=(mols // PAIR,), out_shape=[jax.ShapeDty...  14.7 us
    all_to_all x1, starting transfers between devices, on_device(): got = lax.all_to_all(small, ('dp', 'mp'), 0, 0, tiled=True)  9.01 us
    all_to_all x1, starting transfers between devices, on_device(): got1 = lax.all_to_all(sum1, 'dp', 0, 0, tiled=True)  8.02 us
    ppermute x6, starting transfers between devices, hop(): return lax.ppermute(value, 'dp', [(i, i ^ flip) for i in range(size)])  7.67 us
    pallas_call x1, Pallas kernels, embed(): pl.pallas_call(embed_kernel, grid=(mols // PAIR,), out_shape=[jax.ShapeDt...  7.17 us
  transfers between devices with their start and end apart: 15, of which 6 were waited for; matrix products, arithmetic and copies ran while one was open for 5% of the time, Pallas kernels for 20%

profile of v2, /device:TPU:0, one launch (start us, length us, event | category | flops | bytes accessed | tf_op | source)
XLA Modules:
  0.0 193.1 jit_solution(4340294086048384259)
XLA Ops:
  1.8 7.2 %embed.1 = (f32[768,1024]{1,0:T(8,128)}, bf16[768,1024]{1,0:T(8,128)(2,1)}, bf16[256,1024]{1,0:T(8,128)(2,1)}, bf16[768,1024]{1,0:T(8,128)(2,1)}) custom-call(bf16[8,128,768]{2,1,0:T(8,128)(2,1)} %tok_ref.1, bf16[8,128,768]{2,1,0:T(8,128)(2,1)} %cot_ref.1, s32[8,1,128]{2,1,0:T(1,128)} %bitcast.63, s32[8,2,128]{2,1,0:T(2,128)} %bitcast.62, ...), custom_call_target="tpu_custom_call" | custom-call | flops 8000000000 | bytes 10000000 | tf_op jit(solution)/shard_map/embed/pallas_call | solution.py:529
  10.7 54.2 %front.1 = (bf16[8,128,768]{2,1,0:T(8,128)(2,1)}, f32[768,1024]{1,0:T(8,128)}, bf16[8,1024,128]{2,1,0:T(8,128)(2,1)}, bf16[8,1024,128]{2,1,0:T(8,128)(2,1)}, bf1...) custom-call(s32[8]{0:T(128)} %len_ref.1, ...), custom_call_target="tpu_custom_call" | custom-call | flops 60000002048 | bytes 50000000 | tf_op jit(solution)/shard_map/front/pallas_call | solution.py:578
  65.4 3.5 %collective-permute-done.4 = bf16[16,48,1152]{2,1,0:T(8,128)(2,1)S(1)} collective-permute-done((bf16[16,48,1152]{2,1,0:T(8,128)(2,1)}, bf16[16,48,1152]{2,1,0:T(8,128)(2,1)S(1)}, u32[]{:S(2)}, u32[]{:S(2)}) %collective-permute-start.4) | collective-permute-done | bytes 1769504 | tf_op jit(solution)/shard_map/ppermute | solution.py:699
  68.9 3.1 %add_convert_fusion.1 = bf16[16,48,1152]{2,1,0:T(8,128)(2,1)} fusion(bf16[16,48,1152]{2,1,0:T(8,128)(2,1)S(1)} %collective-permute-done.4, bf16[16,48,1152]{2,1,0:T(8,128)(2,1)} %get-tuple-element.80), kind=kLoop, calls=%fused_computation.1 | loop fusion | flops 3538944 | bytes 5308416 | tf_op jit(solution)/shard_map/convert_element_type | solution.py:776
  72.1 17.3 %middle.3 = (bf16[1152,1024]{1,0:T(8,128)(2,1)}, bf16[16,48,1152]{2,1,0:T(8,128)(2,1)}) custom-call(bf16[768,1024]{1,0:T(8,128)(2,1)} %get-tuple-element.74.na_ref, bf16[8,1024,128]{2,1,0:T(8,128)(2,1)} %get-tuple-element.77.q_ref, bf16[8,1024,128]{2,1,0:T(8,128)(2,1)} %get-tuple-element.78.k_ref, bf16[8,1024,128]{2,1,0:T(8,128)(2,1)} %get-tuple-element.79.v_ref, ...), custom_call_target="tpu_custom_call" | custom-call | flops 20000000000 | bytes 12000000 | tf_op jit(solution)/shard_map/middle/pallas_call | solution.py:614
  89.7 8.0 %all-to-all-start = ((bf16[16,48,1152]{2,1,0:T(8,128)(2,1)}), bf16[16,48,1152]{2,1,0:T(8,128)(2,1)S(1)}, u32[]{:S(2)}, u32[]{:S(2)}) async-start(bf16[16,48,1152]{2,1,0:T(8,128)(2,1)} %add_convert_fusion.1), calls=%async_computation | async-start | bytes 3538944 | tf_op jit(solution)/shard_map/all_to_all | solution.py:779
  97.8 17.2 %middle.2 = (bf16[1152,1024]{1,0:T(8,128)(2,1)}, bf16[16,48,1152]{2,1,0:T(8,128)(2,1)}) custom-call(bf16[768,1024]{1,0:T(8,128)(2,1)} %get-tuple-element.74.na_ref, bf16[8,1024,128]{2,1,0:T(8,128)(2,1)} %get-tuple-element.77.q_ref, bf16[8,1024,128]{2,1,0:T(8,128)(2,1)} %get-tuple-element.78.k_ref, bf16[8,1024,128]{2,1,0:T(8,128)(2,1)} %get-tuple-element.79.v_ref, ...), custom_call_target="tpu_custom_call" | custom-call | flops 20000000000 | bytes 12000000 | tf_op jit(solution)/shard_map/middle/pallas_call | solution.py:614
  116.2 2.4 %add_convert_fusion = bf16[16,48,1152]{2,1,0:T(8,128)(2,1)S(1)} fusion(bf16[16,48,1152]{2,1,0:T(8,128)(2,1)} %copy-done.1, bf16[16,48,1152]{2,1,0:T(8,128)(2,1)} %get-tuple-element.85), kind=kLoop, calls=%fused_computation | loop fusion | flops 3538944 | bytes 5308416 | tf_op jit(solution)/shard_map/convert_element_type | solution.py:783
  119.8 1.9 collective-permute-start.6
  121.7 1.5 collective-permute-start.7
  123.3 14.7 %back.1 = (f32[8,128,768]{2,1,0:T(8,128)}, f32[32,8,128]{2,1,0:T(8,128)}) custom-call(bf16[1152,1024]{1,0:T(8,128)(2,1)} %get-tuple-element.88.dxo_ref, bf16[1152,1024]{1,0:T(8,128)(2,1)} %get-tuple-element.89.dxp_ref, bf16[3,768,384]{2,1,0:T(8,128)(2,1)} %bitcast.54, bf16[3,768,384]{2,1,0:T(8,128)(2,1)} %copy-done.7, f32[768,1024]{1,0:T(8,128)} %get-tuple-element.73.h0_ref, ...), custom_call_target="tpu_custom_call" | custom-call | flops 17999998976 | bytes 15000000 | tf_op jit(solution)/shard_map/back/pallas_call | solution.py:642
  138.0 1.5 collective-permute-done.6
  139.4 8.4 %collective-permute-done.7 = bf16[4,48,1152]{2,1,0:T(8,128)(2,1)} collective-permute-done((bf16[4,48,1152]{2,1,0:T(8,128)(2,1)}, bf16[4,48,1152]{2,1,0:T(8,128)(2,1)}, u32[]{:S(2)}, u32[]{:S(2)}) %collective-permute-start.7) | collective-permute-done | bytes 442400 | tf_op jit(solution)/shard_map/ppermute | solution.py:704
  147.8 2.1 %fusion.2 = bf16[4,48,1152]{2,1,0:T(8,128)(2,1)} fusion(bf16[4,48,1152]{2,1,0:T(8,128)(2,1)} %collective-permute-done.8, bf16[4,48,1152]{2,1,0:T(8,128)(2,1)} %collective-permute-done.7, bf16[4,48,1152]{2,1,0:T(8,128)(2,1)S(1)} %collective-permute-done.6, bf16[4,4,48,1152]{3,2,1,0:T(8,128)(2,1)S(1)} %bitcast.43, s32[]{:T(128)S(6)} %select_n.33), kind=kLoop, calls=%fused_computation.5 | loop fusion | flops 1769472 | bytes 2211844 | tf_op jit(solution)/shard_map/convert_element_type | solution.py:802
  150.0 9.0 %all-to-all-start.1 = ((f32[32,8,128]{2,1,0:T(8,128)}), f32[32,8,128]{2,1,0:T(8,128)S(1)}, u32[]{:S(2)}, u32[]{:S(2)}) async-start(f32[32,8,128]{2,1,0:T(8,128)} %get-tuple-element.101), calls=%async_computation.1 | async-start | bytes 262144 | tf_op jit(solution)/shard_map/all_to_all | solution.py:804
  159.0 1.7 dynamic-slice_bitcast_fusion.3
  160.8 2.7 %collective-permute-start.10 = (bf16[48,1152]{1,0:T(8,128)(2,1)S(1)}, bf16[48,1152]{1,0:T(8,128)(2,1)S(1)}, u32[]{:S(2)}, u32[]{:S(2)}) collective-permute-start(bf16[48,1152]{1,0:T(8,128)(2,1)S(1)} %get-tuple-element.129), channel_id=1, source_target_pairs={{0,16},{2,18},{4,20},{6,22},{8,24},{10,26},{12,28},{14,30},{16,0},... | collective-permute-start | bytes 331784 | tf_op jit(solution)/shard_map/ppermute | solution.py:704
  163.4 1.5 collective-permute-start.11
  165.8 7.1 %collective-permute-done.10.b_ref = bf16[48,1152]{1,0:T(8,128)(2,1)S(1)} collective-permute-done((bf16[48,1152]{1,0:T(8,128)(2,1)S(1)}, bf16[48,1152]{1,0:T(8,128)(2,1)S(1)}, u32[]{:S(2)}, u32[]{:S(2)}) %collective-permute-start.10) | collective-permute-done | bytes 110624 | tf_op jit(solution)/shard_map/ppermute | solution.py:704
  174.6 2.8 %gather.1 = (f32[48,1152]{1,0:T(8,128)}, f32[48,1152]{1,0:T(8,128)}, f32[8,128]{1,0:T(8,128)}, f32[32,128]{1,0:T(8,128)}) custom-call(bf16[16,48,1152]{2,1,0:T(8,128)(2,1)} %copy-done, bf16[48,1152]{1,0:T(8,128)(2,1)} %get-tuple-element.131.own_ref, bf16[48,1152]{1,0:T(8,128)(2,1)} %copy-done.5, bf16[48,1152]{1,0:T(8,128)(2,1)} %copy-done.3, ...), custom_call_target="tpu_custom_call" | custom-call | tf_op jit(solution)/shard_map/gather/pallas_call | solution.py:675
  177.4 4.9 %all-to-all-start.2 = ((f32[32,1,128]{2,1,0:T(1,128)}), f32[32,1,128]{2,1,0:T(1,128)S(1)}, u32[]{:S(2)}, u32[]{:S(2)}) async-start(f32[32,1,128]{2,1,0:T(1,128)} %bitcast.49), calls=%async_computation.2 | async-start | bytes 32768 | tf_op jit(solution)/shard_map/all_to_all | solution.py:808
  182.3 1.4 constant_dynamic-slice_fusion.1.refs_16_
  184.3 5.0 %all-to-all-done.2 = f32[32,1,128]{2,1,0:T(1,128)S(1)} async-done(((f32[32,1,128]{2,1,0:T(1,128)}), f32[32,1,128]{2,1,0:T(1,128)S(1)}, u32[]{:S(2)}, u32[]{:S(2)}) %all-to-all-start.2) | async-done | bytes 16416 | tf_op jit(solution)/shard_map/all_to_all | solution.py:808
  190.0 2.9 %adam.1 = (f32[1,128]{1,0:T(1,128)}, f32[3,48,384]{2,1,0:T(8,128)}, f32[3,48,384]{2,1,0:T(8,128)}, f32[3,48,384]{2,1,0:T(8,128)}, f32[24,768]{1,0:T(8,128)}, /*i...) custom-call(f32[32,128]{1,0:T(8,128)} %bitcast.47, ...), custom_call_target="tpu_custom_call" | custom-call | tf_op jit(solution)/shard_map/adam/pallas_call | solution.py:689
  (43 shorter events, 10.1 us)
Async XLA Ops:
  0.7 8.3 %collective-permute-start = (bf16[3,768,384]{2,1,0:T(8,128)(2,1)}, bf16[3,768,384]{2,1,0:T(8,128)(2,1)S(1)}, u32[]{:S(2)}, u32[]{:S(2)}) collective-permute-start(bf16[3,768,384]{2,1,0:T(8,128)(2,1)} %bitcast.52), channel_id=1, source_target_pairs={{0,1},{1,0},{2,3},{3,2},{4,5},{5,4},{6,7},{7,6},{8,9},{9,8},{10,11... | collective-permute-start | bytes 5308424 | tf_op jit(solution)/shard_map/ppermute | solution.py:699
  1.2 7.8 %collective-permute-start.1 = (bf16[384,768]{1,0:T(8,128)(2,1)}, bf16[384,768]{1,0:T(8,128)(2,1)S(1)}, u32[]{:S(2)}, u32[]{:S(2)}) collective-permute-start(bf16[384,768]{1,0:T(8,128)(2,1)} %out_o.1), channel_id=1, source_target_pairs={{0,1},{1,0},{2,3},{3,2},{4,5},{5,4},{6,7},{7,6},{8,9},{9,8},{10,11... | collective-permute-start | bytes 1769480 | tf_op jit(solution)/shard_map/ppermute | solution.py:699
  1.3 7.7 %collective-permute-start.2 = (bf16[768,384]{1,0:T(8,128)(2,1)}, bf16[768,384]{1,0:T(8,128)(2,1)S(1)}, u32[]{:S(2)}, u32[]{:S(2)}) collective-permute-start(bf16[768,384]{1,0:T(8,128)(2,1)} %up_o.1), channel_id=1, source_target_pairs={{0,1},{1,0},{2,3},{3,2},{4,5},{5,4},{6,7},{7,6},{8,9},{9,8},{10,11... | collective-permute-start | bytes 1769480 | tf_op jit(solution)/shard_map/ppermute | solution.py:699
  1.7 7.3 %collective-permute-start.3 = (bf16[384,768]{1,0:T(8,128)(2,1)}, bf16[384,768]{1,0:T(8,128)(2,1)S(1)}, u32[]{:S(2)}, u32[]{:S(2)}) collective-permute-start(bf16[384,768]{1,0:T(8,128)(2,1)} %down_o.1), channel_id=1, source_target_pairs={{0,1},{1,0},{2,3},{3,2},{4,5},{5,4},{6,7},{7,6},{8,9},{9,8},{10,11... | collective-permute-start | bytes 1769480 | tf_op jit(solution)/shard_map/ppermute | solution.py:699
  8.9 0.8 copy-start.8
  9.0 1.0 copy-start.9
  9.0 1.2 copy-start.10
  9.0 1.7 copy-start.7
  64.9 4.0 %collective-permute-start.4 = (bf16[16,48,1152]{2,1,0:T(8,128)(2,1)}, bf16[16,48,1152]{2,1,0:T(8,128)(2,1)S(1)}, u32[]{:S(2)}, u32[]{:S(2)}) collective-permute-start(bf16[16,48,1152]{2,1,0:T(8,128)(2,1)} %get-tuple-element.81), channel_id=1, source_target_pairs={{0,1},{1,0},{2,3},{3,2},{4,5},{5,4},{6,7},{7,6},{8,9},{9,8},{10,11... | collective-permute-start | bytes 5308424 | tf_op jit(solution)/shard_map/ppermute | solution.py:699
  89.4 25.6 %collective-permute-start.5 = (bf16[16,48,1152]{2,1,0:T(8,128)(2,1)}, bf16[16,48,1152]{2,1,0:T(8,128)(2,1)S(1)}, u32[]{:S(2)}, u32[]{:S(2)}) collective-permute-start(bf16[16,48,1152]{2,1,0:T(8,128)(2,1)} %get-tuple-element.86), channel_id=1, source_target_pairs={{0,1},{1,0},{2,3},{3,2},{4,5},{5,4},{6,7},{7,6},{8,9},{9,8},{10,11... | collective-permute-start | bytes 5308424 | tf_op jit(solution)/shard_map/ppermute | solution.py:699
  89.7 60.3 %all-to-all-start = ((bf16[16,48,1152]{2,1,0:T(8,128)(2,1)}), bf16[16,48,1152]{2,1,0:T(8,128)(2,1)S(1)}, u32[]{:S(2)}, u32[]{:S(2)}) async-start(bf16[16,48,1152]{2,1,0:T(8,128)(2,1)} %add_convert_fusion.1), calls=%async_computation | async-start | bytes 3538944 | tf_op jit(solution)/shard_map/all_to_all | solution.py:779
  115.0 1.2 copy-start.1
  119.8 19.6 %collective-permute-start.6 = (bf16[4,48,1152]{2,1,0:T(8,128)(2,1)}, bf16[4,48,1152]{2,1,0:T(8,128)(2,1)S(1)}, u32[]{:S(2)}, u32[]{:S(2)}) collective-permute-start(bf16[4,48,1152]{2,1,0:T(8,128)(2,1)} %get-tuple-element.96), channel_id=1, source_target_pairs={{0,2},{2,0},{4,6},{6,4},{8,10},{10,8},{12,14},{14,12},{16,18},{18,... | collective-permute-start | bytes 1327112 | tf_op jit(solution)/shard_map/ppermute | solution.py:704
  121.7 26.1 %collective-permute-start.7 = (bf16[4,48,1152]{2,1,0:T(8,128)(2,1)}, bf16[4,48,1152]{2,1,0:T(8,128)(2,1)}, u32[]{:S(2)}, u32[]{:S(2)}) collective-permute-start(bf16[4,48,1152]{2,1,0:T(8,128)(2,1)} %get-tuple-element.97), channel_id=1, source_target_pairs={{0,4},{2,6},{4,0},{6,2},{8,12},{10,14},{12,8},{14,10},{16,20},{18,... | collective-permute-start | bytes 1327112 | tf_op jit(solution)/shard_map/ppermute | solution.py:704
  123.2 24.7 %collective-permute-start.8 = (bf16[4,48,1152]{2,1,0:T(8,128)(2,1)}, bf16[4,48,1152]{2,1,0:T(8,128)(2,1)}, u32[]{:S(2)}, u32[]{:S(2)}) collective-permute-start(bf16[4,48,1152]{2,1,0:T(8,128)(2,1)} %get-tuple-element.98), channel_id=1, source_target_pairs={{0,6},{2,4},{4,2},{6,0},{8,14},{10,12},{12,10},{14,8},{16,22},{18,... | collective-permute-start | bytes 1327112 | tf_op jit(solution)/shard_map/ppermute | solution.py:704
  150.0 24.0 %copy-start = (bf16[16,48,1152]{2,1,0:T(8,128)(2,1)}, bf16[16,48,1152]{2,1,0:T(8,128)(2,1)S(1)}, u32[]{:S(2)}) copy-start(bf16[16,48,1152]{2,1,0:T(8,128)(2,1)S(1)} %all-to-all-done.got1_ref) | copy-start | bytes 5308420
  150.0 23.9 %all-to-all-start.1 = ((f32[32,8,128]{2,1,0:T(8,128)}), f32[32,8,128]{2,1,0:T(8,128)S(1)}, u32[]{:S(2)}, u32[]{:S(2)}) async-start(f32[32,8,128]{2,1,0:T(8,128)} %get-tuple-element.101), calls=%async_computation.1 | async-start | bytes 262144 | tf_op jit(solution)/shard_map/all_to_all | solution.py:804
  160.8 12.1 %collective-permute-start.10 = (bf16[48,1152]{1,0:T(8,128)(2,1)S(1)}, bf16[48,1152]{1,0:T(8,128)(2,1)S(1)}, u32[]{:S(2)}, u32[]{:S(2)}) collective-permute-start(bf16[48,1152]{1,0:T(8,128)(2,1)S(1)} %get-tuple-element.129), channel_id=1, source_target_pairs={{0,16},{2,18},{4,20},{6,22},{8,24},{10,26},{12,28},{14,30},{16,0},... | collective-permute-start | bytes 331784 | tf_op jit(solution)/shard_map/ppermute | solution.py:704
  163.4 9.4 %collective-permute-start.11 = (bf16[48,1152]{1,0:T(8,128)(2,1)S(1)}, bf16[48,1152]{1,0:T(8,128)(2,1)S(1)}, u32[]{:S(2)}, u32[]{:S(2)}) collective-permute-start(bf16[48,1152]{1,0:T(8,128)(2,1)S(1)} %get-tuple-element.128), channel_id=1, source_target_pairs={{0,24},{2,26},{4,28},{6,30},{8,16},{10,18},{12,20},{14,22},{16,8},... | collective-permute-start | bytes 331784 | tf_op jit(solution)/shard_map/ppermute | solution.py:704
  164.9 9.0 %collective-permute-start.9 = (bf16[48,1152]{1,0:T(8,128)(2,1)S(1)}, bf16[48,1152]{1,0:T(8,128)(2,1)S(1)}, u32[]{:S(2)}, u32[]{:S(2)}) collective-permute-start(bf16[48,1152]{1,0:T(8,128)(2,1)S(1)} %get-tuple-element.130), channel_id=1, source_target_pairs={{0,8},{2,10},{4,12},{6,14},{8,0},{10,2},{12,4},{14,6},{16,24},{18,... | collective-permute-start | bytes 331784 | tf_op jit(solution)/shard_map/ppermute | solution.py:704
  172.9 1.1 copy-start.3
  172.9 1.1 copy-start.4
  173.9 0.7 copy-start.2
  177.4 12.0 %all-to-all-start.2 = ((f32[32,1,128]{2,1,0:T(1,128)}), f32[32,1,128]{2,1,0:T(1,128)S(1)}, u32[]{:S(2)}, u32[]{:S(2)}) async-start(f32[32,1,128]{2,1,0:T(1,128)} %bitcast.49), calls=%async_computation.2 | async-start | bytes 32768 | tf_op jit(solution)/shard_map/all_to_all | solution.py:808
  (2 other events, 1.2 us)

commit v3 on v2

--- a/solution.py
+++ b/solution.py
@@ -28,6 +28,8 @@
 IDENT_USED = 34
 PAIR = 2
 VMEM_BYTES = 60 * 1024 * 1024
+FRONT_UNROLL = 8
+MIDDLE_UNROLL = 8
 
 F32 = jnp.float32
 BF16 = jnp.bfloat16
@@ -150,6 +152,25 @@
         ct_ref[:, lanes] = cot_ref[j].T
 
 
+def block_pair(rows):
+    zero = jnp.zeros((PAD_DIM, rows.shape[1]), rows.dtype)
+    left = jnp.concatenate([rows[0:PAD_DIM], zero], axis=0)
+    right = jnp.concatenate([zero, rows[PAD_DIM:]], axis=0)
+    return jnp.concatenate([left, right], axis=1)
+
+
+def staged(at, first, second, third):
+    one, two = {}, {}
+    count = len(at)
+    for n in range(count + 2):
+        if n < count:
+            one[n] = first(*at[n])
+        if 0 <= n - 1 < count:
+            two[n - 1] = second(*at[n - 1], one.pop(n - 1))
+        if 0 <= n - 2 < count:
+            third(*at[n - 2], two.pop(n - 2))
+
+
 def front_kernel(
     len_ref,
     h0_ref,
@@ -164,8 +185,9 @@
     up_p,
     down_o,
     down_p,
-    output_ref,
     gh1_ref,
+    h1_s,
+    act_s,
     q_ref,
     k_ref,
     v_ref,
@@ -177,34 +199,37 @@
     qkvt,
     outt,
     upt,
-    downt,
+    outw,
+    upw,
+    downw,
     nb,
-    act_s,
     nbt_s,
     gp_s,
     mix_s,
     ga_s,
     mixf,
-    h1_s,
     nrm_s,
-    dgel_s,
     rec_s,
 ):
     step = pl.program_id(0)
     steps = pl.num_programs(0)
-    slots = output_ref.shape[1]
-    width = output_ref.shape[2]
+    slots = e_ref.shape[2]
+    width = h0_ref.shape[0]
     half = width // 2
     halves = ((qkv_o, out_o, up_o, down_o), (qkv_p, out_p, up_p, down_p))
 
     @pl.when(step == 0)
     def _():
         for h, (qkv, out, up, down) in enumerate(halves):
+            part = slice(h * half, (h + 1) * half)
             for c in range(3):
-                qkvt[h, c * half : (c + 1) * half, :] = qkv[c].T
-            outt[h] = out[...].T
-            upt[h] = up[...].T
-            downt[h] = down[...].T
+                at = (3 * h + c) * half
+                qkvt[at : at + half, :] = qkv[c].T
+            outt[:, part] = out[...].T
+            upt[part, :] = up[...].T
+            outw[part, :] = out[...]
+            upw[:, part] = up[...]
+            downw[part, :] = down[...]
         for row in range(2):
             nb[row] = lane_columns(norm_ref[row + 2 : row + 3, :], slots)
         lnacc_ref[...] = jnp.zeros_like(lnacc_ref)
@@ -212,114 +237,134 @@
     base = pl.multiple_of(step * PAIR * slots, PAIR * slots)
     span = pl.ds(base, PAIR * slots)
 
-    row_iota = lax.broadcasted_iota(jnp.int32, (8, slots), 0)
-    lane_iota = lax.broadcasted_iota(jnp.int32, (1, slots), 1)
-
-    one_row = jnp.where(row_iota == 0, 1.0, 0.0)
-    two_rows = jnp.where(row_iota < 2, 1.0, 0.0)
-    for h in range(2):
-        proj = dot_nn(qkvt[h], na_ref[...])
-        rows = slice(h * (half // HEAD_DIM) * PAD_DIM, (h + 1) * (half // HEAD_DIM) * PAD_DIM)
+    phase = pl.when(step >= 0)
+    groups = width // (4 * HEAD_DIM)
+    inv = 1.0 / width
+    parts = tuple(slice(h * half, (h + 1) * half) for h in range(2))
+    sides = tuple(slice(j * slots, (j + 1) * slots) for j in range(PAIR))
+    columns = tuple(
+        pl.ds(pl.multiple_of(base + j * slots, slots), slots) for j in range(PAIR)
+    )
+
+    @phase
+    def _():
+        row_iota = lax.broadcasted_iota(jnp.int32, (8, slots), 0)
+        lane_iota = lax.broadcasted_iota(jnp.int32, (1, slots), 1)
+        one_row = jnp.where(row_iota == 0, 1.0, 0.0)
+        two_rows = jnp.where(row_iota < 2, 1.0, 0.0)
+        padded = half // HEAD_DIM * PAD_DIM
+        for h in range(2):
+            rows = slice(h * padded, (h + 1) * padded)
+            for c, ref in enumerate((q_ref, k_ref, v_ref)):
+                at = (3 * h + c) * half
+                proj = dot_nn(qkvt[at : at + half, :], na_ref[...])
+                for j in range(PAIR):
+                    own = proj[:, sides[j]]
+                    if c == 0:
+                        own, tail = own * (SCORE_SCALE * LOG2E), one_row
+                    elif c == 1:
+                        length = len_ref[step * PAIR + j]
+                        bias = jnp.where(lane_iota < length, 0.0, MASK_VALUE)
+                        tail = jnp.where(row_iota == 0, bias, 0.0)
+                    else:
+                        tail = two_rows
+                    ref[j, rows, :] = head_rows(own, tail).astype(BF16)
+
+    def score(j, g):
+        rows = pl.ds(pl.multiple_of(g * 4 * PAD_DIM, 4 * PAD_DIM), 4 * PAD_DIM)
+        return dot_nn(k_ref[j, rows, :].T, block_columns(q_ref[j, rows, :]))
+
+    def weigh(j, g, scores):
+        exps = []
+        for a in range(4):
+            own = scores[:, a * slots : (a + 1) * slots]
+            ex = jnp.exp2(own - jnp.max(own, axis=0, keepdims=True)).astype(BF16)
+            e_ref[j, g * 4 + a] = ex
+            exps.append(ex)
+        return exps
+
+    def mix_values(j, g, exps):
+        rows = pl.ds(pl.multiple_of(g * 4 * PAD_DIM, 4 * PAD_DIM), 4 * PAD_DIM)
+        vals = v_ref[j, rows, :]
+        mixes = []
+        for a in range(0, 4, 2):
+            two = dot_nn(
+                vals[a * PAD_DIM : (a + 2) * PAD_DIM], jnp.concatenate(exps[a : a + 2], axis=1)
+            )
+            for b in range(2):
+                got = two[b * PAD_DIM : (b + 1) * PAD_DIM, b * slots : (b + 1) * slots]
+                rec = 1.0 / got[HEAD_DIM : HEAD_DIM + 1]
+                rec_s[j, g, a + b : a + b + 1, :] = rec
+                mixes.append(got[0:HEAD_DIM] * rec)
+        out_rows = pl.ds(pl.multiple_of(g * 4 * HEAD_DIM, 4 * HEAD_DIM), 4 * HEAD_DIM)
+        mixf[j, out_rows, :] = jnp.concatenate(mixes, axis=0)
+
+    def attend(i, carry):
+        at = [i * FRONT_UNROLL + u for u in range(FRONT_UNROLL)]
+        at = [(lax.div(n, groups), lax.rem(n, groups)) for n in at]
+        staged(at, score, weigh, mix_values)
+        return carry
+
+    lax.fori_loop(0, PAIR * groups // FRONT_UNROLL, attend, 0)
+
+    @phase
+    def _():
         for j in range(PAIR):
-            lanes = slice(j * slots, (j + 1) * slots)
-            length = len_ref[step * PAIR + j]
-            bias = jnp.where(lane_iota < length, 0.0, MASK_VALUE)
-            bias_row = jnp.where(row_iota == 0, bias, 0.0)
-            q = proj[0:half, lanes] * (SCORE_SCALE * LOG2E)
-            q_ref[j, rows, :] = head_rows(q, one_row).astype(BF16)
-            k_ref[j, rows, :] = head_rows(proj[half : 2 * half, lanes], bias_row).astype(BF16)
-            v_ref[j, rows, :] = head_rows(proj[2 * half :, lanes], two_rows).astype(BF16)
-
-    groups = width // (4 * HEAD_DIM)
-    for j in range(PAIR):
-        lanes = slice(j * slots, (j + 1) * slots)
-
-        def attend(g, carry, j=j, lanes=lanes):
-            rows = pl.ds(pl.multiple_of(g * 4 * PAD_DIM, 4 * PAD_DIM), 4 * PAD_DIM)
-            keys = k_ref[j, rows, :].T
-            vals = v_ref[j, rows, :]
-            scores = dot_nn(keys, block_columns(q_ref[j, rows, :]))
-            mixes, recs = [], []
-            for a in range(4):
-                own = scores[:, a * slots : (a + 1) * slots]
-                top = jnp.max(own, axis=0, keepdims=True)
-                ex = jnp.exp2(own - top).astype(BF16)
-                e_ref[j, g * 4 + a] = ex
-                got = dot_nn(vals[a * PAD_DIM : (a + 1) * PAD_DIM], ex)
-                rec = 1.0 / got[HEAD_DIM : HEAD_DIM + 1]
-                rec_s[j, g, a : a + 1, :] = rec
-                mixes.append(got[0:HEAD_DIM] * rec)
-            out_rows = pl.ds(pl.multiple_of(g * 4 * HEAD_DIM, 4 * HEAD_DIM), 4 * HEAD_DIM)
-            mixf[out_rows, lanes] = jnp.concatenate(mixes, axis=0)
-            return carry
-
-        lax.fori_loop(0, groups, attend, 0, unroll=4)
-
-    mix = mixf[...].astype(BF16)
-    mix_s[:, span] = mix
-    attn = dot_nn(outt[0], mix[0:half]) + dot_nn(outt[1], mix[half:])
-    for j in range(PAIR):
-        lanes = slice(j * slots, (j + 1) * slots)
-        h1 = h0_ref[:, lanes] + attn[:, lanes]
-        h1_s[:, lanes] = h1
-        centred, rec = norm_parts(h1)
-        unit = centred * rec
-        nrm_s[:, lanes] = unit
-        rec_s[j, groups, 0:1, :] = rec
-        nbt_s[:, pl.ds(pl.multiple_of(base + j * slots, slots), slots)] = (
-            unit * nb[0] + nb[1]
-        ).astype(BF16)
-
-    for h in range(2):
-        rows = slice(h * half, (h + 1) * half)
-        act, slope = gelu_parts(dot_nn(upt[h], nbt_s[:, span]))
-        act_s[rows, span] = act.astype(BF16)
-        dgel_s[rows, :] = slope
-    ffn = dot_nn(downt[0], act_s[0:half, span]) + dot_nn(downt[1], act_s[half:, span])
-    for j in range(PAIR):
-        lanes = slice(j * slots, (j + 1) * slots)
-        output_ref[j] = (h1_s[:, lanes] + ffn[:, lanes]).astype(BF16).T
-
-    for h in range(2):
-        rows = slice(h * half, (h + 1) * half)
-        back = dot_nn(halves[h][3][...], cot_s[:, span])
-        gp_s[rows, span] = (back * dgel_s[rows, :]).astype(BF16)
-    grad_b = dot_nn(up_o[...], gp_s[0:half, span]) + dot_nn(up_p[...], gp_s[half:, span])
-    inv = 1.0 / width
-    for j in range(PAIR):
-        lanes = slice(j * slots, (j + 1) * slots)
-        cols = pl.ds(pl.multiple_of(base + j * slots, slots), slots)
-        gb = grad_b[:, lanes]
-        unit = nrm_s[:, lanes]
-        lnacc_ref[0] += gb * unit
-        lnacc_ref[1] += gb
-        f = gb * nb[0]
-        f_mean = jnp.sum(f, axis=0, keepdims=True) * inv
-        fn_mean = jnp.sum(f * unit, axis=0, keepdims=True) * inv
-        gh1 = cot_s[:, cols].astype(F32) + rec_s[j, groups, 0:1, :] * (
-            f - f_mean - unit * fn_mean
-        )
-        gh1_ref[:, lanes] = gh1
-        ga_s[:, cols] = gh1.astype(BF16)
-
-    for h in range(2):
-        gm = dot_nn(halves[h][1][...], ga_s[:, span])
+            mix_s[:, columns[j]] = mixf[j].astype(BF16)
+        attn = jnp.concatenate([dot_nn(outt[part, :], mix_s[:, span]) for part in parts], axis=0)
         for j in range(PAIR):
-            lanes = slice(j * slots, (j + 1) * slots)
-            for g in range(groups // 2):
-                at = h * (groups // 2) + g
-                grad = gm[g * 96 : (g + 1) * 96, lanes].reshape(4, HEAD_DIM, slots)
-                mixed = mixf[at * 96 : (at + 1) * 96, lanes].reshape(4, HEAD_DIM, slots)
-                rec = rec_s[j, at].reshape(8, 1, slots)[0:4]
-                inner = -(jnp.sum(grad * mixed, axis=1, keepdims=True) * rec)
-                high = inner.astype(BF16).astype(F32)
-                low = inner - high
-                rows8 = lax.broadcasted_iota(jnp.int32, (4, 8, slots), 1)
-                tail = jnp.where(rows8 == 0, high, jnp.where(rows8 == 1, low, 0.0))
-                full = jnp.concatenate([grad * rec, tail], axis=1)
-                do_ref[j, at * 128 : (at + 1) * 128, :] = (
-                    full.reshape(4 * PAD_DIM, slots).astype(BF16)
-                )
+            h1 = h0_ref[:, sides[j]] + attn[:, sides[j]]
+            h1_s[:, sides[j]] = h1
+            centred, rec = norm_parts(h1)
+            unit = centred * rec
+            nrm_s[:, sides[j]] = unit
+            rec_s[j, groups, 0:1, :] = rec
+            nbt_s[:, columns[j]] = (unit * nb[0] + nb[1]).astype(BF16)
+
+    @phase
+    def _():
+        for part in parts:
+            act, slope = gelu_parts(dot_nn(upt[part, :], nbt_s[:, span]))
+            act_s[part, span] = act.astype(BF16)
+            back = dot_nn(downw[part, :], cot_s[:, span])
+            gp_s[part, span] = (back * slope).astype(BF16)
+
+    @phase
+    def _():
+        grad_b = jnp.concatenate([dot_nn(upw[part, :], gp_s[:, span]) for part in parts], axis=0)
+        for j in range(PAIR):
+            gb = grad_b[:, sides[j]]
+            unit = nrm_s[:, sides[j]]
+            lnacc_ref[0] += gb * unit
+            lnacc_ref[1] += gb
+            f = gb * nb[0]
+            f_mean = jnp.sum(f, axis=0, keepdims=True) * inv
+            fn_mean = jnp.sum(f * unit, axis=0, keepdims=True) * inv
+            gh1 = cot_s[:, columns[j]].astype(F32) + rec_s[j, groups, 0:1, :] * (
+                f - f_mean - unit * fn_mean
+            )
+            gh1_ref[:, sides[j]] = gh1
+            ga_s[:, columns[j]] = gh1.astype(BF16)
+
+    @phase
+    def _():
+        rows8 = lax.broadcasted_iota(jnp.int32, (4, 8, slots), 1)
+        for h, part in enumerate(parts):
+            gm = dot_nn(outw[part, :], ga_s[:, span])
+            for j in range(PAIR):
+                for g in range(groups // 2):
+                    at = h * (groups // 2) + g
+                    grad = gm[g * 96 : (g + 1) * 96, sides[j]].reshape(4, HEAD_DIM, slots)
+                    mixed = mixf[j, at * 96 : (at + 1) * 96, :].reshape(4, HEAD_DIM, slots)
+                    rec = rec_s[j, at].reshape(8, 1, slots)[0:4]
+                    inner = -(jnp.sum(grad * mixed, axis=1, keepdims=True) * rec)
+                    high = inner.astype(BF16).astype(F32)
+                    low = inner - high
+                    tail = jnp.where(rows8 == 0, high, jnp.where(rows8 == 1, low, 0.0))
+                    full = jnp.concatenate([grad * rec, tail], axis=1)
+                    do_ref[j, at * 128 : (at + 1) * 128, :] = (
+                        full.reshape(4 * PAD_DIM, slots).astype(BF16)
+                    )
 
     @pl.when(step == steps - 1)
     def _():
@@ -339,51 +384,112 @@
 
 
 def middle_kernel(na_ref, q_ref, k_ref, v_ref, do_ref, e_ref, dx_ref, g_ref):
+    attention_back(q_ref, k_ref, v_ref, do_ref, e_ref, dx_ref)
+    half = dx_ref.shape[0] // 3
+
+    @pl.when(pl.program_id(0) == pl.num_programs(0) - 1)
+    def _():
+        for c in range(3):
+            cut = slice(c * half, (c + 1) * half)
+            grad = dot_nt(na_ref[...], dx_ref[cut, :])
+            g_ref[:, :, cut] = grad.reshape(g_ref.shape[0:2] + (half,)).astype(BF16)
+
+
+def middle_own_kernel(
+    plane_ref, na_ref, q_ref, k_ref, v_ref, do_ref, e_ref, got_ref, dx_ref, g0, g1, g2, g3, total
+):
+    attention_back(q_ref, k_ref, v_ref, do_ref, e_ref, dx_ref)
+    half = dx_ref.shape[0] // 3
+
+    @pl.when(pl.program_id(0) == pl.num_programs(0) - 1)
+    def _():
+        for c in range(3):
+            cut = slice(c * half, (c + 1) * half)
+            grad = dot_nt(na_ref[...], dx_ref[cut, :]).reshape(total.shape[0:2] + (half,))
+            total[:, :, cut] = (grad + got_ref[:, :, cut].astype(F32)).astype(BF16)
+        plane = plane_ref[0]
+        for k, g_ref in enumerate((g0, g1, g2, g3)):
+            for line in range(4):
+                g_ref[line] = total[line * 4 + (plane ^ k)]
+
+
+def attention_back(q_ref, k_ref, v_ref, do_ref, e_ref, dx_ref):
     step = pl.program_id(0)
-    steps = pl.num_programs(0)
     slots = q_ref.shape[2]
     half = dx_ref.shape[0] // 3
     base = pl.multiple_of(step * PAIR * slots, PAIR * slots)
     groups = half // (4 * HEAD_DIM)
-    for j in range(PAIR):
+
+    def rows_of(g):
+        return pl.ds(pl.multiple_of(g * 4 * PAD_DIM, 4 * PAD_DIM), 4 * PAD_DIM)
+
+    def score(j, g):
+        return dot_nn(v_ref[j, rows_of(g), :].T, block_columns(do_ref[j, rows_of(g), :]))
+
+    def weigh(j, g, back):
+        grads = []
+        for a in range(4):
+            ex = e_ref[j, g * 4 + a].astype(F32)
+            grads.append((ex * back[:, a * slots : (a + 1) * slots]).astype(BF16))
+        return grads
+
+    def products(j, g, grads):
+        dos = do_ref[j, rows_of(g), :]
+        qs = q_ref[j, rows_of(g), :]
+        ks = k_ref[j, rows_of(g), :]
+        dq, dk, dv = [], [], []
+        for a in range(0, 4, 2):
+            cut = slice(a * PAD_DIM, (a + 2) * PAD_DIM)
+            both = jnp.concatenate(grads[a : a + 2], axis=1)
+            exps = jnp.concatenate([e_ref[j, g * 4 + a + b].T for b in range(2)], axis=1)
+            two = dot_nn(ks[cut], both)
+            dq.append(two[0:HEAD_DIM, 0:slots])
+            dq.append(two[PAD_DIM : PAD_DIM + HEAD_DIM, slots:])
+            two = dot_nt(block_pair(qs[cut]), both)
+            dk.append(two[0:HEAD_DIM])
+            dk.append(two[PAD_DIM : PAD_DIM + HEAD_DIM])
+            two = dot_nn(dos[cut], exps)
+            dv.append(two[0:HEAD_DIM, 0:slots])
+            dv.append(two[PAD_DIM : PAD_DIM + HEAD_DIM, slots:])
         cols = pl.ds(pl.multiple_of(base + j * slots, slots), slots)
-
-        def attend(g, carry, j=j, cols=cols):
-            rows = pl.ds(pl.multiple_of(g * 4 * PAD_DIM, 4 * PAD_DIM), 4 * PAD_DIM)
-            vals = v_ref[j, rows, :].T
-            dos = do_ref[j, rows, :]
-            qs = q_ref[j, rows, :]
-            ks = k_ref[j, rows, :]
-            back = dot_nn(vals, block_columns(dos))
-            dq, dk, dv = [], [], []
-            for a in range(4):
-                cut = slice(a * PAD_DIM, (a + 1) * PAD_DIM)
-                ex = e_ref[j, g * 4 + a]
-                ds = (ex.astype(F32) * back[:, a * slots : (a + 1) * slots]).astype(BF16)
-                dq.append(dot_nn(ks[cut], ds)[0:HEAD_DIM])
-                dk.append(dot_nt(qs[cut], ds)[0:HEAD_DIM])
-                dv.append(dot_nt(dos[cut], ex)[0:HEAD_DIM])
-            for c, (parts, scale) in enumerate(((dq, SCORE_SCALE), (dk, LN2), (dv, None))):
-                at = pl.ds(pl.multiple_of(c * half + g * 96, 32), 96)
-                whole = jnp.concatenate(parts, axis=0)
-                if scale is not None:
-                    whole = whole * scale
-                dx_ref[at, cols] = whole.astype(BF16)
-            return carry
-
-        lax.fori_loop(0, groups, attend, 0, unroll=4)
-
-    @pl.when(step == steps - 1)
-    def _():
-        for c in range(3):
-            grad = dot_nt(na_ref[...], dx_ref[c * half : (c + 1) * half, :])
-            g_ref[:, :, c * half : (c + 1) * half] = grad.reshape(
-                g_ref.shape[0], g_ref.shape[1], half
-            ).astype(g_ref.dtype)
+        for c, (parts, scale) in enumerate(((dq, SCORE_SCALE), (dk, LN2), (dv, None))):
+            at = pl.ds(pl.multiple_of(c * half + g * 96, 32), 96)
+            whole = jnp.concatenate(parts, axis=0)
+            if scale is not None:
+                whole = whole * scale
+            dx_ref[at, cols] = whole.astype(BF16)
+
+    def attend(i, carry):
+        at = [i * MIDDLE_UNROLL + u for u in range(MIDDLE_UNROLL)]
+        at = [(lax.div(n, groups), lax.rem(n, groups)) for n in at]
+        staged(at, score, weigh, products)
+        return carry
+
+    lax.fori_loop(0, PAIR * groups // MIDDLE_UNROLL, attend, 0)
 
 
 def back_kernel(
-    dxo_ref, dxp_ref, qkv_o, qkv_p, h0_ref, gh1_ref, fs_ref, gain_ref, lnb_ref, ig_ref, small_ref, nb, lnacc, ge
+    dxo_ref,
+    dxp_ref,
+    qkv_o,
+    qkv_p,
+    h0_ref,
+    gh1_ref,
+    fs_ref,
+    gain_ref,
+    lnb_ref,
+    h1_ref,
+    act_ref,
+    down_o,
+    down_p,
+    ig_ref,
+    output_ref,
+    small_ref,
+    nb,
+    lnacc,
+    ge,
+    qkvw,
+    downt,
 ):
     step = pl.program_id(0)
     slots = ig_ref.shape[1]
@@ -396,12 +502,17 @@
         lnacc[...] = jnp.zeros_like(lnacc)
         ge[...] = jnp.zeros_like(ge)
         nb[...] = lane_columns(gain_ref[0:1, :], slots)
-
-    total = None
-    for qkv, dx in ((qkv_o, dxo_ref), (qkv_p, dxp_ref)):
-        for c in range(3):
-            part = dot_nn(qkv[c], dx[c * half : (c + 1) * half, :])
-            total = part if total is None else total + part
+        for h, (qkv, down) in enumerate(((qkv_o, down_o), (qkv_p, down_p))):
+            for c in range(3):
+                at = (3 * h + c) * half
+                qkvw[:, at : at + half] = qkv[c]
+            downt[:, h * half : (h + 1) * half] = down[...].T
+
+    total = dot_nn(qkvw[...], jnp.concatenate([dxo_ref[...], dxp_ref[...]], axis=0))
+    ffn = dot_nn(downt[...], act_ref[...])
+    for j in range(PAIR):
+        lanes = slice(j * slots, (j + 1) * slots)
+        output_ref[j] = (h1_ref[:, lanes] + ffn[:, lanes]).astype(BF16).T
     highs, lows = [], []
     for j in range(PAIR):
         lanes = slice(j * slots, (j + 1) * slots)
@@ -442,25 +553,33 @@
             small_ref[...] = packed.reshape(small_ref.shape)
 
 
-def gather_kernel(got1_ref, own_ref, a_ref, b_ref, c_ref, got_ref, red1_ref, red2_ref, small_ref, sq_ref):
-    red1 = got1_ref[0].astype(F32)
-    for o in range(1, got1_ref.shape[0]):
-        red1 = red1 + got1_ref[o].astype(F32)
-    red2 = own_ref[...].astype(F32) + a_ref[...].astype(F32)
-    red2 = red2 + b_ref[...].astype(F32) + c_ref[...].astype(F32)
+def square_sum(value, lanes):
+    both = value * value
+    folded = both[:, 0:lanes]
+    for c in range(1, both.shape[1] // lanes):
+        folded = folded + both[:, c * lanes : (c + 1) * lanes]
+    return jnp.sum(folded, axis=0, keepdims=True)
+
+
+def first_kernel(got_ref, red_ref, sq_ref):
+    red = got_ref[0].astype(F32)
+    for o in range(1, got_ref.shape[0]):
+        red = red + got_ref[o].astype(F32)
+    red_ref[...] = red
+    sq_ref[...] = square_sum(red, sq_ref.shape[1])
+
+
+def gather_kernel(own_ref, a_ref, b_ref, c_ref, got_ref, sq1_ref, red_ref, small_ref, sq_ref):
+    red = own_ref[...].astype(F32) + a_ref[...].astype(F32)
+    red = red + b_ref[...].astype(F32) + c_ref[...].astype(F32)
     small = got_ref[0]
     for o in range(1, got_ref.shape[0]):
         small = small + got_ref[o]
-    red1_ref[...] = red1
-    red2_ref[...] = red2
+    red_ref[...] = red
     small_ref[...] = small
-    both = red1 * red1 + red2 * red2
     lanes = sq_ref.shape[1]
-    folded = both[:, 0:lanes]
-    for c in range(1, both.shape[1] // lanes):
-        folded = folded + both[:, c * lanes : (c + 1) * lanes]
-    total = jnp.sum(folded) + jnp.sum(small * small)
-    sq_ref[...] = jnp.full(sq_ref.shape, total, F32)
+    rows = sq1_ref[...] + square_sum(red, lanes) + square_sum(small, lanes)
+    sq_ref[...] = jnp.full(sq_ref.shape, jnp.sum(rows), F32)
 
 
 def adam_kernel(*refs):
@@ -564,8 +683,9 @@
     gshape = (owners, 2 * half // owners, 3 * half)
     padded = jax.ShapeDtypeStruct((mols, heads * PAD_DIM, slots), BF16)
     outs = [
-        (jax.ShapeDtypeStruct((mols, slots, width), BF16), lead_spec(slots, width)),
         (jax.ShapeDtypeStruct((width, toks), F32), col),
+        (jax.ShapeDtypeStruct((width, toks), F32), col),
+        (jax.ShapeDtypeStruct((width, toks), BF16), whole_spec((width, toks))),
         (padded, lead_spec(heads * PAD_DIM, slots)),
         (padded, lead_spec(heads * PAD_DIM, slots)),
         (padded, lead_spec(heads * PAD_DIM, slots)),
@@ -589,14 +709,12 @@
         ]
         + [whole_spec(w.shape) for w in weights],
         scratch_shapes=[
-            pltpu.VMEM((2, 3 * half, width), BF16),
-            pltpu.VMEM((2, width, half), BF16),
-            pltpu.VMEM((2, half, width), BF16),
-            pltpu.VMEM((2, width, half), BF16),
-            pltpu.VMEM((2, width, slots), F32),
+            pltpu.VMEM((6 * half, width), BF16),
         ]
-        + [pltpu.VMEM((width, toks), BF16)] * 5
-        + [pltpu.VMEM((width, PAIR * slots), F32)] * 4
+        + [pltpu.VMEM((width, width), BF16)] * 5
+        + [pltpu.VMEM((2, width, slots), F32)]
+        + [pltpu.VMEM((width, toks), BF16)] * 4
+        + [pltpu.VMEM((PAIR, width, slots), F32), pltpu.VMEM((width, PAIR * slots), F32)]
         + [pltpu.VMEM((PAIR, heads // 4 + 1, 8, slots), F32)],
         compiler_params=pltpu.CompilerParams(vmem_limit_bytes=VMEM_BYTES),
         cost_estimate=costs(60_000_000_000, 50_000_000),
@@ -604,36 +722,49 @@
     )(lengths, h0, na, cot, norm_params, *weights)
 
 
-def middle(which, na, q, k, v, do, e):
+def middle(which, na, q, k, v, do, e, got=None, plane=None):
     mols, heads, slots, _ = e.shape
     width, toks = na.shape
     half = width // 2
     rows = heads // 2 * PAD_DIM
     part = pl.BlockSpec((PAIR, rows, slots), lambda i: (i, which, 0))
     gshape = (16, width // 16, 3 * half)
-    return pl.pallas_call(
-        middle_kernel,
+    dx = jax.ShapeDtypeStruct((3 * half, toks), BF16)
+    specs = [
+        whole_spec(na.shape),
+        part,
+        part,
+        part,
+        part,
+        pl.BlockSpec((PAIR, heads // 2, slots, slots), lambda i: (i, which, 0, 0)),
+    ]
+    common = dict(
         grid=(mols // PAIR,),
-        out_shape=[
-            jax.ShapeDtypeStruct((3 * half, toks), BF16),
-            jax.ShapeDtypeStruct(gshape, BF16),
-        ],
-        in_specs=[
-            whole_spec(na.shape),
-            part,
-            part,
-            part,
-            part,
-            pl.BlockSpec((PAIR, heads // 2, slots, slots), lambda i: (i, which, 0, 0)),
-        ],
-        out_specs=[whole_spec((3 * half, toks)), whole_spec(gshape)],
         compiler_params=pltpu.CompilerParams(vmem_limit_bytes=VMEM_BYTES),
         cost_estimate=costs(20_000_000_000, 12_000_000),
-        name="middle",
-    )(na, q, k, v, do, e)
-
-
-def back(dxo, dxp, qkv_o, qkv_p, h0, gh1, fs, gain, lnb, mols, packed):
+    )
+    if got is None:
+        return pl.pallas_call(
+            middle_kernel,
+            out_shape=[dx, jax.ShapeDtypeStruct(gshape, BF16)],
+            in_specs=specs,
+            out_specs=[whole_spec(dx.shape), whole_spec(gshape)],
+            name="middle_peer",
+            **common,
+        )(na, q, k, v, do, e)
+    piece = (4,) + gshape[1:]
+    return pl.pallas_call(
+        middle_own_kernel,
+        out_shape=[dx] + [jax.ShapeDtypeStruct(piece, BF16)] * 4,
+        in_specs=[pl.BlockSpec(memory_space=pltpu.SMEM)] + specs + [whole_spec(gshape)],
+        out_specs=[whole_spec(dx.shape)] + [whole_spec(piece)] * 4,
+        scratch_shapes=[pltpu.VMEM(gshape, BF16)],
+        name="middle_own",
+        **common,
+    )(plane, na, q, k, v, do, e, got)
+
+
+def back(dxo, dxp, qkv_o, qkv_p, h0, gh1, fs, gain, lnb, h1, act, down_o, down_p, mols, packed):
     width, toks = h0.shape
     slots = toks // mols
     col = column_spec(width, slots)
@@ -644,6 +775,7 @@
         grid=(mols // PAIR,),
         out_shape=[
             jax.ShapeDtypeStruct((mols, slots, width), F32),
+            jax.ShapeDtypeStruct((mols, slots, width), BF16),
             jax.ShapeDtypeStruct(small, F32),
         ],
         in_specs=[
@@ -656,33 +788,52 @@
             column_spec(fs.shape[0], slots),
             whole_spec(gain.shape),
             whole_spec(lnb.shape),
+            col,
+            col,
+            whole_spec(down_o.shape),
+            whole_spec(down_p.shape),
         ],
-        out_specs=[lead_spec(slots, width), whole_spec(small)],
+        out_specs=[lead_spec(slots, width), lead_spec(slots, width), whole_spec(small)],
         scratch_shapes=[
             pltpu.VMEM((width, slots), F32),
             pltpu.VMEM((2, width, slots), F32),
             pltpu.VMEM((width, fs.shape[0]), F32),
+            pltpu.VMEM((width, 3 * width), BF16),
+            pltpu.VMEM((width, width), BF16),
         ],
         compiler_params=pltpu.CompilerParams(vmem_limit_bytes=VMEM_BYTES),
         cost_estimate=costs(18_000_000_000, 15_000_000),
         name="back",
-    )(dxo, dxp, qkv_o, qkv_p, h0, gh1, fs, gain, lnb)
-
-
-def gather(got1, own2, others2, got):
-    rows, columns = got1.shape[1:]
+    )(dxo, dxp, qkv_o, qkv_p, h0, gh1, fs, gain, lnb, h1, act, down_o, down_p)
+
+
+def first_sum(got):
+    rows, columns = got.shape[1:]
+    return pl.pallas_call(
+        first_kernel,
+        out_shape=[
+            jax.ShapeDtypeStruct((rows, columns), F32),
+            jax.ShapeDtypeStruct((1, 128), F32),
+        ],
+        compiler_params=pltpu.CompilerParams(vmem_limit_bytes=VMEM_BYTES),
+        cost_estimate=costs(1_000_000, 2_000_000),
+        name="first_sum",
+    )(got)
+
+
+def gather(own2, others2, got, squares):
+    rows, columns = own2.shape
     lanes = got.shape[2]
     return pl.pallas_call(
         gather_kernel,
         out_shape=[
-            jax.ShapeDtypeStruct((rows, columns), F32),
             jax.ShapeDtypeStruct((rows, columns), F32),
             jax.ShapeDtypeStruct(got.shape[1:], F32),
             jax.ShapeDtypeStruct((got.shape[0], lanes), F32),
         ],
         compiler_params=pltpu.CompilerParams(vmem_limit_bytes=VMEM_BYTES),
         name="gather",
-    )(got1, own2, *others2, got)
+    )(own2, *others2, got, squares)
 
 
 def adam_all(squares, red1, red2, small, state):
@@ -770,40 +921,55 @@
         embed_weight,
         norm_params,
     )
-    (output, gh1, q, k, v, do, e, gown1, gpeer1, lnb) = front(
+    (gh1, h1, act, q, k, v, do, e, gown1, gpeer1, lnb) = front(
         lengths, h0, na, cot, norm_params, own, peer, mols
     )
-    sum1 = (gown1.astype(F32) + swap(gpeer1).astype(F32)).astype(BF16)
+    got1 = swap(gpeer1)
+    dxp, gpeer2 = middle(1, na, q, k, v, do, e)
+    got1, dxp = lax.optimization_barrier((got1, dxp))
+    sum1 = (gown1.astype(F32) + got1.astype(F32)).astype(BF16)
+    got2 = swap(gpeer2)
     sum1, do = lax.optimization_barrier((sum1, do))
     if fits:
         got1 = lax.all_to_all(sum1, "dp", 0, 0, tiled=True)
-    dxp, gpeer2 = middle(1, na, q, k, v, do, e)
-    got2 = swap(gpeer2)
-    dxo, gown2 = middle(0, na, q, k, v, do, e)
-    sum2 = (gown2.astype(F32) + got2.astype(F32)).astype(BF16)
     index = lax.axis_index("dp")
+    plane, line = (index & 3, index >> 2) if fits else (jnp.int32(0), None)
+    dxo, *pieces = middle(0, na, q, k, v, do, e, got2, plane.reshape(1))
     if fits:
-        plane, line = index & 3, index >> 2
-        grid = sum2.reshape((4, 4) + sum2.shape[1:]).swapaxes(0, 1)
-        own2 = take(grid, plane)
-        sends = [take(grid, plane ^ k) for k in (1, 2, 3)]
-        sends, dxo = lax.optimization_barrier((sends, dxo))
-        near = [hop(piece, k) for piece, k in zip(sends, (1, 2, 3))]
-    input_grad, small = back(dxo, dxp, own[0], peer[0], h0, gh1, fs, norm_params, lnb, mols, fits)
+        pieces, dxo = lax.optimization_barrier((pieces, dxo))
+        near = [hop(piece, k) for piece, k in zip(pieces[1:], (1, 2, 3))]
+    input_grad, output, small = back(
+        dxo,
+        dxp,
+        own[0],
+        peer[0],
+        h0,
+        gh1,
+        fs,
+        norm_params,
+        lnb,
+        h1,
+        act,
+        own[3],
+        peer[3],
+        mols,
+        fits,
+    )
 
     shard_index = index * mp_size + lax.axis_index("mp")
     norm_own = lax.dynamic_slice_in_dim(norm_params, shard_index * shard_width, shard_width, 1)
     embed_own = lax.dynamic_slice_in_dim(embed_weight, shard_index * shard_width, shard_width, 1)
     flip = lambda a: a.transpose(1, 0, 2)
     if fits:
-        plane_sum = own2.astype(F32)
+        small, got1 = lax.optimization_barrier((small, got1))
+        got = lax.all_to_all(small, ("dp", "mp"), 0, 0, tiled=True)
+        red1, squares1 = first_sum(got1)
+        plane_sum = pieces[0].astype(F32)
         for piece in near:
             plane_sum = plane_sum + piece.astype(F32)
         plane_sum = plane_sum.astype(BF16)
-        small, got1, plane_sum = lax.optimization_barrier((small, got1, plane_sum))
-        got = lax.all_to_all(small, ("dp", "mp"), 0, 0, tiled=True)
         far = [hop(take(plane_sum, line ^ k), 4 * k) for k in (1, 2, 3)]
-        red1, red2, small_own, squares = gather(got1, take(plane_sum, line), far, got)
+        red2, small_own, squares = gather(take(plane_sum, line), far, got, squares1)
         lanes = squares.shape[1]
         squares = lax.all_to_all(squares.reshape(world, 1, lanes), ("dp", "mp"), 0, 0, tiled=True)
         state = (
@@ -820,7 +986,8 @@
 
     some = half // 16
     scatter = partial(lax.psum_scatter, axis_name="dp", scatter_dimension=0, tiled=True)
-    sum1, sum2 = sum1.astype(F32), sum2.astype(F32)
+    sum1 = sum1.astype(F32)
+    sum2 = jnp.stack(pieces, axis=1).astype(F32)
     reduced_down = scatter(sum1[:, 0:some, 0:width].reshape(half, width))
     reduced_out = scatter(sum1[:, some:, 0:width].reshape(half, width))
     reduced_up = scatter(sum1[:, :, width:].reshape(width, half))

time: 194 us -> 162 us (0.84)
  Pallas kernels: 116 us -> 97 us
  other arithmetic: 7.72 us -> 1.89 us
  starting transfers between devices: 31.6 us -> 27.7 us
  local copies, waits for them, and re-layouts: 9.94 us -> 6.67 us
    pallas_call x1, Pallas kernels: 54.2 us -> 42.1 us  [front(): pl.pallas_call(front_kernel, grid=(mols // PAIR,), out_shape=[o[0] for o...]
    pallas_call x2 -> x3, Pallas kernels: 34.5 us -> 26.5 us  [the longest x1 12.4 us: middle(): pl.pallas_call(middle_own_kernel, out_shape=[dx] + [jax.ShapeDtypeStruct(...]
    ppermute x6, waiting for transfers between devices: 18 us -> 22 us  [hop(): return lax.ppermute(value, 'dp', [(i, i ^ flip) for i in range(size)])]
    convert_element_type x2 -> x1, other arithmetic: 5.58 us -> 1.67 us  [on_device(): sum1 = (gown1.astype(F32) + got1.astype(F32)).astype(BF16)]
    all_to_all x1, starting transfers between devices: 9.01 us -> 5.38 us  [on_device(): got = lax.all_to_all(small, ('dp', 'mp'), 0, 0, tiled=True)]
    ppermute x6, waiting for transfers between devices: 3.54 us -> 0.02 us  [swap(): return lax.ppermute(value, 'mp', [(0, 1), (1, 0)])]
    squeeze x2 -> x1, local copies, waits for them, and re-layouts: 2.89 us -> 0.7 us  [take(): return lax.dynamic_index_in_dim(value, index, axis, keepdims=False)]
    unnamed x23 -> x25, local copies, waits for them, and re-layouts: 4.85 us -> 3.76 us
  transfers between devices with their start and end apart: 15 -> 15, of which waited for: 6 -> 4; matrix products, arithmetic and copies ran while one was open for 5% -> 3% of each run, Pallas kernels for 20% -> 31%
where the time goes in v3:
time: 162 us; the launch traced here: 161 us
  Pallas kernels  97 us (60%)
  starting transfers between devices  27.7 us (17%)
  waiting for transfers between devices  27.1 us (17%)
  local copies, waits for them, and re-layouts  6.67 us (4%)
  other arithmetic  1.89 us (1%)
    pallas_call x1, Pallas kernels, front(): pl.pallas_call(front_kernel, grid=(mols // PAIR,), out_shape=[o[0] for o...  42.1 us
    ppermute x6, waiting for transfers between devices, hop(): return lax.ppermute(value, 'dp', [(i, i ^ flip) for i in range(size)])  22 us
    pallas_call x1, Pallas kernels, back(): pl.pallas_call(back_kernel, grid=(mols // PAIR,), out_shape=[jax.ShapeDty...  16.5 us
    pallas_call x1, Pallas kernels, middle(): pl.pallas_call(middle_own_kernel, out_shape=[dx] + [jax.ShapeDtypeStruct(...  12.4 us
    pallas_call x1, Pallas kernels, middle(): pl.pallas_call(middle_kernel, out_shape=[dx, jax.ShapeDtypeStruct(gshape,...  11.7 us
    all_to_all x1, starting transfers between devices, on_device(): got1 = lax.all_to_all(sum1, 'dp', 0, 0, tiled=True)  8.17 us
    ppermute x6, starting transfers between devices, hop(): return lax.ppermute(value, 'dp', [(i, i ^ flip) for i in range(size)])  7.68 us
    pallas_call x1, Pallas kernels, embed(): pl.pallas_call(embed_kernel, grid=(mols // PAIR,), out_shape=[jax.ShapeDt...  7.03 us
  transfers between devices with their start and end apart: 15, of which 4 were waited for; matrix products, arithmetic and copies ran while one was open for 3% of the time, Pallas kernels for 31%

profile of v3, /device:TPU:0, one launch (start us, length us, event | category | flops | bytes accessed | tf_op | source)
XLA Modules:
  0.0 161.3 jit_solution(6428526882040076625)
XLA Ops:
  1.8 7.0 %embed.1 = (f32[768,1024]{1,0:T(8,128)}, bf16[768,1024]{1,0:T(8,128)(2,1)}, bf16[256,1024]{1,0:T(8,128)(2,1)}, bf16[768,1024]{1,0:T(8,128)(2,1)}) custom-call(bf16[8,128,768]{2,1,0:T(8,128)(2,1)} %tok_ref.1, bf16[8,128,768]{2,1,0:T(8,128)(2,1)} %cot_ref.1, s32[8,1,128]{2,1,0:T(1,128)} %bitcast.50, s32[8,2,128]{2,1,0:T(2,128)} %bitcast.49, ...), custom_call_target="tpu_custom_call" | custom-call | flops 8000000000 | bytes 10000000 | tf_op jit(solution)/shard_map/embed/pallas_call | solution.py:648
  8.9 0.8 copy-done.9
  10.6 42.1 %front.1 = (f32[768,1024]{1,0:T(8,128)}, f32[768,1024]{1,0:T(8,128)}, bf16[768,1024]{1,0:T(8,128)(2,1)}, bf16[8,1024,128]{2,1,0:T(8,128)(2,1)}, bf16[8,1024,128]...) custom-call(s32[8]{0:T(128)} %len_ref.1, ...), custom_call_target="tpu_custom_call" | custom-call | flops 60000002048 | bytes 50000000 | tf_op jit(solution)/shard_map/front/pallas_call | solution.py:698
  53.2 11.7 %middle_peer.1 = (bf16[1152,1024]{1,0:T(8,128)(2,1)}, bf16[16,48,1152]{2,1,0:T(8,128)(2,1)}) custom-call(bf16[768,1024]{1,0:T(8,128)(2,1)} %get-tuple-element.81.na_ref, bf16[8,1024,128]{2,1,0:T(8,128)(2,1)} %get-tuple-element.84.q_ref, bf16[8,1024,128]{2,1,0:T(8,128)(2,1)} %get-tuple-element.85.k_ref, bf16[8,1024,128]{2,1,0:T(8,128)(2,1)} %get-tuple-element.86.v_ref, ...), custom_call_target="tpu_custom_call" | custom-call | flops 20000000000 | bytes 12000000 | tf_op jit(solution)/shard_map/middle_peer/pallas_call | solution.py:747
  65.1 1.7 %add_convert_fusion = bf16[16,48,1152]{2,1,0:T(8,128)(2,1)} fusion(bf16[16,48,1152]{2,1,0:T(8,128)(2,1)S(1)} %collective-permute-done.4, bf16[16,48,1152]{2,1,0:T(8,128)(2,1)S(1)} %copy-done.1), kind=kLoop, calls=%fused_computation | loop fusion | flops 3538944 | bytes 5308416 | tf_op jit(solution)/shard_map/convert_element_type | solution.py:930
  66.8 8.2 %all-to-all-start = ((bf16[16,48,1152]{2,1,0:T(8,128)(2,1)}), bf16[16,48,1152]{2,1,0:T(8,128)(2,1)S(1)}, u32[]{:S(2)}, u32[]{:S(2)}) async-start(bf16[16,48,1152]{2,1,0:T(8,128)(2,1)} %add_convert_fusion), calls=%async_computation | async-start | bytes 3538944 | tf_op jit(solution)/shard_map/all_to_all | solution.py:934
  75.0 12.4 %middle_own.1 = (bf16[1152,1024]{1,0:T(8,128)(2,1)}, bf16[4,48,1152]{2,1,0:T(8,128)(2,1)}, bf16[4,48,1152]{2,1,0:T(8,128)(2,1)}, bf16[4,48,1152]{2,1,0:T(8,128)(2,1)}, bf16[4,48,1152]{2,1,0:T(8,128)(2,1)}) custom-call(s32[1]{0:T(128)} %bitcast.plane_ref, bf16[768,1024]{1,0:T(8,128)(2,1)} %get-tuple-element.81.na_ref, ...), custom_call_target="tpu_custom_call" | custom-call | flops 20000000000 | bytes 12000000 | tf_op jit(solution)/shard_map/middle_own/pallas_call | solution.py:756
  87.4 1.9 %collective-permute-start.6 = (bf16[4,48,1152]{2,1,0:T(8,128)(2,1)}, bf16[4,48,1152]{2,1,0:T(8,128)(2,1)S(1)}, u32[]{:S(2)}, u32[]{:S(2)}) collective-permute-start(bf16[4,48,1152]{2,1,0:T(8,128)(2,1)} %get-tuple-element.110), channel_id=1, source_target_pairs={{0,2},{2,0},{4,6},{6,4},{8,10},{10,8},{12,14},{14,12},{16,18},{18,... | collective-permute-start | bytes 1327112 | tf_op jit(solution)/shard_map/ppermute | solution.py:855
  89.3 1.5 collective-permute-start.7
  90.9 16.5 %back.1 = (f32[8,128,768]{2,1,0:T(8,128)}, bf16[8,128,768]{2,1,0:T(8,128)(2,1)}, f32[32,8,128]{2,1,0:T(8,128)}) custom-call(bf16[1152,1024]{1,0:T(8,128)(2,1)} %get-tuple-element.100.dxo_ref, bf16[1152,1024]{1,0:T(8,128)(2,1)} %get-tuple-element.101.dxp_ref, bf16[3,768,384]{2,1,0:T(8,128)(2,1)} %bitcast.41, bf16[3,768,384]{2,1,0:T(8,128)(2,1)} %copy-done.8, ...), custom_call_target="tpu_custom_call" | custom-call | flops 17999998976 | bytes 15000000 | tf_op jit(solution)/shard_map/back/pallas_call | solution.py:773
  107.4 6.5 %collective-permute-done.6 = bf16[4,48,1152]{2,1,0:T(8,128)(2,1)S(1)} collective-permute-done((bf16[4,48,1152]{2,1,0:T(8,128)(2,1)}, bf16[4,48,1152]{2,1,0:T(8,128)(2,1)S(1)}, u32[]{:S(2)}, u32[]{:S(2)}) %collective-permute-start.6) | collective-permute-done | bytes 442400 | tf_op jit(solution)/shard_map/ppermute | solution.py:855
  113.8 9.5 %collective-permute-done.8 = bf16[4,48,1152]{2,1,0:T(8,128)(2,1)S(1)} collective-permute-done((bf16[4,48,1152]{2,1,0:T(8,128)(2,1)}, bf16[4,48,1152]{2,1,0:T(8,128)(2,1)S(1)}, u32[]{:S(2)}, u32[]{:S(2)}) %collective-permute-start.8) | collective-permute-done | bytes 442400 | tf_op jit(solution)/shard_map/ppermute | solution.py:855
  123.6 5.4 %all-to-all-start.1 = ((f32[32,8,128]{2,1,0:T(8,128)}), f32[32,8,128]{2,1,0:T(8,128)S(1)}, u32[]{:S(2)}, u32[]{:S(2)}) async-start(f32[32,8,128]{2,1,0:T(8,128)} %get-tuple-element.115), calls=%async_computation.1 | async-start | bytes 262144 | tf_op jit(solution)/shard_map/all_to_all | solution.py:965
  129.0 0.7 dynamic-slice_bitcast_fusion
  129.7 2.7 %collective-permute-start.10 = (bf16[48,1152]{1,0:T(8,128)(2,1)S(1)}, bf16[48,1152]{1,0:T(8,128)(2,1)S(1)}, u32[]{:S(2)}, u32[]{:S(2)}) collective-permute-start(bf16[48,1152]{1,0:T(8,128)(2,1)S(1)} %get-tuple-element.142), channel_id=1, source_target_pairs={{0,16},{2,18},{4,20},{6,22},{8,24},{10,26},{12,28},{14,30},{16,0},... | collective-permute-start | bytes 331784 | tf_op jit(solution)/shard_map/ppermute | solution.py:855
  132.3 1.5 collective-permute-start.11
  133.9 0.9 constant_dynamic-slice_fusion
  134.7 2.4 %first_sum.1 = (f32[48,1152]{1,0:T(8,128)}, f32[1,128]{1,0:T(1,128)}) custom-call(bf16[16,48,1152]{2,1,0:T(8,128)(2,1)} %copy-done), custom_call_target="tpu_custom_call" | custom-call | flops 1000000 | bytes 2000000 | tf_op jit(solution)/shard_map/first_sum/pallas_call | solution.py:812
  137.1 6.0 %collective-permute-done.10.b_ref = bf16[48,1152]{1,0:T(8,128)(2,1)S(1)} collective-permute-done((bf16[48,1152]{1,0:T(8,128)(2,1)S(1)}, bf16[48,1152]{1,0:T(8,128)(2,1)S(1)}, u32[]{:S(2)}, u32[]{:S(2)}) %collective-permute-start.10) | collective-permute-done | bytes 110624 | tf_op jit(solution)/shard_map/ppermute | solution.py:855
  143.9 1.9 %gather.1 = (f32[48,1152]{1,0:T(8,128)}, f32[8,128]{1,0:T(8,128)}, f32[32,128]{1,0:T(8,128)}) custom-call(bf16[48,1152]{1,0:T(8,128)(2,1)} %get-tuple-element.144.own_ref, bf16[48,1152]{1,0:T(8,128)(2,1)} %copy-done.6, bf16[48,1152]{1,0:T(8,128)(2,1)} %copy-done.4, bf16[48,1152]{1,0:T(8,128)(2,1)} %copy-done.5, f32[32,8,128]{2,1,0:T(8,128)} %copy-done.2, ...), custom_call_target="tpu_custom_call" | custom-call | tf_op jit(solution)/shard_map/gather/pallas_call | solution.py:827
  145.9 4.6 %all-to-all-start.2 = ((f32[32,1,128]{2,1,0:T(1,128)}), f32[32,1,128]{2,1,0:T(1,128)S(1)}, u32[]{:S(2)}, u32[]{:S(2)}) async-start(f32[32,1,128]{2,1,0:T(1,128)} %bitcast.36), calls=%async_computation.2 | async-start | bytes 32768 | tf_op jit(solution)/shard_map/all_to_all | solution.py:974
  150.5 1.4 constant_dynamic-slice_fusion.1.refs_16_
  152.5 5.0 %all-to-all-done.2 = f32[32,1,128]{2,1,0:T(1,128)S(1)} async-done(((f32[32,1,128]{2,1,0:T(1,128)}), f32[32,1,128]{2,1,0:T(1,128)S(1)}, u32[]{:S(2)}, u32[]{:S(2)}) %all-to-all-start.2) | async-done | bytes 16416 | tf_op jit(solution)/shard_map/all_to_all | solution.py:974
  158.2 2.9 %adam.1 = (f32[1,128]{1,0:T(1,128)}, f32[3,48,384]{2,1,0:T(8,128)}, f32[3,48,384]{2,1,0:T(8,128)}, f32[3,48,384]{2,1,0:T(8,128)}, f32[24,768]{1,0:T(8,128)}, /*i...) custom-call(f32[32,128]{1,0:T(8,128)} %bitcast.34, ...), custom_call_target="tpu_custom_call" | custom-call | tf_op jit(solution)/shard_map/adam/pallas_call | solution.py:840
  (44 shorter events, 5.2 us)
Async XLA Ops:
  0.7 8.2 %collective-permute-start = (bf16[3,768,384]{2,1,0:T(8,128)(2,1)}, bf16[3,768,384]{2,1,0:T(8,128)(2,1)S(1)}, u32[]{:S(2)}, u32[]{:S(2)}) collective-permute-start(bf16[3,768,384]{2,1,0:T(8,128)(2,1)} %bitcast.39), channel_id=1, source_target_pairs={{0,1},{1,0},{2,3},{3,2},{4,5},{5,4},{6,7},{7,6},{8,9},{9,8},{10,11... | collective-permute-start | bytes 5308424 | tf_op jit(solution)/shard_map/ppermute | solution.py:850
  1.2 7.6 %collective-permute-start.3 = (bf16[384,768]{1,0:T(8,128)(2,1)}, bf16[384,768]{1,0:T(8,128)(2,1)S(1)}, u32[]{:S(2)}, u32[]{:S(2)}) collective-permute-start(bf16[384,768]{1,0:T(8,128)(2,1)} %down_o.3), channel_id=1, source_target_pairs={{0,1},{1,0},{2,3},{3,2},{4,5},{5,4},{6,7},{7,6},{8,9},{9,8},{10,11... | collective-permute-start | bytes 1769480 | tf_op jit(solution)/shard_map/ppermute | solution.py:850
  1.3 7.6 %collective-permute-start.1 = (bf16[384,768]{1,0:T(8,128)(2,1)}, bf16[384,768]{1,0:T(8,128)(2,1)S(1)}, u32[]{:S(2)}, u32[]{:S(2)}) collective-permute-start(bf16[384,768]{1,0:T(8,128)(2,1)} %out_o.1), channel_id=1, source_target_pairs={{0,1},{1,0},{2,3},{3,2},{4,5},{5,4},{6,7},{7,6},{8,9},{9,8},{10,11... | collective-permute-start | bytes 1769480 | tf_op jit(solution)/shard_map/ppermute | solution.py:850
  1.7 7.2 %collective-permute-start.2 = (bf16[768,384]{1,0:T(8,128)(2,1)}, bf16[768,384]{1,0:T(8,128)(2,1)S(1)}, u32[]{:S(2)}, u32[]{:S(2)}) collective-permute-start(bf16[768,384]{1,0:T(8,128)(2,1)} %up_o.1), channel_id=1, source_target_pairs={{0,1},{1,0},{2,3},{3,2},{4,5},{5,4},{6,7},{7,6},{8,9},{9,8},{10,11... | collective-permute-start | bytes 1769480 | tf_op jit(solution)/shard_map/ppermute | solution.py:850
  8.8 0.8 copy-start.9
  8.8 1.0 copy-start.10
  8.8 1.2 copy-start.11
  8.9 1.8 %copy-start.8 = (bf16[3,768,384]{2,1,0:T(8,128)(2,1)}, bf16[3,768,384]{2,1,0:T(8,128)(2,1)S(1)}, u32[]{:S(2)}) copy-start(bf16[3,768,384]{2,1,0:T(8,128)(2,1)S(1)} %collective-permute-done.qkv_p) | copy-start | bytes 5308420
  52.7 12.4 %collective-permute-start.4 = (bf16[16,48,1152]{2,1,0:T(8,128)(2,1)}, bf16[16,48,1152]{2,1,0:T(8,128)(2,1)S(1)}, u32[]{:S(2)}, u32[]{:S(2)}) collective-permute-start(bf16[16,48,1152]{2,1,0:T(8,128)(2,1)} %get-tuple-element.88), channel_id=1, source_target_pairs={{0,1},{1,0},{2,3},{3,2},{4,5},{5,4},{6,7},{7,6},{8,9},{9,8},{10,11... | collective-permute-start | bytes 5308424 | tf_op jit(solution)/shard_map/ppermute | solution.py:850
  53.2 11.9 %copy-start.1 = (bf16[16,48,1152]{2,1,0:T(8,128)(2,1)S(1)}, bf16[16,48,1152]{2,1,0:T(8,128)(2,1)}, u32[]{:S(2)}) copy-start(bf16[16,48,1152]{2,1,0:T(8,128)(2,1)} %get-tuple-element.87) | copy-start | bytes 5308420
  64.9 10.1 %collective-permute-start.5 = (bf16[16,48,1152]{2,1,0:T(8,128)(2,1)}, bf16[16,48,1152]{2,1,0:T(8,128)(2,1)}, u32[]{:S(2)}, u32[]{:S(2)}) collective-permute-start(bf16[16,48,1152]{2,1,0:T(8,128)(2,1)} %get-tuple-element.94), channel_id=1, source_target_pairs={{0,1},{1,0},{2,3},{3,2},{4,5},{5,4},{6,7},{7,6},{8,9},{9,8},{10,11... | collective-permute-start | bytes 5308424 | tf_op jit(solution)/shard_map/ppermute | solution.py:850
  66.8 56.7 %all-to-all-start = ((bf16[16,48,1152]{2,1,0:T(8,128)(2,1)}), bf16[16,48,1152]{2,1,0:T(8,128)(2,1)S(1)}, u32[]{:S(2)}, u32[]{:S(2)}) async-start(bf16[16,48,1152]{2,1,0:T(8,128)(2,1)} %add_convert_fusion), calls=%async_computation | async-start | bytes 3538944 | tf_op jit(solution)/shard_map/all_to_all | solution.py:934
  87.4 26.4 %collective-permute-start.6 = (bf16[4,48,1152]{2,1,0:T(8,128)(2,1)}, bf16[4,48,1152]{2,1,0:T(8,128)(2,1)S(1)}, u32[]{:S(2)}, u32[]{:S(2)}) collective-permute-start(bf16[4,48,1152]{2,1,0:T(8,128)(2,1)} %get-tuple-element.110), channel_id=1, source_target_pairs={{0,2},{2,0},{4,6},{6,4},{8,10},{10,8},{12,14},{14,12},{16,18},{18,... | collective-permute-start | bytes 1327112 | tf_op jit(solution)/shard_map/ppermute | solution.py:855
  89.3 24.5 %collective-permute-start.7 = (bf16[4,48,1152]{2,1,0:T(8,128)(2,1)}, bf16[4,48,1152]{2,1,0:T(8,128)(2,1)S(1)}, u32[]{:S(2)}, u32[]{:S(2)}) collective-permute-start(bf16[4,48,1152]{2,1,0:T(8,128)(2,1)} %get-tuple-element.111), channel_id=1, source_target_pairs={{0,4},{2,6},{4,0},{6,2},{8,12},{10,14},{12,8},{14,10},{16,20},{18,... | collective-permute-start | bytes 1327112 | tf_op jit(solution)/shard_map/ppermute | solution.py:855
  90.8 32.6 %collective-permute-start.8 = (bf16[4,48,1152]{2,1,0:T(8,128)(2,1)}, bf16[4,48,1152]{2,1,0:T(8,128)(2,1)S(1)}, u32[]{:S(2)}, u32[]{:S(2)}) collective-permute-start(bf16[4,48,1152]{2,1,0:T(8,128)(2,1)} %get-tuple-element.112), channel_id=1, source_target_pairs={{0,6},{2,4},{4,2},{6,0},{8,14},{10,12},{12,10},{14,8},{16,22},{18,... | collective-permute-start | bytes 1327112 | tf_op jit(solution)/shard_map/ppermute | solution.py:855
  90.9 32.5 %copy-start.3 = (bf16[4,48,1152]{2,1,0:T(8,128)(2,1)S(1)}, bf16[4,48,1152]{2,1,0:T(8,128)(2,1)}, u32[]{:S(2)}) copy-start(bf16[4,48,1152]{2,1,0:T(8,128)(2,1)} %get-tuple-element.109) | copy-start | bytes 1327108
  123.6 11.1 %copy-start = (bf16[16,48,1152]{2,1,0:T(8,128)(2,1)}, bf16[16,48,1152]{2,1,0:T(8,128)(2,1)S(1)}, u32[]{:S(2)}) copy-start(bf16[16,48,1152]{2,1,0:T(8,128)(2,1)S(1)} %all-to-all-done.got_ref) | copy-start | bytes 5308420
  123.6 19.6 %all-to-all-start.1 = ((f32[32,8,128]{2,1,0:T(8,128)}), f32[32,8,128]{2,1,0:T(8,128)S(1)}, u32[]{:S(2)}, u32[]{:S(2)}) async-start(f32[32,8,128]{2,1,0:T(8,128)} %get-tuple-element.115), calls=%async_computation.1 | async-start | bytes 262144 | tf_op jit(solution)/shard_map/all_to_all | solution.py:965
  129.7 13.5 %collective-permute-start.10 = (bf16[48,1152]{1,0:T(8,128)(2,1)S(1)}, bf16[48,1152]{1,0:T(8,128)(2,1)S(1)}, u32[]{:S(2)}, u32[]{:S(2)}) collective-permute-start(bf16[48,1152]{1,0:T(8,128)(2,1)S(1)} %get-tuple-element.142), channel_id=1, source_target_pairs={{0,16},{2,18},{4,20},{6,22},{8,24},{10,26},{12,28},{14,30},{16,0},... | collective-permute-start | bytes 331784 | tf_op jit(solution)/shard_map/ppermute | solution.py:855
  132.3 10.8 %collective-permute-start.11 = (bf16[48,1152]{1,0:T(8,128)(2,1)S(1)}, bf16[48,1152]{1,0:T(8,128)(2,1)S(1)}, u32[]{:S(2)}, u32[]{:S(2)}) collective-permute-start(bf16[48,1152]{1,0:T(8,128)(2,1)S(1)} %get-tuple-element.141), channel_id=1, source_target_pairs={{0,24},{2,26},{4,28},{6,30},{8,16},{10,18},{12,20},{14,22},{16,8},... | collective-permute-start | bytes 331784 | tf_op jit(solution)/shard_map/ppermute | solution.py:855
  133.8 9.4 %collective-permute-start.9 = (bf16[48,1152]{1,0:T(8,128)(2,1)S(1)}, bf16[48,1152]{1,0:T(8,128)(2,1)S(1)}, u32[]{:S(2)}, u32[]{:S(2)}) collective-permute-start(bf16[48,1152]{1,0:T(8,128)(2,1)S(1)} %get-tuple-element.143), channel_id=1, source_target_pairs={{0,8},{2,10},{4,12},{6,14},{8,0},{10,2},{12,4},{14,6},{16,24},{18,... | collective-permute-start | bytes 331784 | tf_op jit(solution)/shard_map/ppermute | solution.py:855
  143.2 0.7 copy-start.6
  143.2 0.7 copy-start.2
  145.9 11.7 %all-to-all-start.2 = ((f32[32,1,128]{2,1,0:T(1,128)}), f32[32,1,128]{2,1,0:T(1,128)S(1)}, u32[]{:S(2)}, u32[]{:S(2)}) async-start(f32[32,1,128]{2,1,0:T(1,128)} %bitcast.36), calls=%async_computation.2 | async-start | bytes 32768 | tf_op jit(solution)/shard_map/all_to_all | solution.py:974
  (3 other events, 1.9 us)

commit v4 on v3

--- a/solution.py
+++ b/solution.py
@@ -468,6 +468,22 @@
     lax.fori_loop(0, PAIR * groups // MIDDLE_UNROLL, attend, 0)
 
 
+def output_kernel(h1_ref, act_ref, down_o, down_p, output_ref, downt):
+    slots = output_ref.shape[1]
+    half = down_o.shape[0]
+
+    @pl.when(pl.program_id(0) == 0)
+    def _():
+        for h, down in enumerate((down_o, down_p)):
+            downt[:, h * half : (h + 1) * half] = down[...].T
+
+    ffn = [dot_nn(downt[h * half : (h + 1) * half, :], act_ref[...]) for h in range(2)]
+    ffn = jnp.concatenate(ffn, axis=0)
+    for j in range(PAIR):
+        lanes = slice(j * slots, (j + 1) * slots)
+        output_ref[j] = (h1_ref[:, lanes] + ffn[:, lanes]).astype(BF16).T
+
+
 def back_kernel(
     dxo_ref,
     dxp_ref,
@@ -478,18 +494,12 @@
     fs_ref,
     gain_ref,
     lnb_ref,
-    h1_ref,
-    act_ref,
-    down_o,
-    down_p,
     ig_ref,
-    output_ref,
     small_ref,
     nb,
     lnacc,
     ge,
     qkvw,
-    downt,
 ):
     step = pl.program_id(0)
     slots = ig_ref.shape[1]
@@ -502,23 +512,22 @@
         lnacc[...] = jnp.zeros_like(lnacc)
         ge[...] = jnp.zeros_like(ge)
         nb[...] = lane_columns(gain_ref[0:1, :], slots)
-        for h, (qkv, down) in enumerate(((qkv_o, down_o), (qkv_p, down_p))):
+        for h, qkv in enumerate((qkv_o, qkv_p)):
             for c in range(3):
                 at = (3 * h + c) * half
                 qkvw[:, at : at + half] = qkv[c]
-            downt[:, h * half : (h + 1) * half] = down[...].T
-
-    total = dot_nn(qkvw[...], jnp.concatenate([dxo_ref[...], dxp_ref[...]], axis=0))
-    ffn = dot_nn(downt[...], act_ref[...])
+
+    units = []
     for j in range(PAIR):
-        lanes = slice(j * slots, (j + 1) * slots)
-        output_ref[j] = (h1_ref[:, lanes] + ffn[:, lanes]).astype(BF16).T
+        centred, rec = norm_parts(h0_ref[:, j * slots : (j + 1) * slots])
+        units.append((centred * rec, rec))
+    dxs = jnp.concatenate([dxo_ref[...], dxp_ref[...]], axis=0)
+    total = jnp.concatenate([dot_nn(qkvw[0:half, :], dxs), dot_nn(qkvw[half:, :], dxs)], axis=0)
     highs, lows = [], []
     for j in range(PAIR):
         lanes = slice(j * slots, (j + 1) * slots)
         ga = total[:, lanes]
-        centred, rec = norm_parts(h0_ref[:, lanes])
-        unit = centred * rec
+        unit, rec = units[j]
         lnacc[0] += ga * unit
         lnacc[1] += ga
         f = ga * nb[...]
@@ -561,24 +570,23 @@
     return jnp.sum(folded, axis=0, keepdims=True)
 
 
-def first_kernel(got_ref, red_ref, sq_ref):
-    red = got_ref[0].astype(F32)
-    for o in range(1, got_ref.shape[0]):
-        red = red + got_ref[o].astype(F32)
-    red_ref[...] = red
-    sq_ref[...] = square_sum(red, sq_ref.shape[1])
-
-
-def gather_kernel(own_ref, a_ref, b_ref, c_ref, got_ref, sq1_ref, red_ref, small_ref, sq_ref):
-    red = own_ref[...].astype(F32) + a_ref[...].astype(F32)
-    red = red + b_ref[...].astype(F32) + c_ref[...].astype(F32)
+def gather_kernel(*refs):
+    firsts, seconds, got_ref = refs[0:4], refs[4:8], refs[8]
+    red1_ref, red2_ref, small_ref, sq_ref = refs[9:]
+    lanes = sq_ref.shape[1]
+    rows = None
+    for refs4, red_ref in ((firsts, red1_ref), (seconds, red2_ref)):
+        red = refs4[0][...].astype(F32)
+        for ref in refs4[1:]:
+            red = red + ref[...].astype(F32)
+        red_ref[...] = red
+        part = square_sum(red, lanes)
+        rows = part if rows is None else rows + part
     small = got_ref[0]
     for o in range(1, got_ref.shape[0]):
         small = small + got_ref[o]
-    red_ref[...] = red
     small_ref[...] = small
-    lanes = sq_ref.shape[1]
-    rows = sq1_ref[...] + square_sum(red, lanes) + square_sum(small, lanes)
+    rows = rows + square_sum(small, lanes)
     sq_ref[...] = jnp.full(sq_ref.shape, jnp.sum(rows), F32)
 
 
@@ -741,7 +749,7 @@
     common = dict(
         grid=(mols // PAIR,),
         compiler_params=pltpu.CompilerParams(vmem_limit_bytes=VMEM_BYTES),
-        cost_estimate=costs(20_000_000_000, 12_000_000),
+        cost_estimate=costs(200_000_000, 120_000),
     )
     if got is None:
         return pl.pallas_call(
@@ -764,7 +772,24 @@
     )(plane, na, q, k, v, do, e, got)
 
 
-def back(dxo, dxp, qkv_o, qkv_p, h0, gh1, fs, gain, lnb, h1, act, down_o, down_p, mols, packed):
+def finish_output(h1, act, down_o, down_p, mols):
+    width, toks = h1.shape
+    slots = toks // mols
+    col = column_spec(width, slots)
+    return pl.pallas_call(
+        output_kernel,
+        grid=(mols // PAIR,),
+        out_shape=jax.ShapeDtypeStruct((mols, slots, width), BF16),
+        in_specs=[col, col, whole_spec(down_o.shape), whole_spec(down_p.shape)],
+        out_specs=lead_spec(slots, width),
+        scratch_shapes=[pltpu.VMEM((width, width), BF16)],
+        compiler_params=pltpu.CompilerParams(vmem_limit_bytes=VMEM_BYTES),
+        cost_estimate=costs(60_000_000, 70_000),
+        name="finish_output",
+    )(h1, act, down_o, down_p)
+
+
+def back(dxo, dxp, qkv_o, qkv_p, h0, gh1, fs, gain, lnb, mols, packed):
     width, toks = h0.shape
     slots = toks // mols
     col = column_spec(width, slots)
@@ -775,7 +800,6 @@
         grid=(mols // PAIR,),
         out_shape=[
             jax.ShapeDtypeStruct((mols, slots, width), F32),
-            jax.ShapeDtypeStruct((mols, slots, width), BF16),
             jax.ShapeDtypeStruct(small, F32),
         ],
         in_specs=[
@@ -788,52 +812,34 @@
             column_spec(fs.shape[0], slots),
             whole_spec(gain.shape),
             whole_spec(lnb.shape),
-            col,
-            col,
-            whole_spec(down_o.shape),
-            whole_spec(down_p.shape),
         ],
-        out_specs=[lead_spec(slots, width), lead_spec(slots, width), whole_spec(small)],
+        out_specs=[lead_spec(slots, width), whole_spec(small)],
         scratch_shapes=[
             pltpu.VMEM((width, slots), F32),
             pltpu.VMEM((2, width, slots), F32),
             pltpu.VMEM((width, fs.shape[0]), F32),
             pltpu.VMEM((width, 3 * width), BF16),
-            pltpu.VMEM((width, width), BF16),
         ],
         compiler_params=pltpu.CompilerParams(vmem_limit_bytes=VMEM_BYTES),
         cost_estimate=costs(18_000_000_000, 15_000_000),
         name="back",
-    )(dxo, dxp, qkv_o, qkv_p, h0, gh1, fs, gain, lnb, h1, act, down_o, down_p)
-
-
-def first_sum(got):
-    rows, columns = got.shape[1:]
-    return pl.pallas_call(
-        first_kernel,
-        out_shape=[
-            jax.ShapeDtypeStruct((rows, columns), F32),
-            jax.ShapeDtypeStruct((1, 128), F32),
-        ],
-        compiler_params=pltpu.CompilerParams(vmem_limit_bytes=VMEM_BYTES),
-        cost_estimate=costs(1_000_000, 2_000_000),
-        name="first_sum",
-    )(got)
-
-
-def gather(own2, others2, got, squares):
-    rows, columns = own2.shape
+    )(dxo, dxp, qkv_o, qkv_p, h0, gh1, fs, gain, lnb)
+
+
+def gather(firsts, seconds, got):
+    rows, columns = firsts[0].shape
     lanes = got.shape[2]
     return pl.pallas_call(
         gather_kernel,
         out_shape=[
+            jax.ShapeDtypeStruct((rows, columns), F32),
             jax.ShapeDtypeStruct((rows, columns), F32),
             jax.ShapeDtypeStruct(got.shape[1:], F32),
             jax.ShapeDtypeStruct((got.shape[0], lanes), F32),
         ],
         compiler_params=pltpu.CompilerParams(vmem_limit_bytes=VMEM_BYTES),
         name="gather",
-    )(own2, *others2, got, squares)
+    )(*firsts, *seconds, got)
 
 
 def adam_all(squares, red1, red2, small, state):
@@ -857,6 +863,14 @@
 
 def take(value, index, axis=0):
     return lax.dynamic_index_in_dim(value, index, axis, keepdims=False)
+
+
+def line_pieces(own, near, line):
+    total = own.astype(F32)
+    for piece in near:
+        total = total + piece.astype(F32)
+    total = total.astype(BF16)
+    return take(total, line), [take(total, line ^ k) for k in (1, 2, 3)]
 
 
 def adam_step(master, mean_old, square_old, gradient, rate, decay, clip_scale):
@@ -924,21 +938,29 @@
     (gh1, h1, act, q, k, v, do, e, gown1, gpeer1, lnb) = front(
         lengths, h0, na, cot, norm_params, own, peer, mols
     )
+    index = lax.axis_index("dp")
+    plane, line = (index & 3, index >> 2) if fits else (jnp.int32(0), None)
     got1 = swap(gpeer1)
     dxp, gpeer2 = middle(1, na, q, k, v, do, e)
     got1, dxp = lax.optimization_barrier((got1, dxp))
     sum1 = (gown1.astype(F32) + got1.astype(F32)).astype(BF16)
     got2 = swap(gpeer2)
-    sum1, do = lax.optimization_barrier((sum1, do))
     if fits:
-        got1 = lax.all_to_all(sum1, "dp", 0, 0, tiled=True)
-    index = lax.axis_index("dp")
-    plane, line = (index & 3, index >> 2) if fits else (jnp.int32(0), None)
+        grid = sum1.reshape((4, 4) + sum1.shape[1:]).swapaxes(0, 1)
+        pieces1 = [take(grid, plane ^ k) for k in range(4)]
+        pieces1, do = lax.optimization_barrier((pieces1, do))
+        near1 = [hop(piece, k) for piece, k in zip(pieces1[1:], (1, 2, 3))]
     dxo, *pieces = middle(0, na, q, k, v, do, e, got2, plane.reshape(1))
     if fits:
-        pieces, dxo = lax.optimization_barrier((pieces, dxo))
+        h1, pieces = lax.optimization_barrier((h1, pieces))
         near = [hop(piece, k) for piece, k in zip(pieces[1:], (1, 2, 3))]
-    input_grad, output, small = back(
+    output = finish_output(h1, act, own[3], peer[3], mols)
+    if fits:
+        near1, output = lax.optimization_barrier((near1, output))
+        own1, sends1 = line_pieces(pieces1[0], near1, line)
+        sends1, dxo = lax.optimization_barrier((sends1, dxo))
+        far1 = [hop(piece, 4 * k) for piece, k in zip(sends1, (1, 2, 3))]
+    input_grad, small = back(
         dxo,
         dxp,
         own[0],
@@ -948,10 +970,6 @@
         fs,
         norm_params,
         lnb,
-        h1,
-        act,
-        own[3],
-        peer[3],
         mols,
         fits,
     )
@@ -961,15 +979,11 @@
     embed_own = lax.dynamic_slice_in_dim(embed_weight, shard_index * shard_width, shard_width, 1)
     flip = lambda a: a.transpose(1, 0, 2)
     if fits:
-        small, got1 = lax.optimization_barrier((small, got1))
+        small, far1[1:] = lax.optimization_barrier((small, far1[1:]))
         got = lax.all_to_all(small, ("dp", "mp"), 0, 0, tiled=True)
-        red1, squares1 = first_sum(got1)
-        plane_sum = pieces[0].astype(F32)
-        for piece in near:
-            plane_sum = plane_sum + piece.astype(F32)
-        plane_sum = plane_sum.astype(BF16)
-        far = [hop(take(plane_sum, line ^ k), 4 * k) for k in (1, 2, 3)]
-        red2, small_own, squares = gather(take(plane_sum, line), far, got, squares1)
+        own2, sends2 = line_pieces(pieces[0], near, line)
+        far2 = [hop(piece, 4 * k) for piece, k in zip(sends2, (1, 2, 3))]
+        red1, red2, small_own, squares = gather([own1, *far1], [own2, *far2], got)
         lanes = squares.shape[1]
         squares = lax.all_to_all(squares.reshape(world, 1, lanes), ("dp", "mp"), 0, 0, tiled=True)
         state = (

time: 162 us -> 153 us (0.944)
  waiting for transfers between devices: 27.1 us -> 12.9 us
  local copies, waits for them, and re-layouts: 6.67 us -> 8.72 us
  other arithmetic: 1.89 us -> 3.65 us
    ppermute x6 -> x12, waiting for transfers between devices: 22 us -> 7.84 us  [hop(): return lax.ppermute(value, 'dp', [(i, i ^ flip) for i in range(size)])]
    ppermute x6 -> x12, starting transfers between devices: 7.68 us -> 17.5 us  [hop(): return lax.ppermute(value, 'dp', [(i, i ^ flip) for i in range(size)])]
    all_to_all x1 -> x0, starting transfers between devices: 8.17 us -> none  [on_device(): got1 = lax.all_to_all(sum1, 'dp', 0, 0, tiled=True)]
    pallas_call x1, Pallas kernels: 16.5 us -> 12.8 us  [back(): pl.pallas_call(back_kernel, grid=(mols // PAIR,), out_shape=[jax.ShapeDty...]
    pallas_call x1, Pallas kernels: 2.41 us -> 5.91 us  [finish_output(): pl.pallas_call(output_kernel, grid=(mols // PAIR,), out_shape=jax.ShapeDt...]
    unnamed x25 -> x31, local copies, waits for them, and re-layouts: 3.76 us -> 4.97 us
  transfers between devices with their start and end apart: 15 -> 20, of which waited for: 4 -> 5; matrix products, arithmetic and copies ran while one was open for 3% -> 5% of each run, Pallas kernels for 31% -> 33%
where the time goes in v4:
time: 153 us; the launch traced here: 152 us
  Pallas kernels  96.9 us (63%)
  starting transfers between devices  28.7 us (19%)
  waiting for transfers between devices  12.9 us (8%)
  local copies, waits for them, and re-layouts  8.72 us (6%)
  other arithmetic  3.65 us (2%)
    pallas_call x1, Pallas kernels, front(): pl.pallas_call(front_kernel, grid=(mols // PAIR,), out_shape=[o[0] for o...  42 us
    ppermute x12, starting transfers between devices, hop(): return lax.ppermute(value, 'dp', [(i, i ^ flip) for i in range(size)])  17.5 us
    pallas_call x1, Pallas kernels, back(): pl.pallas_call(back_kernel, grid=(mols // PAIR,), out_shape=[jax.ShapeDty...  12.8 us
    pallas_call x1, Pallas kernels, middle(): pl.pallas_call(middle_own_kernel, out_shape=[dx] + [jax.ShapeDtypeStruct(...  12.3 us
    pallas_call x1, Pallas kernels, middle(): pl.pallas_call(middle_kernel, out_shape=[dx, jax.ShapeDtypeStruct(gshape,...  11.7 us
    ppermute x12, waiting for transfers between devices, hop(): return lax.ppermute(value, 'dp', [(i, i ^ flip) for i in range(size)])  7.84 us
    pallas_call x1, Pallas kernels, embed(): pl.pallas_call(embed_kernel, grid=(mols // PAIR,), out_shape=[jax.ShapeDt...  7.01 us
    pallas_call x1, Pallas kernels, finish_output(): pl.pallas_call(output_kernel, grid=(mols // PAIR,), out_shape=jax.ShapeDt...  5.91 us
  transfers between devices with their start and end apart: 20, of which 5 were waited for; matrix products, arithmetic and copies ran while one was open for 5% of the time, Pallas kernels for 33%

profile of v4, /device:TPU:0, one launch (start us, length us, event | category | flops | bytes accessed | tf_op | source)
XLA Modules:
  0.0 151.9 jit_solution(9614420672726456290)
XLA Ops:
  1.8 7.0 %embed.1 = (f32[768,1024]{1,0:T(8,128)}, bf16[768,1024]{1,0:T(8,128)(2,1)}, bf16[256,1024]{1,0:T(8,128)(2,1)}, bf16[768,1024]{1,0:T(8,128)(2,1)}) custom-call(bf16[8,128,768]{2,1,0:T(8,128)(2,1)} %tok_ref.1, bf16[8,128,768]{2,1,0:T(8,128)(2,1)} %cot_ref.1, s32[8,1,128]{2,1,0:T(1,128)} %bitcast.68, s32[8,2,128]{2,1,0:T(2,128)} %bitcast.67, ...), custom_call_target="tpu_custom_call" | custom-call | flops 8000000000 | bytes 10000000 | tf_op jit(solution)/shard_map/embed/pallas_call | solution.py:656
  10.6 42.0 %front.1 = (f32[768,1024]{1,0:T(8,128)}, f32[768,1024]{1,0:T(8,128)}, bf16[768,1024]{1,0:T(8,128)(2,1)}, bf16[8,1024,128]{2,1,0:T(8,128)(2,1)}, bf16[8,1024,128]...) custom-call(s32[8]{0:T(128)} %len_ref.1, ...), custom_call_target="tpu_custom_call" | custom-call | flops 60000002048 | bytes 50000000 | tf_op jit(solution)/shard_map/front/pallas_call | solution.py:706
  53.1 11.7 %middle_peer.1 = (bf16[1152,1024]{1,0:T(8,128)(2,1)}, bf16[16,48,1152]{2,1,0:T(8,128)(2,1)}) custom-call(bf16[768,1024]{1,0:T(8,128)(2,1)} %get-tuple-element.92.na_ref, bf16[8,1024,128]{2,1,0:T(8,128)(2,1)} %get-tuple-element.96.q_ref, bf16[8,1024,128]{2,1,0:T(8,128)(2,1)} %get-tuple-element.97.k_ref, bf16[8,1024,128]{2,1,0:T(8,128)(2,1)} %get-tuple-element.98.v_ref, ...), custom_call_target="tpu_custom_call" | custom-call | flops 200000000 | bytes 120000 | tf_op jit(solution)/shard_map/middle_peer/pallas_call | solution.py:755
  65.1 1.9 %add_convert_fusion = bf16[16,48,1152]{2,1,0:T(8,128)(2,1)S(1)} fusion(bf16[16,48,1152]{2,1,0:T(8,128)(2,1)} %collective-permute-done.4, bf16[16,48,1152]{2,1,0:T(8,128)(2,1)S(1)} %copy-done.1), kind=kLoop, calls=%fused_computation | loop fusion | flops 3538944 | bytes 5308416 | tf_op jit(solution)/shard_map/convert_element_type | solution.py:946
  67.2 2.8 %collective-permute-start.5 = (bf16[4,48,1152]{2,1,0:T(8,128)(2,1)S(1)}, bf16[4,48,1152]{2,1,0:T(8,128)(2,1)}, u32[]{:S(2)}, u32[]{:S(2)}) collective-permute-start(bf16[4,48,1152]{2,1,0:T(8,128)(2,1)S(1)} %get-tuple-element.103), channel_id=1, source_target_pairs={{0,2},{2,0},{4,6},{6,4},{8,10},{10,8},{12,14},{14,12},{16,18},{18,... | collective-permute-start | bytes 1327112 | tf_op jit(solution)/shard_map/ppermute | solution.py:861
  70.0 1.5 collective-permute-start.6
  72.8 12.3 %middle_own.1 = (bf16[1152,1024]{1,0:T(8,128)(2,1)}, bf16[4,48,1152]{2,1,0:T(8,128)(2,1)}, bf16[4,48,1152]{2,1,0:T(8,128)(2,1)}, bf16[4,48,1152]{2,1,0:T(8,128)(2,1)}, bf16[4,48,1152]{2,1,0:T(8,128)(2,1)}) custom-call(s32[1]{0:T(128)} %bitcast.9.plane_ref, bf16[768,1024]{1,0:T(8,128)(2,1)} %get-tuple-element.92.na_ref, ...), custom_call_target="tpu_custom_call" | custom-call | flops 200000000 | bytes 120000 | tf_op jit(solution)/shard_map/middle_own/pallas_call | solution.py:764
  85.1 1.9 %collective-permute-start.12 = (bf16[4,48,1152]{2,1,0:T(8,128)(2,1)}, bf16[4,48,1152]{2,1,0:T(8,128)(2,1)S(1)}, u32[]{:S(2)}, u32[]{:S(2)}) collective-permute-start(bf16[4,48,1152]{2,1,0:T(8,128)(2,1)} %get-tuple-element.134), channel_id=1, source_target_pairs={{0,2},{2,0},{4,6},{6,4},{8,10},{10,8},{12,14},{14,12},{16,18},{18,... | collective-permute-start | bytes 1327112 | tf_op jit(solution)/shard_map/ppermute | solution.py:861
  87.0 1.5 collective-permute-start.13
  88.5 5.9 %finish_output.1 = bf16[8,128,768]{2,1,0:T(8,128)(2,1)} custom-call(f32[768,1024]{1,0:T(8,128)} %get-tuple-element.113.h1_ref, bf16[768,1024]{1,0:T(8,128)(2,1)} %get-tuple-element.114.act_ref, bf16[384,768]{1,0:T(8,128)(2,1)} %down_o.3, bf16[384,768]{1,0:T(8,128)(2,1)} %copy-done.2), custom_call_target="tpu_custom_call" | custom-call | flops 60000000 | bytes 70000 | tf_op jit(solution)/shard_map/finish_output/pallas_call | solution.py:779
  94.5 1.5 add_convert_fusion.2
  96.7 3.0 %collective-permute-start.10 = (bf16[48,1152]{1,0:T(8,128)(2,1)S(1)}, bf16[48,1152]{1,0:T(8,128)(2,1)S(1)}, u32[]{:S(2)}, u32[]{:S(2)}) collective-permute-start(bf16[48,1152]{1,0:T(8,128)(2,1)S(1)} %get-tuple-element.129), channel_id=1, source_target_pairs={{0,16},{2,18},{4,20},{6,22},{8,24},{10,26},{12,28},{14,30},{16,0},... | collective-permute-start | bytes 331784 | tf_op jit(solution)/shard_map/ppermute | solution.py:861
  99.7 1.4 collective-permute-start.11
  101.1 12.8 %back.1 = (f32[8,128,768]{2,1,0:T(8,128)}, f32[32,8,128]{2,1,0:T(8,128)}) custom-call(bf16[1152,1024]{1,0:T(8,128)(2,1)} %get-tuple-element.121.dxo_ref, bf16[1152,1024]{1,0:T(8,128)(2,1)} %get-tuple-element.122.dxp_ref, bf16[3,768,384]{2,1,0:T(8,128)(2,1)} %bitcast.59, bf16[3,768,384]{2,1,0:T(8,128)(2,1)} %copy-done.12, ...), custom_call_target="tpu_custom_call" | custom-call | flops 17999998976 | bytes 15000000 | tf_op jit(solution)/shard_map/back/pallas_call | solution.py:798
  114.2 4.7 %all-to-all-start = ((f32[32,8,128]{2,1,0:T(8,128)}), f32[32,8,128]{2,1,0:T(8,128)S(1)}, u32[]{:S(2)}, u32[]{:S(2)}) async-start(f32[32,8,128]{2,1,0:T(8,128)} %get-tuple-element.137), calls=%async_computation | async-start | bytes 262144 | tf_op jit(solution)/shard_map/all_to_all | solution.py:983
  119.7 1.8 %collective-permute-start.15 = (bf16[48,1152]{1,0:T(8,128)(2,1)S(1)}, bf16[48,1152]{1,0:T(8,128)(2,1)S(1)}, u32[]{:S(2)}, u32[]{:S(2)}) collective-permute-start(bf16[48,1152]{1,0:T(8,128)(2,1)S(1)} %get-tuple-element.167), channel_id=1, source_target_pairs={{0,8},{2,10},{4,12},{6,14},{8,0},{10,2},{12,4},{14,6},{16,24},{18,... | collective-permute-start | bytes 331784 | tf_op jit(solution)/shard_map/ppermute | solution.py:861
  121.5 2.4 %collective-permute-start.16 = (bf16[48,1152]{1,0:T(8,128)(2,1)S(1)}, bf16[48,1152]{1,0:T(8,128)(2,1)S(1)}, u32[]{:S(2)}, u32[]{:S(2)}) collective-permute-start(bf16[48,1152]{1,0:T(8,128)(2,1)S(1)} %get-tuple-element.166), channel_id=1, source_target_pairs={{0,16},{2,18},{4,20},{6,22},{8,24},{10,26},{12,28},{14,30},{16,0},... | collective-permute-start | bytes 331784 | tf_op jit(solution)/shard_map/ppermute | solution.py:861
  125.8 3.3 %collective-permute-done.15.refs_5_ = bf16[48,1152]{1,0:T(8,128)(2,1)S(1)} collective-permute-done((bf16[48,1152]{1,0:T(8,128)(2,1)S(1)}, bf16[48,1152]{1,0:T(8,128)(2,1)S(1)}, u32[]{:S(2)}, u32[]{:S(2)}) %collective-permute-start.15) | collective-permute-done | bytes 110624 | tf_op jit(solution)/shard_map/ppermute | solution.py:861
  129.1 3.9 %collective-permute-done.16.refs_6_ = bf16[48,1152]{1,0:T(8,128)(2,1)S(1)} collective-permute-done((bf16[48,1152]{1,0:T(8,128)(2,1)S(1)}, bf16[48,1152]{1,0:T(8,128)(2,1)S(1)}, u32[]{:S(2)}, u32[]{:S(2)}) %collective-permute-start.16) | collective-permute-done | bytes 110624 | tf_op jit(solution)/shard_map/ppermute | solution.py:861
  134.3 2.2 %gather.1 = (f32[48,1152]{1,0:T(8,128)}, f32[48,1152]{1,0:T(8,128)}, f32[8,128]{1,0:T(8,128)}, f32[32,128]{1,0:T(8,128)}) custom-call(bf16[48,1152]{1,0:T(8,128)(2,1)} %get-tuple-element.169.refs_0_, bf16[48,1152]{1,0:T(8,128)(2,1)} %copy-done.10, bf16[48,1152]{1,0:T(8,128)(2,1)} %copy-done.5, bf16[48,1152]{1,0:T(8,128)(2,1)} %copy-done.6, ...), custom_call_target="tpu_custom_call" | custom-call | tf_op jit(solution)/shard_map/gather/pallas_call | solution.py:832
  136.5 4.6 %all-to-all-start.1 = ((f32[32,1,128]{2,1,0:T(1,128)}), f32[32,1,128]{2,1,0:T(1,128)S(1)}, u32[]{:S(2)}, u32[]{:S(2)}) async-start(f32[32,1,128]{2,1,0:T(1,128)} %bitcast.54), calls=%async_computation.1 | async-start | bytes 32768 | tf_op jit(solution)/shard_map/all_to_all | solution.py:988
  141.1 1.4 constant_dynamic-slice_fusion.1.refs_16_
  143.1 5.0 %all-to-all-done.1 = f32[32,1,128]{2,1,0:T(1,128)S(1)} async-done(((f32[32,1,128]{2,1,0:T(1,128)}), f32[32,1,128]{2,1,0:T(1,128)S(1)}, u32[]{:S(2)}, u32[]{:S(2)}) %all-to-all-start.1) | async-done | bytes 16416 | tf_op jit(solution)/shard_map/all_to_all | solution.py:988
  148.8 2.9 %adam.1 = (f32[1,128]{1,0:T(1,128)}, f32[3,48,384]{2,1,0:T(8,128)}, f32[3,48,384]{2,1,0:T(8,128)}, f32[3,48,384]{2,1,0:T(8,128)}, f32[24,768]{1,0:T(8,128)}, /*i...) custom-call(f32[32,128]{1,0:T(8,128)} %bitcast.52, ...), custom_call_target="tpu_custom_call" | custom-call | tf_op jit(solution)/shard_map/adam/pallas_call | solution.py:846
  (63 shorter events, 11.2 us)
Async XLA Ops:
  0.7 8.2 %collective-permute-start = (bf16[3,768,384]{2,1,0:T(8,128)(2,1)}, bf16[3,768,384]{2,1,0:T(8,128)(2,1)S(1)}, u32[]{:S(2)}, u32[]{:S(2)}) collective-permute-start(bf16[3,768,384]{2,1,0:T(8,128)(2,1)} %bitcast.57), channel_id=1, source_target_pairs={{0,1},{1,0},{2,3},{3,2},{4,5},{5,4},{6,7},{7,6},{8,9},{9,8},{10,11... | collective-permute-start | bytes 5308424 | tf_op jit(solution)/shard_map/ppermute | solution.py:856
  1.2 7.6 %collective-permute-start.3 = (bf16[384,768]{1,0:T(8,128)(2,1)}, bf16[384,768]{1,0:T(8,128)(2,1)S(1)}, u32[]{:S(2)}, u32[]{:S(2)}) collective-permute-start(bf16[384,768]{1,0:T(8,128)(2,1)} %down_o.3), channel_id=1, source_target_pairs={{0,1},{1,0},{2,3},{3,2},{4,5},{5,4},{6,7},{7,6},{8,9},{9,8},{10,11... | collective-permute-start | bytes 1769480 | tf_op jit(solution)/shard_map/ppermute | solution.py:856
  1.3 7.5 %collective-permute-start.1 = (bf16[384,768]{1,0:T(8,128)(2,1)}, bf16[384,768]{1,0:T(8,128)(2,1)S(1)}, u32[]{:S(2)}, u32[]{:S(2)}) collective-permute-start(bf16[384,768]{1,0:T(8,128)(2,1)} %out_o.1), channel_id=1, source_target_pairs={{0,1},{1,0},{2,3},{3,2},{4,5},{5,4},{6,7},{7,6},{8,9},{9,8},{10,11... | collective-permute-start | bytes 1769480 | tf_op jit(solution)/shard_map/ppermute | solution.py:856
  1.7 7.1 %collective-permute-start.2 = (bf16[768,384]{1,0:T(8,128)(2,1)}, bf16[768,384]{1,0:T(8,128)(2,1)S(1)}, u32[]{:S(2)}, u32[]{:S(2)}) collective-permute-start(bf16[768,384]{1,0:T(8,128)(2,1)} %up_o.1), channel_id=1, source_target_pairs={{0,1},{1,0},{2,3},{3,2},{4,5},{5,4},{6,7},{7,6},{8,9},{9,8},{10,11... | collective-permute-start | bytes 1769480 | tf_op jit(solution)/shard_map/ppermute | solution.py:856
  52.6 12.4 %collective-permute-start.4 = (bf16[16,48,1152]{2,1,0:T(8,128)(2,1)}, bf16[16,48,1152]{2,1,0:T(8,128)(2,1)}, u32[]{:S(2)}, u32[]{:S(2)}) collective-permute-start(bf16[16,48,1152]{2,1,0:T(8,128)(2,1)} %get-tuple-element.95), channel_id=1, source_target_pairs={{0,1},{1,0},{2,3},{3,2},{4,5},{5,4},{6,7},{7,6},{8,9},{9,8},{10,11... | collective-permute-start | bytes 5308424 | tf_op jit(solution)/shard_map/ppermute | solution.py:856
  53.1 11.9 %copy-start.1 = (bf16[16,48,1152]{2,1,0:T(8,128)(2,1)S(1)}, bf16[16,48,1152]{2,1,0:T(8,128)(2,1)}, u32[]{:S(2)}) copy-start(bf16[16,48,1152]{2,1,0:T(8,128)(2,1)} %get-tuple-element.94) | copy-start | bytes 5308420
  64.9 6.7 %collective-permute-start.8 = (bf16[16,48,1152]{2,1,0:T(8,128)(2,1)}, bf16[16,48,1152]{2,1,0:T(8,128)(2,1)S(1)}, u32[]{:S(2)}, u32[]{:S(2)}) collective-permute-start(bf16[16,48,1152]{2,1,0:T(8,128)(2,1)} %get-tuple-element.108), channel_id=1, source_target_pairs={{0,1},{1,0},{2,3},{3,2},{4,5},{5,4},{6,7},{7,6},{8,9},{9,8},{10,11... | collective-permute-start | bytes 5308424 | tf_op jit(solution)/shard_map/ppermute | solution.py:856
  67.2 27.3 %collective-permute-start.5 = (bf16[4,48,1152]{2,1,0:T(8,128)(2,1)S(1)}, bf16[4,48,1152]{2,1,0:T(8,128)(2,1)}, u32[]{:S(2)}, u32[]{:S(2)}) collective-permute-start(bf16[4,48,1152]{2,1,0:T(8,128)(2,1)S(1)} %get-tuple-element.103), channel_id=1, source_target_pairs={{0,2},{2,0},{4,6},{6,4},{8,10},{10,8},{12,14},{14,12},{16,18},{18,... | collective-permute-start | bytes 1327112 | tf_op jit(solution)/shard_map/ppermute | solution.py:861
  70.0 24.5 %collective-permute-start.6 = (bf16[4,48,1152]{2,1,0:T(8,128)(2,1)S(1)}, bf16[4,48,1152]{2,1,0:T(8,128)(2,1)}, u32[]{:S(2)}, u32[]{:S(2)}) collective-permute-start(bf16[4,48,1152]{2,1,0:T(8,128)(2,1)S(1)} %get-tuple-element.104), channel_id=1, source_target_pairs={{0,4},{2,6},{4,0},{6,2},{8,12},{10,14},{12,8},{14,10},{16,20},{18,... | collective-permute-start | bytes 1327112 | tf_op jit(solution)/shard_map/ppermute | solution.py:861
  71.5 23.0 %collective-permute-start.7 = (bf16[4,48,1152]{2,1,0:T(8,128)(2,1)S(1)}, bf16[4,48,1152]{2,1,0:T(8,128)(2,1)}, u32[]{:S(2)}, u32[]{:S(2)}) collective-permute-start(bf16[4,48,1152]{2,1,0:T(8,128)(2,1)S(1)} %get-tuple-element.105), channel_id=1, source_target_pairs={{0,6},{2,4},{4,2},{6,0},{8,14},{10,12},{12,10},{14,8},{16,22},{18,... | collective-permute-start | bytes 1327112 | tf_op jit(solution)/shard_map/ppermute | solution.py:861
  85.1 28.8 %collective-permute-start.12 = (bf16[4,48,1152]{2,1,0:T(8,128)(2,1)}, bf16[4,48,1152]{2,1,0:T(8,128)(2,1)S(1)}, u32[]{:S(2)}, u32[]{:S(2)}) collective-permute-start(bf16[4,48,1152]{2,1,0:T(8,128)(2,1)} %get-tuple-element.134), channel_id=1, source_target_pairs={{0,2},{2,0},{4,6},{6,4},{8,10},{10,8},{12,14},{14,12},{16,18},{18,... | collective-permute-start | bytes 1327112 | tf_op jit(solution)/shard_map/ppermute | solution.py:861
  87.0 26.9 %collective-permute-start.13 = (bf16[4,48,1152]{2,1,0:T(8,128)(2,1)}, bf16[4,48,1152]{2,1,0:T(8,128)(2,1)S(1)}, u32[]{:S(2)}, u32[]{:S(2)}) collective-permute-start(bf16[4,48,1152]{2,1,0:T(8,128)(2,1)} %get-tuple-element.135), channel_id=1, source_target_pairs={{0,4},{2,6},{4,0},{6,2},{8,12},{10,14},{12,8},{14,10},{16,20},{18,... | collective-permute-start | bytes 1327112 | tf_op jit(solution)/shard_map/ppermute | solution.py:861
  94.5 19.5 %collective-permute-start.14 = (bf16[4,48,1152]{2,1,0:T(8,128)(2,1)}, bf16[4,48,1152]{2,1,0:T(8,128)(2,1)S(1)}, u32[]{:S(2)}, u32[]{:S(2)}) collective-permute-start(bf16[4,48,1152]{2,1,0:T(8,128)(2,1)} %get-tuple-element.136), channel_id=1, source_target_pairs={{0,6},{2,4},{4,2},{6,0},{8,14},{10,12},{12,10},{14,8},{16,22},{18,... | collective-permute-start | bytes 1327112 | tf_op jit(solution)/shard_map/ppermute | solution.py:861
  96.7 17.5 %collective-permute-start.10 = (bf16[48,1152]{1,0:T(8,128)(2,1)S(1)}, bf16[48,1152]{1,0:T(8,128)(2,1)S(1)}, u32[]{:S(2)}, u32[]{:S(2)}) collective-permute-start(bf16[48,1152]{1,0:T(8,128)(2,1)S(1)} %get-tuple-element.129), channel_id=1, source_target_pairs={{0,16},{2,18},{4,20},{6,22},{8,24},{10,26},{12,28},{14,30},{16,0},... | collective-permute-start | bytes 331784 | tf_op jit(solution)/shard_map/ppermute | solution.py:861
  99.7 14.5 %collective-permute-start.11 = (bf16[48,1152]{1,0:T(8,128)(2,1)S(1)}, bf16[48,1152]{1,0:T(8,128)(2,1)S(1)}, u32[]{:S(2)}, u32[]{:S(2)}) collective-permute-start(bf16[48,1152]{1,0:T(8,128)(2,1)S(1)} %get-tuple-element.130), channel_id=1, source_target_pairs={{0,24},{2,26},{4,28},{6,30},{8,16},{10,18},{12,20},{14,22},{16,8},... | collective-permute-start | bytes 331784 | tf_op jit(solution)/shard_map/ppermute | solution.py:861
  101.1 12.9 %copy-start.4 = (bf16[4,48,1152]{2,1,0:T(8,128)(2,1)S(1)}, bf16[4,48,1152]{2,1,0:T(8,128)(2,1)}, u32[]{:S(2)}) copy-start(bf16[4,48,1152]{2,1,0:T(8,128)(2,1)} %get-tuple-element.133) | copy-start | bytes 1327108
  114.2 19.4 %copy-start.5 = (bf16[48,1152]{1,0:T(8,128)(2,1)}, bf16[48,1152]{1,0:T(8,128)(2,1)S(1)}, u32[]{:S(2)}) copy-start(bf16[48,1152]{1,0:T(8,128)(2,1)S(1)} %collective-permute-done.10.refs_2_) | copy-start | bytes 331780
  114.2 19.4 %copy-start.6 = (bf16[48,1152]{1,0:T(8,128)(2,1)}, bf16[48,1152]{1,0:T(8,128)(2,1)S(1)}, u32[]{:S(2)}) copy-start(bf16[48,1152]{1,0:T(8,128)(2,1)S(1)} %collective-permute-done.11.refs_3_) | copy-start | bytes 331780
  114.2 19.4 %all-to-all-start = ((f32[32,8,128]{2,1,0:T(8,128)}), f32[32,8,128]{2,1,0:T(8,128)S(1)}, u32[]{:S(2)}, u32[]{:S(2)}) async-start(f32[32,8,128]{2,1,0:T(8,128)} %get-tuple-element.137), calls=%async_computation | async-start | bytes 262144 | tf_op jit(solution)/shard_map/all_to_all | solution.py:983
  119.7 9.4 %collective-permute-start.15 = (bf16[48,1152]{1,0:T(8,128)(2,1)S(1)}, bf16[48,1152]{1,0:T(8,128)(2,1)S(1)}, u32[]{:S(2)}, u32[]{:S(2)}) collective-permute-start(bf16[48,1152]{1,0:T(8,128)(2,1)S(1)} %get-tuple-element.167), channel_id=1, source_target_pairs={{0,8},{2,10},{4,12},{6,14},{8,0},{10,2},{12,4},{14,6},{16,24},{18,... | collective-permute-start | bytes 331784 | tf_op jit(solution)/shard_map/ppermute | solution.py:861
  121.5 11.5 %collective-permute-start.16 = (bf16[48,1152]{1,0:T(8,128)(2,1)S(1)}, bf16[48,1152]{1,0:T(8,128)(2,1)S(1)}, u32[]{:S(2)}, u32[]{:S(2)}) collective-permute-start(bf16[48,1152]{1,0:T(8,128)(2,1)S(1)} %get-tuple-element.166), channel_id=1, source_target_pairs={{0,16},{2,18},{4,20},{6,22},{8,24},{10,26},{12,28},{14,30},{16,0},... | collective-permute-start | bytes 331784 | tf_op jit(solution)/shard_map/ppermute | solution.py:861
  123.9 9.6 %collective-permute-start.17 = (bf16[48,1152]{1,0:T(8,128)(2,1)S(1)}, bf16[48,1152]{1,0:T(8,128)(2,1)S(1)}, u32[]{:S(2)}, u32[]{:S(2)}) collective-permute-start(bf16[48,1152]{1,0:T(8,128)(2,1)S(1)} %get-tuple-element.165), channel_id=1, source_target_pairs={{0,24},{2,26},{4,28},{6,30},{8,16},{10,18},{12,20},{14,22},{16,8},... | collective-permute-start | bytes 331784 | tf_op jit(solution)/shard_map/ppermute | solution.py:861
  124.1 9.6 %collective-permute-start.9 = (bf16[48,1152]{1,0:T(8,128)(2,1)S(1)}, bf16[48,1152]{1,0:T(8,128)(2,1)S(1)}, u32[]{:S(2)}, u32[]{:S(2)}) collective-permute-start(bf16[48,1152]{1,0:T(8,128)(2,1)S(1)} %get-tuple-element.127), channel_id=1, source_target_pairs={{0,8},{2,10},{4,12},{6,14},{8,0},{10,2},{12,4},{14,6},{16,24},{18,... | collective-permute-start | bytes 331784 | tf_op jit(solution)/shard_map/ppermute | solution.py:861
  136.5 11.7 %all-to-all-start.1 = ((f32[32,1,128]{2,1,0:T(1,128)}), f32[32,1,128]{2,1,0:T(1,128)S(1)}, u32[]{:S(2)}, u32[]{:S(2)}) async-start(f32[32,1,128]{2,1,0:T(1,128)} %bitcast.54), calls=%async_computation.1 | async-start | bytes 32768 | tf_op jit(solution)/shard_map/all_to_all | solution.py:988
  (11 other events, 13.9 us)

commit v5 on v4

--- a/solution.py
+++ b/solution.py
@@ -27,7 +27,7 @@
 IDENT_ROWS = 40
 IDENT_USED = 34
 PAIR = 2
-VMEM_BYTES = 60 * 1024 * 1024
+MEGA = 1024 * 1024
 FRONT_UNROLL = 8
 MIDDLE_UNROLL = 8
 
@@ -48,6 +48,48 @@
     centred = values - jnp.sum(values, axis=0, keepdims=True) * scale
     spread = jnp.sum(centred * centred, axis=0, keepdims=True) * scale
     return centred, lax.rsqrt(spread + NORM_EPS)
+
+
+ROWS = 96
+
+
+def fold(values):
+    return jnp.sum(values.reshape(-1, 8, values.shape[1]), axis=0)
+
+
+def row_chunks(width):
+    return [slice(r, r + ROWS) for r in range(0, width, ROWS)]
+
+
+def norm_forward(ref, lanes):
+    width = ref.shape[0]
+    total = None
+    for r in row_chunks(width):
+        part = fold(ref[r, lanes])
+        total = part if total is None else total + part
+    mean = jnp.sum(total, axis=0, keepdims=True) * (1.0 / width)
+    total = None
+    for r in row_chunks(width):
+        centred = ref[r, lanes] - mean
+        part = fold(centred * centred)
+        total = part if total is None else total + part
+    spread = jnp.sum(total, axis=0, keepdims=True) * (1.0 / width)
+    return mean, lax.rsqrt(spread + NORM_EPS)
+
+
+def norm_sums(grad_ref, unit_ref, gain_ref, acc_ref, lanes):
+    width = grad_ref.shape[0]
+    first = second = None
+    for r in row_chunks(width):
+        grad = grad_ref[r, lanes]
+        both = grad * unit_ref[r, lanes]
+        acc_ref[0, r, :] += both
+        acc_ref[1, r, :] += grad
+        gain = gain_ref[r, :]
+        one, two = fold(grad * gain), fold(both * gain)
+        first = one if first is None else first + one
+        second = two if second is None else second + two
+    return tuple(jnp.sum(v, axis=0, keepdims=True) * (1.0 / width) for v in (first, second))
 
 
 def gelu_parts(x):
@@ -145,10 +187,11 @@
         f3 = jnp.concatenate([lf[2 * ident :], rf[2 * ident :], none], axis=0)
         stack = jnp.concatenate([f1, f1, f1, none, f2, f2, f3, none], axis=0).astype(BF16)
         fs_ref[:, lanes] = stack
-        h0 = tok_ref[j].T.astype(F32) + dot_nn(est[...], stack)
-        h0_ref[:, lanes] = h0
-        centred, rec = norm_parts(h0)
-        na_ref[:, lanes] = (centred * rec * nb[0] + nb[1]).astype(BF16)
+        h0_ref[:, lanes] = tok_ref[j].T.astype(F32) + dot_nn(est[...], stack)
+        mean, rec = norm_forward(h0_ref, lanes)
+        for r in row_chunks(width):
+            unit = (h0_ref[r, lanes] - mean) * rec
+            na_ref[r, lanes] = (unit * nb[0, r, :] + nb[1, r, :]).astype(BF16)
         ct_ref[:, lanes] = cot_ref[j].T
 
 
@@ -187,7 +230,7 @@
     down_p,
     gh1_ref,
     h1_s,
-    act_s,
+    act_ref,
     q_ref,
     k_ref,
     v_ref,
@@ -203,12 +246,14 @@
     upw,
     downw,
     nb,
+    act_s,
     nbt_s,
     gp_s,
     mix_s,
     ga_s,
     mixf,
     nrm_s,
+    gb_s,
     rec_s,
 ):
     step = pl.program_id(0)
@@ -239,7 +284,6 @@
 
     phase = pl.when(step >= 0)
     groups = width // (4 * HEAD_DIM)
-    inv = 1.0 / width
     parts = tuple(slice(h * half, (h + 1) * half) for h in range(2))
     sides = tuple(slice(j * slots, (j + 1) * slots) for j in range(PAIR))
     columns = tuple(
@@ -311,40 +355,40 @@
     def _():
         for j in range(PAIR):
             mix_s[:, columns[j]] = mixf[j].astype(BF16)
-        attn = jnp.concatenate([dot_nn(outt[part, :], mix_s[:, span]) for part in parts], axis=0)
+        for part in parts:
+            h1_s[part, :] = h0_ref[part, :] + dot_nn(outt[part, :], mix_s[:, span])
         for j in range(PAIR):
-            h1 = h0_ref[:, sides[j]] + attn[:, sides[j]]
-            h1_s[:, sides[j]] = h1
-            centred, rec = norm_parts(h1)
-            unit = centred * rec
-            nrm_s[:, sides[j]] = unit
+            mean, rec = norm_forward(h1_s, sides[j])
             rec_s[j, groups, 0:1, :] = rec
-            nbt_s[:, columns[j]] = (unit * nb[0] + nb[1]).astype(BF16)
+            for r in row_chunks(width):
+                unit = (h1_s[r, sides[j]] - mean) * rec
+                nrm_s[r, sides[j]] = unit
+                nbt_s[r, columns[j]] = (unit * nb[0, r, :] + nb[1, r, :]).astype(BF16)
 
     @phase
     def _():
         for part in parts:
             act, slope = gelu_parts(dot_nn(upt[part, :], nbt_s[:, span]))
-            act_s[part, span] = act.astype(BF16)
+            low = act.astype(BF16)
+            act_s[part, span] = low
+            act_ref[part, :] = low
             back = dot_nn(downw[part, :], cot_s[:, span])
             gp_s[part, span] = (back * slope).astype(BF16)
 
     @phase
     def _():
-        grad_b = jnp.concatenate([dot_nn(upw[part, :], gp_s[:, span]) for part in parts], axis=0)
+        for part in parts:
+            gb_s[part, :] = dot_nn(upw[part, :], gp_s[:, span])
         for j in range(PAIR):
-            gb = grad_b[:, sides[j]]
-            unit = nrm_s[:, sides[j]]
-            lnacc_ref[0] += gb * unit
-            lnacc_ref[1] += gb
-            f = gb * nb[0]
-            f_mean = jnp.sum(f, axis=0, keepdims=True) * inv
-            fn_mean = jnp.sum(f * unit, axis=0, keepdims=True) * inv
-            gh1 = cot_s[:, columns[j]].astype(F32) + rec_s[j, groups, 0:1, :] * (
-                f - f_mean - unit * fn_mean
-            )
-            gh1_ref[:, sides[j]] = gh1
-            ga_s[:, columns[j]] = gh1.astype(BF16)
+            f_mean, fn_mean = norm_sums(gb_s, nrm_s, nb.at[0], lnacc_ref, sides[j])
+            rec = rec_s[j, groups, 0:1, :]
+            for r in row_chunks(width):
+                f = gb_s[r, sides[j]] * nb[0, r, :]
+                gh1 = cot_s[r, columns[j]].astype(F32) + rec * (
+                    f - f_mean - nrm_s[r, sides[j]] * fn_mean
+                )
+                gh1_ref[r, sides[j]] = gh1
+                ga_s[r, columns[j]] = gh1.astype(BF16)
 
     @phase
     def _():
@@ -383,29 +427,46 @@
             g_ref[:, :, width:] = gup.reshape(owners, 2 * some, half).astype(g_ref.dtype)
 
 
-def middle_kernel(na_ref, q_ref, k_ref, v_ref, do_ref, e_ref, dx_ref, g_ref):
-    attention_back(q_ref, k_ref, v_ref, do_ref, e_ref, dx_ref)
+def middle_kernel(
+    na_ref, q_ref, k_ref, v_ref, do_ref, e_ref, dx_ref, g_ref, na_s, dx_s
+):
+    attention_back(na_ref, q_ref, k_ref, v_ref, do_ref, e_ref, dx_ref, na_s, dx_s)
     half = dx_ref.shape[0] // 3
 
     @pl.when(pl.program_id(0) == pl.num_programs(0) - 1)
     def _():
         for c in range(3):
             cut = slice(c * half, (c + 1) * half)
-            grad = dot_nt(na_ref[...], dx_ref[cut, :])
+            grad = dot_nt(na_s[...], dx_s[cut, :])
             g_ref[:, :, cut] = grad.reshape(g_ref.shape[0:2] + (half,)).astype(BF16)
 
 
 def middle_own_kernel(
-    plane_ref, na_ref, q_ref, k_ref, v_ref, do_ref, e_ref, got_ref, dx_ref, g0, g1, g2, g3, total
+    plane_ref,
+    na_ref,
+    q_ref,
+    k_ref,
+    v_ref,
+    do_ref,
+    e_ref,
+    got_ref,
+    dx_ref,
+    g0,
+    g1,
+    g2,
+    g3,
+    na_s,
+    dx_s,
+    total,
 ):
-    attention_back(q_ref, k_ref, v_ref, do_ref, e_ref, dx_ref)
+    attention_back(na_ref, q_ref, k_ref, v_ref, do_ref, e_ref, dx_ref, na_s, dx_s)
     half = dx_ref.shape[0] // 3
 
     @pl.when(pl.program_id(0) == pl.num_programs(0) - 1)
     def _():
         for c in range(3):
             cut = slice(c * half, (c + 1) * half)
-            grad = dot_nt(na_ref[...], dx_ref[cut, :]).reshape(total.shape[0:2] + (half,))
+            grad = dot_nt(na_s[...], dx_s[cut, :]).reshape(total.shape[0:2] + (half,))
             total[:, :, cut] = (grad + got_ref[:, :, cut].astype(F32)).astype(BF16)
         plane = plane_ref[0]
         for k, g_ref in enumerate((g0, g1, g2, g3)):
@@ -413,12 +474,14 @@
                 g_ref[line] = total[line * 4 + (plane ^ k)]
 
 
-def attention_back(q_ref, k_ref, v_ref, do_ref, e_ref, dx_ref):
+def attention_back(na_ref, q_ref, k_ref, v_ref, do_ref, e_ref, dx_ref, na_s, dx_s):
     step = pl.program_id(0)
     slots = q_ref.shape[2]
     half = dx_ref.shape[0] // 3
     base = pl.multiple_of(step * PAIR * slots, PAIR * slots)
     groups = half // (4 * HEAD_DIM)
+
+    na_s[:, pl.ds(base, PAIR * slots)] = na_ref[...]
 
     def rows_of(g):
         return pl.ds(pl.multiple_of(g * 4 * PAD_DIM, 4 * PAD_DIM), 4 * PAD_DIM)
@@ -457,7 +520,9 @@
             whole = jnp.concatenate(parts, axis=0)
             if scale is not None:
                 whole = whole * scale
-            dx_ref[at, cols] = whole.astype(BF16)
+            low = whole.astype(BF16)
+            dx_s[at, cols] = low
+            dx_ref[at, pl.ds(pl.multiple_of(j * slots, slots), slots)] = low
 
     def attend(i, carry):
         at = [i * MIDDLE_UNROLL + u for u in range(MIDDLE_UNROLL)]
@@ -672,7 +737,7 @@
             pltpu.VMEM((IDENT_ROWS, width), F32),
             pltpu.VMEM((width, 256), BF16),
         ],
-        compiler_params=pltpu.CompilerParams(vmem_limit_bytes=VMEM_BYTES),
+        compiler_params=pltpu.CompilerParams(vmem_limit_bytes=60 * MEGA),
         cost_estimate=costs(8_000_000_000, 10_000_000),
         name="embed",
     )(tokens, cotangent, token_types.reshape(mols, 1, slots), pairs_t, lap_t, embed_weight, norm_params)
@@ -693,7 +758,7 @@
     outs = [
         (jax.ShapeDtypeStruct((width, toks), F32), col),
         (jax.ShapeDtypeStruct((width, toks), F32), col),
-        (jax.ShapeDtypeStruct((width, toks), BF16), whole_spec((width, toks))),
+        (jax.ShapeDtypeStruct((width, toks), BF16), col),
         (padded, lead_spec(heads * PAD_DIM, slots)),
         (padded, lead_spec(heads * PAD_DIM, slots)),
         (padded, lead_spec(heads * PAD_DIM, slots)),
@@ -721,10 +786,11 @@
         ]
         + [pltpu.VMEM((width, width), BF16)] * 5
         + [pltpu.VMEM((2, width, slots), F32)]
-        + [pltpu.VMEM((width, toks), BF16)] * 4
-        + [pltpu.VMEM((PAIR, width, slots), F32), pltpu.VMEM((width, PAIR * slots), F32)]
+        + [pltpu.VMEM((width, toks), BF16)] * 5
+        + [pltpu.VMEM((PAIR, width, slots), F32)]
+        + [pltpu.VMEM((width, PAIR * slots), F32)] * 2
         + [pltpu.VMEM((PAIR, heads // 4 + 1, 8, slots), F32)],
-        compiler_params=pltpu.CompilerParams(vmem_limit_bytes=VMEM_BYTES),
+        compiler_params=pltpu.CompilerParams(vmem_limit_bytes=52 * MEGA),
         cost_estimate=costs(60_000_000_000, 50_000_000),
         name="front",
     )(lengths, h0, na, cot, norm_params, *weights)
@@ -739,16 +805,17 @@
     gshape = (16, width // 16, 3 * half)
     dx = jax.ShapeDtypeStruct((3 * half, toks), BF16)
     specs = [
-        whole_spec(na.shape),
+        column_spec(width, slots),
         part,
         part,
         part,
         part,
         pl.BlockSpec((PAIR, heads // 2, slots, slots), lambda i: (i, which, 0, 0)),
     ]
+    scratch = [pltpu.VMEM(na.shape, BF16), pltpu.VMEM(dx.shape, BF16)]
     common = dict(
         grid=(mols // PAIR,),
-        compiler_params=pltpu.CompilerParams(vmem_limit_bytes=VMEM_BYTES),
+        compiler_params=pltpu.CompilerParams(vmem_limit_bytes=52 * MEGA),
         cost_estimate=costs(200_000_000, 120_000),
     )
     if got is None:
@@ -756,7 +823,8 @@
             middle_kernel,
             out_shape=[dx, jax.ShapeDtypeStruct(gshape, BF16)],
             in_specs=specs,
-            out_specs=[whole_spec(dx.shape), whole_spec(gshape)],
+            out_specs=[column_spec(3 * half, slots), whole_spec(gshape)],
+            scratch_shapes=scratch,
             name="middle_peer",
             **common,
         )(na, q, k, v, do, e)
@@ -765,8 +833,8 @@
         middle_own_kernel,
         out_shape=[dx] + [jax.ShapeDtypeStruct(piece, BF16)] * 4,
         in_specs=[pl.BlockSpec(memory_space=pltpu.SMEM)] + specs + [whole_spec(gshape)],
-        out_specs=[whole_spec(dx.shape)] + [whole_spec(piece)] * 4,
-        scratch_shapes=[pltpu.VMEM(gshape, BF16)],
+        out_specs=[column_spec(3 * half, slots)] + [whole_spec(piece)] * 4,
+        scratch_shapes=scratch + [pltpu.VMEM(gshape, BF16)],
         name="middle_own",
         **common,
     )(plane, na, q, k, v, do, e, got)
@@ -783,7 +851,7 @@
         in_specs=[col, col, whole_spec(down_o.shape), whole_spec(down_p.shape)],
         out_specs=lead_spec(slots, width),
         scratch_shapes=[pltpu.VMEM((width, width), BF16)],
-        compiler_params=pltpu.CompilerParams(vmem_limit_bytes=VMEM_BYTES),
+        compiler_params=pltpu.CompilerParams(vmem_limit_bytes=48 * MEGA),
         cost_estimate=costs(60_000_000, 70_000),
         name="finish_output",
     )(h1, act, down_o, down_p)
@@ -820,7 +888,7 @@
             pltpu.VMEM((width, fs.shape[0]), F32),
             pltpu.VMEM((width, 3 * width), BF16),
         ],
-        compiler_params=pltpu.CompilerParams(vmem_limit_bytes=VMEM_BYTES),
+        compiler_params=pltpu.CompilerParams(vmem_limit_bytes=46 * MEGA),
         cost_estimate=costs(18_000_000_000, 15_000_000),
         name="back",
     )(dxo, dxp, qkv_o, qkv_p, h0, gh1, fs, gain, lnb)
@@ -837,7 +905,7 @@
             jax.ShapeDtypeStruct(got.shape[1:], F32),
             jax.ShapeDtypeStruct((got.shape[0], lanes), F32),
         ],
-        compiler_params=pltpu.CompilerParams(vmem_limit_bytes=VMEM_BYTES),
+        compiler_params=pltpu.CompilerParams(vmem_limit_bytes=40 * MEGA),
         name="gather",
     )(*firsts, *seconds, got)
 
@@ -847,7 +915,7 @@
         adam_kernel,
         out_shape=[jax.ShapeDtypeStruct((1, squares.shape[1]), F32)]
         + [jax.ShapeDtypeStruct(a.shape, F32) for a in state],
-        compiler_params=pltpu.CompilerParams(vmem_limit_bytes=VMEM_BYTES),
+        compiler_params=pltpu.CompilerParams(vmem_limit_bytes=40 * MEGA),
         name="adam",
     )(squares, red1, red2, small, *state)
 

time: 153 us -> 143 us (0.935)
  Pallas kernels: 96.9 us -> 87.4 us
  local copies, waits for them, and re-layouts: 8.72 us -> 5.52 us
  waiting for transfers between devices: 12.9 us -> 15.4 us
    pallas_call x1, Pallas kernels: 12.8 us -> 10.7 us  [back(): pl.pallas_call(back_kernel, grid=(mols // PAIR,), out_shape=[jax.ShapeDty...]
    pallas_call x1, Pallas kernels: 5.91 us -> 3.92 us  [finish_output(): pl.pallas_call(output_kernel, grid=(mols // PAIR,), out_shape=jax.ShapeDt...]
    all_to_all x1, waiting for transfers between devices: 5.04 us -> 6.92 us  [on_device(): lax.all_to_all(squares.reshape(world, 1, lanes), ('dp', 'mp'), 0, 0, tile...]
    unnamed x31 -> x69, local copies, waits for them, and re-layouts: 4.97 us -> 4.34 us
  transfers between devices with their start and end apart: 20 -> 20, of which waited for: 5 -> 4; matrix products, arithmetic and copies ran while one was open for 5% -> 4% of each run, Pallas kernels for 33% -> 31%
where the time goes in v5:
time: 143 us; the launch traced here: 142 us
  Pallas kernels  87.4 us (61%)
  starting transfers between devices  28.8 us (20%)
  waiting for transfers between devices  15.4 us (11%)
  local copies, waits for them, and re-layouts  5.52 us (4%)
  other arithmetic  3.8 us (3%)
    pallas_call x1, Pallas kernels, front(): pl.pallas_call(front_kernel, grid=(mols // PAIR,), out_shape=[o[0] for o...  40.6 us
    ppermute x12, starting transfers between devices, hop(): return lax.ppermute(value, 'dp', [(i, i ^ flip) for i in range(size)])  17.8 us
    pallas_call x1, Pallas kernels, middle(): pl.pallas_call(middle_own_kernel, out_shape=[dx] + [jax.ShapeDtypeStruct(...  11.6 us
    pallas_call x1, Pallas kernels, middle(): pl.pallas_call(middle_kernel, out_shape=[dx, jax.ShapeDtypeStruct(gshape,...  11.3 us
    pallas_call x1, Pallas kernels, back(): pl.pallas_call(back_kernel, grid=(mols // PAIR,), out_shape=[jax.ShapeDty...  10.7 us
    ppermute x12, waiting for transfers between devices, hop(): return lax.ppermute(value, 'dp', [(i, i ^ flip) for i in range(size)])  8.46 us
    all_to_all x1, waiting for transfers between devices, on_device(): lax.all_to_all(squares.reshape(world, 1, lanes), ('dp', 'mp'), 0, 0, tile...  6.92 us
    pallas_call x1, Pallas kernels, embed(): pl.pallas_call(embed_kernel, grid=(mols // PAIR,), out_shape=[jax.ShapeDt...  6.82 us
  transfers between devices with their start and end apart: 20, of which 4 were waited for; matrix products, arithmetic and copies ran while one was open for 4% of the time, Pallas kernels for 31%

profile of v5, /device:TPU:0, one launch (start us, length us, event | category | flops | bytes accessed | tf_op | source)
XLA Modules:
  0.0 142.1 jit_solution(17848065347481675136)
XLA Ops:
  1.8 6.8 %embed.1 = (f32[768,1024]{1,0:T(8,128)}, bf16[768,1024]{1,0:T(8,128)(2,1)}, bf16[256,1024]{1,0:T(8,128)(2,1)}, bf16[768,1024]{1,0:T(8,128)(2,1)}) custom-call(bf16[8,128,768]{2,1,0:T(8,128)(2,1)} %tok_ref.1, bf16[8,128,768]{2,1,0:T(8,128)(2,1)} %cot_ref.1, s32[8,1,128]{2,1,0:T(1,128)} %bitcast.67, s32[8,2,128]{2,1,0:T(2,128)} %bitcast.66, ...), custom_call_target="tpu_custom_call" | custom-call | flops 8000000000 | bytes 10000000 | tf_op jit(solution)/shard_map/embed/pallas_call | solution.py:721
  8.7 1.3 copy-done.25
  10.1 40.6 %front.1 = (f32[768,1024]{1,0:T(8,128)}, f32[768,1024]{1,0:T(8,128)}, bf16[768,1024]{1,0:T(8,128)(2,1)}, bf16[8,1024,128]{2,1,0:T(8,128)(2,1)}, bf16[8,1024,128]...) custom-call(s32[8]{0:T(128)S(1)} %copy-done.29, ...), custom_call_target="tpu_custom_call" | custom-call | flops 60000002048 | bytes 50000000 | tf_op jit(solution)/shard_map/front/pallas_call | solution.py:771
  51.3 11.3 %middle_peer.1 = (bf16[1152,1024]{1,0:T(8,128)(2,1)}, bf16[16,48,1152]{2,1,0:T(8,128)(2,1)}) custom-call(bf16[768,1024]{1,0:T(8,128)(2,1)S(1)} %copy-done, bf16[8,1024,128]{2,1,0:T(8,128)(2,1)} %get-tuple-element.96.q_ref, bf16[8,1024,128]{2,1,0:T(8,128)(2,1)} %get-tuple-element.97.k_ref, bf16[8,1024,128]{2,1,0:T(8,128)(2,1)} %get-tuple-element.98.v_ref, ...), custom_call_target="tpu_custom_call" | custom-call | flops 200000000 | bytes 120000 | tf_op jit(solution)/shard_map/middle_peer/pallas_call | solution.py:822
  62.7 1.9 %add_convert_fusion = bf16[16,48,1152]{2,1,0:T(8,128)(2,1)S(1)} fusion(bf16[16,48,1152]{2,1,0:T(8,128)(2,1)} %collective-permute-done.4, bf16[16,48,1152]{2,1,0:T(8,128)(2,1)S(1)} %copy-done.33), kind=kLoop, calls=%fused_computation | loop fusion | flops 3538944 | bytes 5308416 | tf_op jit(solution)/shard_map/convert_element_type | solution.py:1014
  64.8 3.0 %collective-permute-start.5 = (bf16[4,48,1152]{2,1,0:T(8,128)(2,1)S(1)}, bf16[4,48,1152]{2,1,0:T(8,128)(2,1)}, u32[]{:S(2)}, u32[]{:S(2)}) collective-permute-start(bf16[4,48,1152]{2,1,0:T(8,128)(2,1)S(1)} %get-tuple-element.103), channel_id=1, source_target_pairs={{0,2},{2,0},{4,6},{6,4},{8,10},{10,8},{12,14},{14,12},{16,18},{18,... | collective-permute-start | bytes 1327112 | tf_op jit(solution)/shard_map/ppermute | solution.py:929
  67.7 1.5 %collective-permute-start.6 = (bf16[4,48,1152]{2,1,0:T(8,128)(2,1)S(1)}, bf16[4,48,1152]{2,1,0:T(8,128)(2,1)}, u32[]{:S(2)}, u32[]{:S(2)}) collective-permute-start(bf16[4,48,1152]{2,1,0:T(8,128)(2,1)S(1)} %get-tuple-element.104), channel_id=1, source_target_pairs={{0,4},{2,6},{4,0},{6,2},{8,12},{10,14},{12,8},{14,10},{16,20},{18,... | collective-permute-start | bytes 1327112 | tf_op jit(solution)/shard_map/ppermute | solution.py:929
  70.5 11.6 %middle_own.1 = (bf16[1152,1024]{1,0:T(8,128)(2,1)}, bf16[4,48,1152]{2,1,0:T(8,128)(2,1)S(1)}, bf16[4,48,1152]{2,1,0:T(8,128)(2,1)S(1)}, bf16[4,48,1152]{2,1,0:T(8,128)(2,1)S(1)}, bf16[4,48,1152]{2,1,0:T(8,128)(2,1)S(1)}) custom-call(s32[1]{0:T(128)} %bitcast.9.plane_ref, bf16[768,1024]{1,0:T(8,128)(2,1)} %get-tuple-element.92.na_ref, ...), custom_call_target="tpu_custom_call" | custom-call | flops 200000000 | bytes 120000 | tf_op jit(solution)/shard_map/middle_own/pallas_call | solution.py:832
  82.1 1.9 %collective-permute-start.12 = (bf16[4,48,1152]{2,1,0:T(8,128)(2,1)S(1)}, bf16[4,48,1152]{2,1,0:T(8,128)(2,1)S(1)}, u32[]{:S(2)}, u32[]{:S(2)}) collective-permute-start(bf16[4,48,1152]{2,1,0:T(8,128)(2,1)S(1)} %get-tuple-element.134), channel_id=1, source_target_pairs={{0,2},{2,0},{4,6},{6,4},{8,10},{10,8},{12,14},{14,12},{16,18},{18,... | collective-permute-start | bytes 1327112 | tf_op jit(solution)/shard_map/ppermute | solution.py:929
  84.1 1.5 %collective-permute-start.13 = (bf16[4,48,1152]{2,1,0:T(8,128)(2,1)S(1)}, bf16[4,48,1152]{2,1,0:T(8,128)(2,1)S(1)}, u32[]{:S(2)}, u32[]{:S(2)}) collective-permute-start(bf16[4,48,1152]{2,1,0:T(8,128)(2,1)S(1)} %get-tuple-element.135), channel_id=1, source_target_pairs={{0,4},{2,6},{4,0},{6,2},{8,12},{10,14},{12,8},{14,10},{16,20},{18,... | collective-permute-start | bytes 1327112 | tf_op jit(solution)/shard_map/ppermute | solution.py:929
  85.6 3.9 %finish_output.1 = bf16[8,128,768]{2,1,0:T(8,128)(2,1)} custom-call(f32[768,1024]{1,0:T(8,128)S(1)} %copy-done.1, bf16[768,1024]{1,0:T(8,128)(2,1)S(1)} %copy-done.2, bf16[384,768]{1,0:T(8,128)(2,1)S(1)} %copy-done.3, bf16[384,768]{1,0:T(8,128)(2,1)S(1)} %copy-done.5), custom_call_target="tpu_custom_call" | custom-call | flops 60000000 | bytes 70000 | tf_op jit(solution)/shard_map/finish_output/pallas_call | solution.py:847
  89.9 1.7 %add_convert_fusion.2 = bf16[4,48,1152]{2,1,0:T(8,128)(2,1)S(1)} fusion(bf16[4,48,1152]{2,1,0:T(8,128)(2,1)} %collective-permute-done.7, bf16[4,48,1152]{2,1,0:T(8,128)(2,1)} %collective-permute-done.6, bf16[4,48,1152]{2,1,0:T(8,128)(2,1)} %collective-permute-done.5, bf16[4,48,1152]{2,1,0:T(8,128)(2,1)S(1)} %get-tuple-element.116), kind=kLoop, calls=%fused_computation.2 | loop fusion | flops 1769472 | bytes 2211840 | tf_op jit(solution)/shard_map/convert_element_type | solution.py:940
  91.6 3.0 %collective-permute-start.10 = (bf16[48,1152]{1,0:T(8,128)(2,1)S(1)}, bf16[48,1152]{1,0:T(8,128)(2,1)S(1)}, u32[]{:S(2)}, u32[]{:S(2)}) collective-permute-start(bf16[48,1152]{1,0:T(8,128)(2,1)S(1)} %get-tuple-element.129), channel_id=1, source_target_pairs={{0,16},{2,18},{4,20},{6,22},{8,24},{10,26},{12,28},{14,30},{16,0},... | collective-permute-start | bytes 331784 | tf_op jit(solution)/shard_map/ppermute | solution.py:929
  94.6 1.3 collective-permute-start.11
  96.0 1.5 %copy-done.24 = bf16[768,3,384]{2,0,1:T(8,128)(2,1)S(1)} copy-done((bf16[768,3,384]{2,0,1:T(8,128)(2,1)S(1)}, bf16[768,3,384]{2,0,1:T(8,128)(2,1)}, u32[]{:S(2)}) %copy-start.24) | copy-done | bytes 1769496
  97.5 10.7 %back.1 = (f32[8,128,768]{2,1,0:T(8,128)}, f32[32,8,128]{2,1,0:T(8,128)}) custom-call(bf16[1152,1024]{1,0:T(8,128)(2,1)S(1)} %copy-done.23, bf16[1152,1024]{1,0:T(8,128)(2,1)} %get-tuple-element.122.dxp_ref, bf16[3,768,384]{2,1,0:T(8,128)(2,1)S(1)} %bitcast.57, bf16[3,768,384]{2,1,0:T(8,128)(2,1)S(1)} %copy-done.26, f32[768,1024]{1,0:T(8,128)} %get-tuple-element.91.h0_ref, ...), custom_call_target="tpu_custom_call" | custom-call | flops 17999998976 | bytes 15000000 | tf_op jit(solution)/shard_map/back/pallas_call | solution.py:866
  108.6 4.7 %all-to-all-start = ((f32[32,8,128]{2,1,0:T(8,128)}), f32[32,8,128]{2,1,0:T(8,128)S(1)}, u32[]{:S(2)}, u32[]{:S(2)}) async-start(f32[32,8,128]{2,1,0:T(8,128)} %get-tuple-element.137), calls=%async_computation | async-start | bytes 262144 | tf_op jit(solution)/shard_map/all_to_all | solution.py:1051
  113.3 1.8 %collective-permute-start.15 = (bf16[48,1152]{1,0:T(8,128)(2,1)S(1)}, bf16[48,1152]{1,0:T(8,128)(2,1)S(1)}, u32[]{:S(2)}, u32[]{:S(2)}) collective-permute-start(bf16[48,1152]{1,0:T(8,128)(2,1)S(1)} %get-tuple-element.167), channel_id=1, source_target_pairs={{0,8},{2,10},{4,12},{6,14},{8,0},{10,2},{12,4},{14,6},{16,24},{18,... | collective-permute-start | bytes 331784 | tf_op jit(solution)/shard_map/ppermute | solution.py:929
  115.1 2.4 %collective-permute-start.16 = (bf16[48,1152]{1,0:T(8,128)(2,1)S(1)}, bf16[48,1152]{1,0:T(8,128)(2,1)S(1)}, u32[]{:S(2)}, u32[]{:S(2)}) collective-permute-start(bf16[48,1152]{1,0:T(8,128)(2,1)S(1)} %get-tuple-element.166), channel_id=1, source_target_pairs={{0,16},{2,18},{4,20},{6,22},{8,24},{10,26},{12,28},{14,30},{16,0},... | collective-permute-start | bytes 331784 | tf_op jit(solution)/shard_map/ppermute | solution.py:929
  119.5 3.9 %collective-permute-done.15.refs_5_ = bf16[48,1152]{1,0:T(8,128)(2,1)S(1)} collective-permute-done((bf16[48,1152]{1,0:T(8,128)(2,1)S(1)}, bf16[48,1152]{1,0:T(8,128)(2,1)S(1)}, u32[]{:S(2)}, u32[]{:S(2)}) %collective-permute-start.15) | collective-permute-done | bytes 110624 | tf_op jit(solution)/shard_map/ppermute | solution.py:929
  123.4 4.3 %collective-permute-done.17.refs_7_ = bf16[48,1152]{1,0:T(8,128)(2,1)S(1)} collective-permute-done((bf16[48,1152]{1,0:T(8,128)(2,1)S(1)}, bf16[48,1152]{1,0:T(8,128)(2,1)S(1)}, u32[]{:S(2)}, u32[]{:S(2)}) %collective-permute-start.17) | collective-permute-done | bytes 110624 | tf_op jit(solution)/shard_map/ppermute | solution.py:929
  128.6 4.7 %all-to-all-start.1 = ((f32[32,1,128]{2,1,0:T(1,128)}), f32[32,1,128]{2,1,0:T(1,128)S(1)}, u32[]{:S(2)}, u32[]{:S(2)}) async-start(f32[32,1,128]{2,1,0:T(1,128)} %bitcast.19), calls=%async_computation.1 | async-start | bytes 32768 | tf_op jit(solution)/shard_map/all_to_all | solution.py:1056
  133.4 6.9 %all-to-all-done.1 = f32[32,1,128]{2,1,0:T(1,128)S(1)} async-done(((f32[32,1,128]{2,1,0:T(1,128)}), f32[32,1,128]{2,1,0:T(1,128)S(1)}, u32[]{:S(2)}, u32[]{:S(2)}) %all-to-all-start.1) | async-done | bytes 16416 | tf_op jit(solution)/shard_map/all_to_all | solution.py:1056
  140.5 1.5 %adam.1 = (f32[1,128]{1,0:T(1,128)}, f32[3,48,384]{2,1,0:T(8,128)}, f32[3,48,384]{2,1,0:T(8,128)}, f32[3,48,384]{2,1,0:T(8,128)}, f32[24,768]{1,0:T(8,128)}, /*i...) custom-call(f32[32,128]{1,0:T(8,128)S(1)} %bitcast.51, ...), custom_call_target="tpu_custom_call" | custom-call | tf_op jit(solution)/shard_map/adam/pallas_call | solution.py:914
  (101 shorter events, 7.0 us)
Async XLA Ops:
  0.7 8.0 %collective-permute-start = (bf16[3,768,384]{2,1,0:T(8,128)(2,1)}, bf16[3,768,384]{2,1,0:T(8,128)(2,1)S(1)}, u32[]{:S(2)}, u32[]{:S(2)}) collective-permute-start(bf16[3,768,384]{2,1,0:T(8,128)(2,1)} %bitcast.55), channel_id=1, source_target_pairs={{0,1},{1,0},{2,3},{3,2},{4,5},{5,4},{6,7},{7,6},{8,9},{9,8},{10,11... | collective-permute-start | bytes 5308424 | tf_op jit(solution)/shard_map/ppermute | solution.py:924
  1.2 7.4 %collective-permute-start.3 = (bf16[384,768]{1,0:T(8,128)(2,1)}, bf16[384,768]{1,0:T(8,128)(2,1)S(1)}, u32[]{:S(2)}, u32[]{:S(2)}) collective-permute-start(bf16[384,768]{1,0:T(8,128)(2,1)} %down_o.3), channel_id=1, source_target_pairs={{0,1},{1,0},{2,3},{3,2},{4,5},{5,4},{6,7},{7,6},{8,9},{9,8},{10,11... | collective-permute-start | bytes 1769480 | tf_op jit(solution)/shard_map/ppermute | solution.py:924
  1.3 7.4 %collective-permute-start.1 = (bf16[384,768]{1,0:T(8,128)(2,1)}, bf16[384,768]{1,0:T(8,128)(2,1)}, u32[]{:S(2)}, u32[]{:S(2)}) collective-permute-start(bf16[384,768]{1,0:T(8,128)(2,1)} %out_o.1), channel_id=1, source_target_pairs={{0,1},{1,0},{2,3},{3,2},{4,5},{5,4},{6,7},{7,6},{8,9},{9,8},{10,11... | collective-permute-start | bytes 1769480 | tf_op jit(solution)/shard_map/ppermute | solution.py:924
  1.7 6.9 %collective-permute-start.2 = (bf16[768,384]{1,0:T(8,128)(2,1)}, bf16[768,384]{1,0:T(8,128)(2,1)}, u32[]{:S(2)}, u32[]{:S(2)}) collective-permute-start(bf16[768,384]{1,0:T(8,128)(2,1)} %up_o.1), channel_id=1, source_target_pairs={{0,1},{1,0},{2,3},{3,2},{4,5},{5,4},{6,7},{7,6},{8,9},{9,8},{10,11... | collective-permute-start | bytes 1769480 | tf_op jit(solution)/shard_map/ppermute | solution.py:924
  10.1 41.2 %copy-start = (bf16[768,1024]{1,0:T(8,128)(2,1)S(1)}, bf16[768,1024]{1,0:T(8,128)(2,1)}, u32[]{:S(2)}) copy-start(bf16[768,1024]{1,0:T(8,128)(2,1)} %get-tuple-element.92.na_ref) | copy-start | bytes 4718596
  50.8 11.9 %collective-permute-start.4 = (bf16[16,48,1152]{2,1,0:T(8,128)(2,1)}, bf16[16,48,1152]{2,1,0:T(8,128)(2,1)}, u32[]{:S(2)}, u32[]{:S(2)}) collective-permute-start(bf16[16,48,1152]{2,1,0:T(8,128)(2,1)} %get-tuple-element.95), channel_id=1, source_target_pairs={{0,1},{1,0},{2,3},{3,2},{4,5},{5,4},{6,7},{7,6},{8,9},{9,8},{10,11... | collective-permute-start | bytes 5308424 | tf_op jit(solution)/shard_map/ppermute | solution.py:924
  62.6 6.7 %collective-permute-start.8 = (bf16[16,48,1152]{2,1,0:T(8,128)(2,1)}, bf16[16,48,1152]{2,1,0:T(8,128)(2,1)S(1)}, u32[]{:S(2)}, u32[]{:S(2)}) collective-permute-start(bf16[16,48,1152]{2,1,0:T(8,128)(2,1)} %get-tuple-element.108), channel_id=1, source_target_pairs={{0,1},{1,0},{2,3},{3,2},{4,5},{5,4},{6,7},{7,6},{8,9},{9,8},{10,11... | collective-permute-start | bytes 5308424 | tf_op jit(solution)/shard_map/ppermute | solution.py:924
  64.8 24.8 %collective-permute-start.5 = (bf16[4,48,1152]{2,1,0:T(8,128)(2,1)S(1)}, bf16[4,48,1152]{2,1,0:T(8,128)(2,1)}, u32[]{:S(2)}, u32[]{:S(2)}) collective-permute-start(bf16[4,48,1152]{2,1,0:T(8,128)(2,1)S(1)} %get-tuple-element.103), channel_id=1, source_target_pairs={{0,2},{2,0},{4,6},{6,4},{8,10},{10,8},{12,14},{14,12},{16,18},{18,... | collective-permute-start | bytes 1327112 | tf_op jit(solution)/shard_map/ppermute | solution.py:929
  67.7 21.9 %collective-permute-start.6 = (bf16[4,48,1152]{2,1,0:T(8,128)(2,1)S(1)}, bf16[4,48,1152]{2,1,0:T(8,128)(2,1)}, u32[]{:S(2)}, u32[]{:S(2)}) collective-permute-start(bf16[4,48,1152]{2,1,0:T(8,128)(2,1)S(1)} %get-tuple-element.104), channel_id=1, source_target_pairs={{0,4},{2,6},{4,0},{6,2},{8,12},{10,14},{12,8},{14,10},{16,20},{18,... | collective-permute-start | bytes 1327112 | tf_op jit(solution)/shard_map/ppermute | solution.py:929
  69.3 20.6 %collective-permute-start.7 = (bf16[4,48,1152]{2,1,0:T(8,128)(2,1)S(1)}, bf16[4,48,1152]{2,1,0:T(8,128)(2,1)}, u32[]{:S(2)}, u32[]{:S(2)}) collective-permute-start(bf16[4,48,1152]{2,1,0:T(8,128)(2,1)S(1)} %get-tuple-element.105), channel_id=1, source_target_pairs={{0,6},{2,4},{4,2},{6,0},{8,14},{10,12},{12,10},{14,8},{16,22},{18,... | collective-permute-start | bytes 1327112 | tf_op jit(solution)/shard_map/ppermute | solution.py:929
  82.1 26.2 %collective-permute-start.12 = (bf16[4,48,1152]{2,1,0:T(8,128)(2,1)S(1)}, bf16[4,48,1152]{2,1,0:T(8,128)(2,1)S(1)}, u32[]{:S(2)}, u32[]{:S(2)}) collective-permute-start(bf16[4,48,1152]{2,1,0:T(8,128)(2,1)S(1)} %get-tuple-element.134), channel_id=1, source_target_pairs={{0,2},{2,0},{4,6},{6,4},{8,10},{10,8},{12,14},{14,12},{16,18},{18,... | collective-permute-start | bytes 1327112 | tf_op jit(solution)/shard_map/ppermute | solution.py:929
  84.1 24.2 %collective-permute-start.13 = (bf16[4,48,1152]{2,1,0:T(8,128)(2,1)S(1)}, bf16[4,48,1152]{2,1,0:T(8,128)(2,1)S(1)}, u32[]{:S(2)}, u32[]{:S(2)}) collective-permute-start(bf16[4,48,1152]{2,1,0:T(8,128)(2,1)S(1)} %get-tuple-element.135), channel_id=1, source_target_pairs={{0,4},{2,6},{4,0},{6,2},{8,12},{10,14},{12,8},{14,10},{16,20},{18,... | collective-permute-start | bytes 1327112 | tf_op jit(solution)/shard_map/ppermute | solution.py:929
  89.5 18.8 %collective-permute-start.14 = (bf16[4,48,1152]{2,1,0:T(8,128)(2,1)S(1)}, bf16[4,48,1152]{2,1,0:T(8,128)(2,1)S(1)}, u32[]{:S(2)}, u32[]{:S(2)}) collective-permute-start(bf16[4,48,1152]{2,1,0:T(8,128)(2,1)S(1)} %get-tuple-element.136), channel_id=1, source_target_pairs={{0,6},{2,4},{4,2},{6,0},{8,14},{10,12},{12,10},{14,8},{16,22},{18,... | collective-permute-start | bytes 1327112 | tf_op jit(solution)/shard_map/ppermute | solution.py:929
  91.6 17.0 %collective-permute-start.10 = (bf16[48,1152]{1,0:T(8,128)(2,1)S(1)}, bf16[48,1152]{1,0:T(8,128)(2,1)S(1)}, u32[]{:S(2)}, u32[]{:S(2)}) collective-permute-start(bf16[48,1152]{1,0:T(8,128)(2,1)S(1)} %get-tuple-element.129), channel_id=1, source_target_pairs={{0,16},{2,18},{4,20},{6,22},{8,24},{10,26},{12,28},{14,30},{16,0},... | collective-permute-start | bytes 331784 | tf_op jit(solution)/shard_map/ppermute | solution.py:929
  94.6 13.9 %collective-permute-start.11 = (bf16[48,1152]{1,0:T(8,128)(2,1)S(1)}, bf16[48,1152]{1,0:T(8,128)(2,1)S(1)}, u32[]{:S(2)}, u32[]{:S(2)}) collective-permute-start(bf16[48,1152]{1,0:T(8,128)(2,1)S(1)} %get-tuple-element.130), channel_id=1, source_target_pairs={{0,24},{2,26},{4,28},{6,30},{8,16},{10,18},{12,20},{14,22},{16,8},... | collective-permute-start | bytes 331784 | tf_op jit(solution)/shard_map/ppermute | solution.py:929
  108.1 32.3 %copy-start.6 = (f32[48,3,384]{2,0,1:T(8,128)S(1)}, f32[48,3,384]{2,0,1:T(8,128)}, u32[]{:S(2)}) copy-start(f32[48,3,384]{2,0,1:T(8,128)} %param.38) | copy-start | bytes 663556
  108.1 32.3 %copy-start.7 = (f32[48,3,384]{2,0,1:T(8,128)S(1)}, f32[48,3,384]{2,0,1:T(8,128)}, u32[]{:S(2)}) copy-start(f32[48,3,384]{2,0,1:T(8,128)} %param.39) | copy-start | bytes 663556
  108.1 32.3 %copy-start.8 = (f32[48,3,384]{2,0,1:T(8,128)S(1)}, f32[48,3,384]{2,0,1:T(8,128)}, u32[]{:S(2)}) copy-start(f32[48,3,384]{2,0,1:T(8,128)} %param.40) | copy-start | bytes 663556
  108.6 19.1 %all-to-all-start = ((f32[32,8,128]{2,1,0:T(8,128)}), f32[32,8,128]{2,1,0:T(8,128)S(1)}, u32[]{:S(2)}, u32[]{:S(2)}) async-start(f32[32,8,128]{2,1,0:T(8,128)} %get-tuple-element.137), calls=%async_computation | async-start | bytes 262144 | tf_op jit(solution)/shard_map/all_to_all | solution.py:1051
  113.3 10.1 %collective-permute-start.15 = (bf16[48,1152]{1,0:T(8,128)(2,1)S(1)}, bf16[48,1152]{1,0:T(8,128)(2,1)S(1)}, u32[]{:S(2)}, u32[]{:S(2)}) collective-permute-start(bf16[48,1152]{1,0:T(8,128)(2,1)S(1)} %get-tuple-element.167), channel_id=1, source_target_pairs={{0,8},{2,10},{4,12},{6,14},{8,0},{10,2},{12,4},{14,6},{16,24},{18,... | collective-permute-start | bytes 331784 | tf_op jit(solution)/shard_map/ppermute | solution.py:929
  115.1 8.3 %collective-permute-start.16 = (bf16[48,1152]{1,0:T(8,128)(2,1)S(1)}, bf16[48,1152]{1,0:T(8,128)(2,1)S(1)}, u32[]{:S(2)}, u32[]{:S(2)}) collective-permute-start(bf16[48,1152]{1,0:T(8,128)(2,1)S(1)} %get-tuple-element.166), channel_id=1, source_target_pairs={{0,16},{2,18},{4,20},{6,22},{8,24},{10,26},{12,28},{14,30},{16,0},... | collective-permute-start | bytes 331784 | tf_op jit(solution)/shard_map/ppermute | solution.py:929
  117.5 10.1 %collective-permute-start.17 = (bf16[48,1152]{1,0:T(8,128)(2,1)S(1)}, bf16[48,1152]{1,0:T(8,128)(2,1)S(1)}, u32[]{:S(2)}, u32[]{:S(2)}) collective-permute-start(bf16[48,1152]{1,0:T(8,128)(2,1)S(1)} %get-tuple-element.165), channel_id=1, source_target_pairs={{0,24},{2,26},{4,28},{6,30},{8,16},{10,18},{12,20},{14,22},{16,8},... | collective-permute-start | bytes 331784 | tf_op jit(solution)/shard_map/ppermute | solution.py:929
  117.7 9.9 %collective-permute-start.9 = (bf16[48,1152]{1,0:T(8,128)(2,1)S(1)}, bf16[48,1152]{1,0:T(8,128)(2,1)S(1)}, u32[]{:S(2)}, u32[]{:S(2)}) collective-permute-start(bf16[48,1152]{1,0:T(8,128)(2,1)S(1)} %get-tuple-element.127), channel_id=1, source_target_pairs={{0,8},{2,10},{4,12},{6,14},{8,0},{10,2},{12,4},{14,6},{16,24},{18,... | collective-permute-start | bytes 331784 | tf_op jit(solution)/shard_map/ppermute | solution.py:929
  128.6 11.8 %all-to-all-start.1 = ((f32[32,1,128]{2,1,0:T(1,128)}), f32[32,1,128]{2,1,0:T(1,128)S(1)}, u32[]{:S(2)}, u32[]{:S(2)}) async-start(f32[32,1,128]{2,1,0:T(1,128)} %bitcast.19), calls=%async_computation.1 | async-start | bytes 32768 | tf_op jit(solution)/shard_map/all_to_all | solution.py:1056
  (30 other events, 563.3 us)

commit v6 on v5

--- a/solution.py
+++ b/solution.py
@@ -28,6 +28,7 @@
 IDENT_USED = 34
 PAIR = 2
 MEGA = 1024 * 1024
+GATHER_COST = 3000000000
 FRONT_UNROLL = 8
 MIDDLE_UNROLL = 8
 
@@ -636,22 +637,25 @@
 
 
 def gather_kernel(*refs):
-    firsts, seconds, got_ref = refs[0:4], refs[4:8], refs[8]
-    red1_ref, red2_ref, small_ref, sq_ref = refs[9:]
-    lanes = sq_ref.shape[1]
+    firsts, seconds = refs[0:4], refs[4:8]
+    red1_ref, red2_ref, sq_ref = refs[8:]
     rows = None
     for refs4, red_ref in ((firsts, red1_ref), (seconds, red2_ref)):
         red = refs4[0][...].astype(F32)
         for ref in refs4[1:]:
             red = red + ref[...].astype(F32)
         red_ref[...] = red
-        part = square_sum(red, lanes)
+        part = square_sum(red, sq_ref.shape[1])
         rows = part if rows is None else rows + part
+    sq_ref[...] = rows
+
+
+def small_kernel(got_ref, rows_ref, small_ref, sq_ref):
     small = got_ref[0]
     for o in range(1, got_ref.shape[0]):
         small = small + got_ref[o]
     small_ref[...] = small
-    rows = rows + square_sum(small, lanes)
+    rows = rows_ref[...] + square_sum(small, sq_ref.shape[1])
     sq_ref[...] = jnp.full(sq_ref.shape, jnp.sum(rows), F32)
 
 
@@ -894,20 +898,31 @@
     )(dxo, dxp, qkv_o, qkv_p, h0, gh1, fs, gain, lnb)
 
 
-def gather(firsts, seconds, got):
+def gather(firsts, seconds):
     rows, columns = firsts[0].shape
-    lanes = got.shape[2]
     return pl.pallas_call(
         gather_kernel,
         out_shape=[
             jax.ShapeDtypeStruct((rows, columns), F32),
             jax.ShapeDtypeStruct((rows, columns), F32),
-            jax.ShapeDtypeStruct(got.shape[1:], F32),
-            jax.ShapeDtypeStruct((got.shape[0], lanes), F32),
+            jax.ShapeDtypeStruct((1, 128), F32),
         ],
         compiler_params=pltpu.CompilerParams(vmem_limit_bytes=40 * MEGA),
+        cost_estimate=costs(GATHER_COST, GATHER_COST // 1000),
         name="gather",
-    )(*firsts, *seconds, got)
+    )(*firsts, *seconds)
+
+
+def gather_small(got, rows):
+    return pl.pallas_call(
+        small_kernel,
+        out_shape=[
+            jax.ShapeDtypeStruct(got.shape[1:], F32),
+            jax.ShapeDtypeStruct((got.shape[0], got.shape[2]), F32),
+        ],
+        compiler_params=pltpu.CompilerParams(vmem_limit_bytes=40 * MEGA),
+        name="gather_small",
+    )(got, rows)
 
 
 def adam_all(squares, red1, red2, small, state):
@@ -1048,10 +1063,12 @@
     flip = lambda a: a.transpose(1, 0, 2)
     if fits:
         small, far1[1:] = lax.optimization_barrier((small, far1[1:]))
+        small, near = lax.optimization_barrier((small, near))
         got = lax.all_to_all(small, ("dp", "mp"), 0, 0, tiled=True)
         own2, sends2 = line_pieces(pieces[0], near, line)
         far2 = [hop(piece, 4 * k) for piece, k in zip(sends2, (1, 2, 3))]
-        red1, red2, small_own, squares = gather([own1, *far1], [own2, *far2], got)
+        red1, red2, rows = gather([own1, *far1], [own2, *far2])
+        small_own, squares = gather_small(got, rows)
         lanes = squares.shape[1]
         squares = lax.all_to_all(squares.reshape(world, 1, lanes), ("dp", "mp"), 0, 0, tiled=True)
         state = (

time: 143 us -> 140 us (0.979)
  starting transfers between devices: 28.8 us -> 26.8 us
  local copies, waits for them, and re-layouts: 5.52 us -> 4.06 us
    all_to_all x1, waiting for transfers between devices: 0.01 us -> 4.92 us  [on_device(): got = lax.all_to_all(small, ('dp', 'mp'), 0, 0, tiled=True)]
    ppermute x12, waiting for transfers between devices: 8.46 us -> 4.2 us  [hop(): return lax.ppermute(value, 'dp', [(i, i ^ flip) for i in range(size)])]
    all_to_all x1, starting transfers between devices: 4.67 us -> 2.94 us  [on_device(): lax.all_to_all(squares.reshape(world, 1, lanes), ('dp', 'mp'), 0, 0, tile...]
    unnamed x69, local copies, waits for them, and re-layouts: 4.34 us -> 2.87 us
  transfers between devices with their start and end apart: 20 -> 20, of which waited for: 4 -> 5; matrix products, arithmetic and copies ran while one was open for 4% -> 4% of each run, Pallas kernels for 31% -> 32%
where the time goes in v6:
time: 140 us; the launch traced here: 139 us
  Pallas kernels  87.4 us (62%)
  starting transfers between devices  26.8 us (19%)
  waiting for transfers between devices  16.1 us (12%)
  local copies, waits for them, and re-layouts  4.06 us (3%)
  other arithmetic  3.78 us (3%)
    pallas_call x1, Pallas kernels, front(): pl.pallas_call(front_kernel, grid=(mols // PAIR,), out_shape=[o[0] for o...  40.6 us
    ppermute x12, starting transfers between devices, hop(): return lax.ppermute(value, 'dp', [(i, i ^ flip) for i in range(size)])  17.3 us
    pallas_call x1, Pallas kernels, middle(): pl.pallas_call(middle_own_kernel, out_shape=[dx] + [jax.ShapeDtypeStruct(...  11.7 us
    pallas_call x1, Pallas kernels, middle(): pl.pallas_call(middle_kernel, out_shape=[dx, jax.ShapeDtypeStruct(gshape,...  11.3 us
    pallas_call x1, Pallas kernels, back(): pl.pallas_call(back_kernel, grid=(mols // PAIR,), out_shape=[jax.ShapeDty...  10.7 us
    all_to_all x1, waiting for transfers between devices, on_device(): lax.all_to_all(squares.reshape(world, 1, lanes), ('dp', 'mp'), 0, 0, tile...  6.92 us
    pallas_call x1, Pallas kernels, embed(): pl.pallas_call(embed_kernel, grid=(mols // PAIR,), out_shape=[jax.ShapeDt...  6.83 us
    all_to_all x1, waiting for transfers between devices, on_device(): got = lax.all_to_all(small, ('dp', 'mp'), 0, 0, tiled=True)  4.92 us
  transfers between devices with their start and end apart: 20, of which 5 were waited for; matrix products, arithmetic and copies ran while one was open for 4% of the time, Pallas kernels for 32%

profile of v6, /device:TPU:0, one launch (start us, length us, event | category | flops | bytes accessed | tf_op | source)
XLA Modules:
  0.0 139.3 jit_solution(14386068523962126732)
XLA Ops:
  1.8 6.8 %embed.1 = (f32[768,1024]{1,0:T(8,128)}, bf16[768,1024]{1,0:T(8,128)(2,1)}, bf16[256,1024]{1,0:T(8,128)(2,1)}, bf16[768,1024]{1,0:T(8,128)(2,1)}) custom-call(bf16[8,128,768]{2,1,0:T(8,128)(2,1)} %tok_ref.1, bf16[8,128,768]{2,1,0:T(8,128)(2,1)} %cot_ref.1, s32[8,1,128]{2,1,0:T(1,128)} %bitcast.67, s32[8,2,128]{2,1,0:T(2,128)} %bitcast.66, ...), custom_call_target="tpu_custom_call" | custom-call | flops 8000000000 | bytes 10000000 | tf_op jit(solution)/shard_map/embed/pallas_call | solution.py:725
  8.7 1.3 copy-done.25
  10.1 40.6 %front.1 = (f32[768,1024]{1,0:T(8,128)}, f32[768,1024]{1,0:T(8,128)}, bf16[768,1024]{1,0:T(8,128)(2,1)}, bf16[8,1024,128]{2,1,0:T(8,128)(2,1)}, bf16[8,1024,128]...) custom-call(s32[8]{0:T(128)S(1)} %copy-done.29, ...), custom_call_target="tpu_custom_call" | custom-call | flops 60000002048 | bytes 50000000 | tf_op jit(solution)/shard_map/front/pallas_call | solution.py:775
  51.3 11.3 %middle_peer.1 = (bf16[1152,1024]{1,0:T(8,128)(2,1)}, bf16[16,48,1152]{2,1,0:T(8,128)(2,1)}) custom-call(bf16[768,1024]{1,0:T(8,128)(2,1)S(1)} %copy-done, bf16[8,1024,128]{2,1,0:T(8,128)(2,1)} %get-tuple-element.101.q_ref, bf16[8,1024,128]{2,1,0:T(8,128)(2,1)} %get-tuple-element.102.k_ref, bf16[8,1024,128]{2,1,0:T(8,128)(2,1)} %get-tuple-element.103.v_ref, ...), custom_call_target="tpu_custom_call" | custom-call | flops 200000000 | bytes 120000 | tf_op jit(solution)/shard_map/middle_peer/pallas_call | solution.py:826
  62.7 1.9 %add_convert_fusion = bf16[16,48,1152]{2,1,0:T(8,128)(2,1)S(1)} fusion(bf16[16,48,1152]{2,1,0:T(8,128)(2,1)} %collective-permute-done.4, bf16[16,48,1152]{2,1,0:T(8,128)(2,1)S(1)} %copy-done.33), kind=kLoop, calls=%fused_computation | loop fusion | flops 3538944 | bytes 5308416 | tf_op jit(solution)/shard_map/convert_element_type | solution.py:1029
  64.8 3.0 %collective-permute-start.5 = (bf16[4,48,1152]{2,1,0:T(8,128)(2,1)S(1)}, bf16[4,48,1152]{2,1,0:T(8,128)(2,1)}, u32[]{:S(2)}, u32[]{:S(2)}) collective-permute-start(bf16[4,48,1152]{2,1,0:T(8,128)(2,1)S(1)} %get-tuple-element.108), channel_id=1, source_target_pairs={{0,2},{2,0},{4,6},{6,4},{8,10},{10,8},{12,14},{14,12},{16,18},{18,... | collective-permute-start | bytes 1327112 | tf_op jit(solution)/shard_map/ppermute | solution.py:944
  67.7 1.5 %collective-permute-start.6 = (bf16[4,48,1152]{2,1,0:T(8,128)(2,1)S(1)}, bf16[4,48,1152]{2,1,0:T(8,128)(2,1)}, u32[]{:S(2)}, u32[]{:S(2)}) collective-permute-start(bf16[4,48,1152]{2,1,0:T(8,128)(2,1)S(1)} %get-tuple-element.109), channel_id=1, source_target_pairs={{0,4},{2,6},{4,0},{6,2},{8,12},{10,14},{12,8},{14,10},{16,20},{18,... | collective-permute-start | bytes 1327112 | tf_op jit(solution)/shard_map/ppermute | solution.py:944
  69.3 1.2 copy-done.32
  70.5 11.7 %middle_own.1 = (bf16[1152,1024]{1,0:T(8,128)(2,1)}, bf16[4,48,1152]{2,1,0:T(8,128)(2,1)S(1)}, bf16[4,48,1152]{2,1,0:T(8,128)(2,1)S(1)}, bf16[4,48,1152]{2,1,0:T(8,128)(2,1)S(1)}, bf16[4,48,1152]{2,1,0:T(8,128)(2,1)S(1)}) custom-call(s32[1]{0:T(128)} %bitcast.9.plane_ref, bf16[768,1024]{1,0:T(8,128)(2,1)} %get-tuple-element.97.na_ref, ...), custom_call_target="tpu_custom_call" | custom-call | flops 200000000 | bytes 120000 | tf_op jit(solution)/shard_map/middle_own/pallas_call | solution.py:836
  82.1 1.9 %collective-permute-start.11 = (bf16[4,48,1152]{2,1,0:T(8,128)(2,1)S(1)}, bf16[4,48,1152]{2,1,0:T(8,128)(2,1)S(1)}, u32[]{:S(2)}, u32[]{:S(2)}) collective-permute-start(bf16[4,48,1152]{2,1,0:T(8,128)(2,1)S(1)} %get-tuple-element.136), channel_id=1, source_target_pairs={{0,2},{2,0},{4,6},{6,4},{8,10},{10,8},{12,14},{14,12},{16,18},{18,... | collective-permute-start | bytes 1327112 | tf_op jit(solution)/shard_map/ppermute | solution.py:944
  84.1 1.5 %collective-permute-start.12 = (bf16[4,48,1152]{2,1,0:T(8,128)(2,1)S(1)}, bf16[4,48,1152]{2,1,0:T(8,128)(2,1)S(1)}, u32[]{:S(2)}, u32[]{:S(2)}) collective-permute-start(bf16[4,48,1152]{2,1,0:T(8,128)(2,1)S(1)} %get-tuple-element.137), channel_id=1, source_target_pairs={{0,4},{2,6},{4,0},{6,2},{8,12},{10,14},{12,8},{14,10},{16,20},{18,... | collective-permute-start | bytes 1327112 | tf_op jit(solution)/shard_map/ppermute | solution.py:944
  85.7 3.9 %finish_output.1 = bf16[8,128,768]{2,1,0:T(8,128)(2,1)} custom-call(f32[768,1024]{1,0:T(8,128)S(1)} %copy-done.1, bf16[768,1024]{1,0:T(8,128)(2,1)S(1)} %copy-done.2, bf16[384,768]{1,0:T(8,128)(2,1)S(1)} %copy-done.3, bf16[384,768]{1,0:T(8,128)(2,1)S(1)} %copy-done.5), custom_call_target="tpu_custom_call" | custom-call | flops 60000000 | bytes 70000 | tf_op jit(solution)/shard_map/finish_output/pallas_call | solution.py:851
  89.8 1.6 %add_convert_fusion.2 = bf16[4,48,1152]{2,1,0:T(8,128)(2,1)S(1)} fusion(bf16[4,48,1152]{2,1,0:T(8,128)(2,1)} %collective-permute-done.7, bf16[4,48,1152]{2,1,0:T(8,128)(2,1)} %collective-permute-done.6, bf16[4,48,1152]{2,1,0:T(8,128)(2,1)} %collective-permute-done.5, bf16[4,48,1152]{2,1,0:T(8,128)(2,1)S(1)} %get-tuple-element.121), kind=kLoop, calls=%fused_computation.2 | loop fusion | flops 1769472 | bytes 2211840 | tf_op jit(solution)/shard_map/convert_element_type | solution.py:955
  91.5 4.0 %collective-permute-start.10 = (bf16[48,1152]{1,0:T(8,128)(2,1)S(1)}, bf16[48,1152]{1,0:T(8,128)(2,1)S(1)}, u32[]{:S(2)}, u32[]{:S(2)}) collective-permute-start(bf16[48,1152]{1,0:T(8,128)(2,1)S(1)} %get-tuple-element.134), channel_id=1, source_target_pairs={{0,24},{2,26},{4,28},{6,30},{8,16},{10,18},{12,20},{14,22},{16,8},... | collective-permute-start | bytes 331784 | tf_op jit(solution)/shard_map/ppermute | solution.py:944
  95.6 10.7 %back.1 = (f32[8,128,768]{2,1,0:T(8,128)}, f32[32,8,128]{2,1,0:T(8,128)}) custom-call(bf16[1152,1024]{1,0:T(8,128)(2,1)S(1)} %copy-done.23, bf16[1152,1024]{1,0:T(8,128)(2,1)} %get-tuple-element.127.dxp_ref, bf16[3,768,384]{2,1,0:T(8,128)(2,1)S(1)} %bitcast.57, bf16[3,768,384]{2,1,0:T(8,128)(2,1)S(1)} %copy-done.26, f32[768,1024]{1,0:T(8,128)} %get-tuple-element.96.h0_ref, ...), custom_call_target="tpu_custom_call" | custom-call | flops 17999998976 | bytes 15000000 | tf_op jit(solution)/shard_map/back/pallas_call | solution.py:870
  107.0 1.0 collective-permute-done.12
  108.3 1.7 %collective-permute-start.15 = (bf16[48,1152]{1,0:T(8,128)(2,1)S(1)}, bf16[48,1152]{1,0:T(8,128)(2,1)S(1)}, u32[]{:S(2)}, u32[]{:S(2)}) collective-permute-start(bf16[48,1152]{1,0:T(8,128)(2,1)S(1)} %get-tuple-element.177), channel_id=1, source_target_pairs={{0,8},{2,10},{4,12},{6,14},{8,0},{10,2},{12,4},{14,6},{16,24},{18,... | collective-permute-start | bytes 331784 | tf_op jit(solution)/shard_map/ppermute | solution.py:944
  110.0 2.6 %collective-permute-start.16 = (bf16[48,1152]{1,0:T(8,128)(2,1)S(1)}, bf16[48,1152]{1,0:T(8,128)(2,1)S(1)}, u32[]{:S(2)}, u32[]{:S(2)}) collective-permute-start(bf16[48,1152]{1,0:T(8,128)(2,1)S(1)} %get-tuple-element.176), channel_id=1, source_target_pairs={{0,16},{2,18},{4,20},{6,22},{8,24},{10,26},{12,28},{14,30},{16,0},... | collective-permute-start | bytes 331784 | tf_op jit(solution)/shard_map/ppermute | solution.py:944
  113.6 4.9 %all-to-all-start = ((f32[32,8,128]{2,1,0:T(8,128)}), f32[32,8,128]{2,1,0:T(8,128)S(1)}, u32[]{:S(2)}, u32[]{:S(2)}) async-start(f32[32,8,128]{2,1,0:T(8,128)} %get-tuple-element.139), calls=%async_computation | async-start | bytes 262144 | tf_op jit(solution)/shard_map/all_to_all | solution.py:1067
  118.5 3.0 %collective-permute-done.16.refs_6_ = bf16[48,1152]{1,0:T(8,128)(2,1)S(1)} collective-permute-done((bf16[48,1152]{1,0:T(8,128)(2,1)S(1)}, bf16[48,1152]{1,0:T(8,128)(2,1)S(1)}, u32[]{:S(2)}, u32[]{:S(2)}) %collective-permute-start.16) | collective-permute-done | bytes 110624 | tf_op jit(solution)/shard_map/ppermute | solution.py:944
  121.8 4.9 %all-to-all-done.got_ref = f32[32,8,128]{2,1,0:T(8,128)S(1)} async-done(((f32[32,8,128]{2,1,0:T(8,128)}), f32[32,8,128]{2,1,0:T(8,128)S(1)}, u32[]{:S(2)}, u32[]{:S(2)}) %all-to-all-start) | async-done | bytes 131104 | tf_op jit(solution)/shard_map/all_to_all | solution.py:1067
  127.5 2.9 %all-to-all-start.1 = ((f32[32,1,128]{2,1,0:T(1,128)}), f32[32,1,128]{2,1,0:T(1,128)S(1)}, u32[]{:S(2)}, u32[]{:S(2)}) async-start(f32[32,1,128]{2,1,0:T(1,128)} %bitcast.19), calls=%async_computation.1 | async-start | bytes 32768 | tf_op jit(solution)/shard_map/all_to_all | solution.py:1073
  130.6 6.9 %all-to-all-done.1 = f32[32,1,128]{2,1,0:T(1,128)S(1)} async-done(((f32[32,1,128]{2,1,0:T(1,128)}), f32[32,1,128]{2,1,0:T(1,128)S(1)}, u32[]{:S(2)}, u32[]{:S(2)}) %all-to-all-start.1) | async-done | bytes 16416 | tf_op jit(solution)/shard_map/all_to_all | solution.py:1073
  137.7 1.5 %adam.1 = (f32[1,128]{1,0:T(1,128)}, f32[3,48,384]{2,1,0:T(8,128)}, f32[3,48,384]{2,1,0:T(8,128)}, f32[3,48,384]{2,1,0:T(8,128)}, f32[24,768]{1,0:T(8,128)}, /*i...) custom-call(f32[32,128]{1,0:T(8,128)S(1)} %bitcast.51, ...), custom_call_target="tpu_custom_call" | custom-call | tf_op jit(solution)/shard_map/adam/pallas_call | solution.py:929
  (102 shorter events, 5.6 us)
Async XLA Ops:
  0.7 8.0 %collective-permute-start = (bf16[3,768,384]{2,1,0:T(8,128)(2,1)}, bf16[3,768,384]{2,1,0:T(8,128)(2,1)S(1)}, u32[]{:S(2)}, u32[]{:S(2)}) collective-permute-start(bf16[3,768,384]{2,1,0:T(8,128)(2,1)} %bitcast.55), channel_id=1, source_target_pairs={{0,1},{1,0},{2,3},{3,2},{4,5},{5,4},{6,7},{7,6},{8,9},{9,8},{10,11... | collective-permute-start | bytes 5308424 | tf_op jit(solution)/shard_map/ppermute | solution.py:939
  1.2 7.4 %collective-permute-start.3 = (bf16[384,768]{1,0:T(8,128)(2,1)}, bf16[384,768]{1,0:T(8,128)(2,1)S(1)}, u32[]{:S(2)}, u32[]{:S(2)}) collective-permute-start(bf16[384,768]{1,0:T(8,128)(2,1)} %down_o.3), channel_id=1, source_target_pairs={{0,1},{1,0},{2,3},{3,2},{4,5},{5,4},{6,7},{7,6},{8,9},{9,8},{10,11... | collective-permute-start | bytes 1769480 | tf_op jit(solution)/shard_map/ppermute | solution.py:939
  1.3 7.4 %collective-permute-start.1 = (bf16[384,768]{1,0:T(8,128)(2,1)}, bf16[384,768]{1,0:T(8,128)(2,1)}, u32[]{:S(2)}, u32[]{:S(2)}) collective-permute-start(bf16[384,768]{1,0:T(8,128)(2,1)} %out_o.1), channel_id=1, source_target_pairs={{0,1},{1,0},{2,3},{3,2},{4,5},{5,4},{6,7},{7,6},{8,9},{9,8},{10,11... | collective-permute-start | bytes 1769480 | tf_op jit(solution)/shard_map/ppermute | solution.py:939
  1.7 7.0 %collective-permute-start.2 = (bf16[768,384]{1,0:T(8,128)(2,1)}, bf16[768,384]{1,0:T(8,128)(2,1)}, u32[]{:S(2)}, u32[]{:S(2)}) collective-permute-start(bf16[768,384]{1,0:T(8,128)(2,1)} %up_o.1), channel_id=1, source_target_pairs={{0,1},{1,0},{2,3},{3,2},{4,5},{5,4},{6,7},{7,6},{8,9},{9,8},{10,11... | collective-permute-start | bytes 1769480 | tf_op jit(solution)/shard_map/ppermute | solution.py:939
  10.1 41.2 %copy-start = (bf16[768,1024]{1,0:T(8,128)(2,1)S(1)}, bf16[768,1024]{1,0:T(8,128)(2,1)}, u32[]{:S(2)}) copy-start(bf16[768,1024]{1,0:T(8,128)(2,1)} %get-tuple-element.97.na_ref) | copy-start | bytes 4718596
  50.8 11.9 %collective-permute-start.4 = (bf16[16,48,1152]{2,1,0:T(8,128)(2,1)}, bf16[16,48,1152]{2,1,0:T(8,128)(2,1)}, u32[]{:S(2)}, u32[]{:S(2)}) collective-permute-start(bf16[16,48,1152]{2,1,0:T(8,128)(2,1)} %get-tuple-element.100), channel_id=1, source_target_pairs={{0,1},{1,0},{2,3},{3,2},{4,5},{5,4},{6,7},{7,6},{8,9},{9,8},{10,11... | collective-permute-start | bytes 5308424 | tf_op jit(solution)/shard_map/ppermute | solution.py:939
  62.6 6.7 %collective-permute-start.8 = (bf16[16,48,1152]{2,1,0:T(8,128)(2,1)}, bf16[16,48,1152]{2,1,0:T(8,128)(2,1)S(1)}, u32[]{:S(2)}, u32[]{:S(2)}) collective-permute-start(bf16[16,48,1152]{2,1,0:T(8,128)(2,1)} %get-tuple-element.113), channel_id=1, source_target_pairs={{0,1},{1,0},{2,3},{3,2},{4,5},{5,4},{6,7},{7,6},{8,9},{9,8},{10,11... | collective-permute-start | bytes 5308424 | tf_op jit(solution)/shard_map/ppermute | solution.py:939
  64.8 24.8 %collective-permute-start.5 = (bf16[4,48,1152]{2,1,0:T(8,128)(2,1)S(1)}, bf16[4,48,1152]{2,1,0:T(8,128)(2,1)}, u32[]{:S(2)}, u32[]{:S(2)}) collective-permute-start(bf16[4,48,1152]{2,1,0:T(8,128)(2,1)S(1)} %get-tuple-element.108), channel_id=1, source_target_pairs={{0,2},{2,0},{4,6},{6,4},{8,10},{10,8},{12,14},{14,12},{16,18},{18,... | collective-permute-start | bytes 1327112 | tf_op jit(solution)/shard_map/ppermute | solution.py:944
  67.7 21.9 %collective-permute-start.6 = (bf16[4,48,1152]{2,1,0:T(8,128)(2,1)S(1)}, bf16[4,48,1152]{2,1,0:T(8,128)(2,1)}, u32[]{:S(2)}, u32[]{:S(2)}) collective-permute-start(bf16[4,48,1152]{2,1,0:T(8,128)(2,1)S(1)} %get-tuple-element.109), channel_id=1, source_target_pairs={{0,4},{2,6},{4,0},{6,2},{8,12},{10,14},{12,8},{14,10},{16,20},{18,... | collective-permute-start | bytes 1327112 | tf_op jit(solution)/shard_map/ppermute | solution.py:944
  69.3 20.6 %collective-permute-start.7 = (bf16[4,48,1152]{2,1,0:T(8,128)(2,1)S(1)}, bf16[4,48,1152]{2,1,0:T(8,128)(2,1)}, u32[]{:S(2)}, u32[]{:S(2)}) collective-permute-start(bf16[4,48,1152]{2,1,0:T(8,128)(2,1)S(1)} %get-tuple-element.110), channel_id=1, source_target_pairs={{0,6},{2,4},{4,2},{6,0},{8,14},{10,12},{12,10},{14,8},{16,22},{18,... | collective-permute-start | bytes 1327112 | tf_op jit(solution)/shard_map/ppermute | solution.py:944
  82.1 24.9 %collective-permute-start.11 = (bf16[4,48,1152]{2,1,0:T(8,128)(2,1)S(1)}, bf16[4,48,1152]{2,1,0:T(8,128)(2,1)S(1)}, u32[]{:S(2)}, u32[]{:S(2)}) collective-permute-start(bf16[4,48,1152]{2,1,0:T(8,128)(2,1)S(1)} %get-tuple-element.136), channel_id=1, source_target_pairs={{0,2},{2,0},{4,6},{6,4},{8,10},{10,8},{12,14},{14,12},{16,18},{18,... | collective-permute-start | bytes 1327112 | tf_op jit(solution)/shard_map/ppermute | solution.py:944
  84.1 24.0 %collective-permute-start.12 = (bf16[4,48,1152]{2,1,0:T(8,128)(2,1)S(1)}, bf16[4,48,1152]{2,1,0:T(8,128)(2,1)S(1)}, u32[]{:S(2)}, u32[]{:S(2)}) collective-permute-start(bf16[4,48,1152]{2,1,0:T(8,128)(2,1)S(1)} %get-tuple-element.137), channel_id=1, source_target_pairs={{0,4},{2,6},{4,0},{6,2},{8,12},{10,14},{12,8},{14,10},{16,20},{18,... | collective-permute-start | bytes 1327112 | tf_op jit(solution)/shard_map/ppermute | solution.py:944
  89.6 18.5 %collective-permute-start.13 = (bf16[4,48,1152]{2,1,0:T(8,128)(2,1)S(1)}, bf16[4,48,1152]{2,1,0:T(8,128)(2,1)S(1)}, u32[]{:S(2)}, u32[]{:S(2)}) collective-permute-start(bf16[4,48,1152]{2,1,0:T(8,128)(2,1)S(1)} %get-tuple-element.138), channel_id=1, source_target_pairs={{0,6},{2,4},{4,2},{6,0},{8,14},{10,12},{12,10},{14,8},{16,22},{18,... | collective-permute-start | bytes 1327112 | tf_op jit(solution)/shard_map/ppermute | solution.py:944
  91.5 14.8 %collective-permute-start.10 = (bf16[48,1152]{1,0:T(8,128)(2,1)S(1)}, bf16[48,1152]{1,0:T(8,128)(2,1)S(1)}, u32[]{:S(2)}, u32[]{:S(2)}) collective-permute-start(bf16[48,1152]{1,0:T(8,128)(2,1)S(1)} %get-tuple-element.134), channel_id=1, source_target_pairs={{0,24},{2,26},{4,28},{6,30},{8,16},{10,18},{12,20},{14,22},{16,8},... | collective-permute-start | bytes 331784 | tf_op jit(solution)/shard_map/ppermute | solution.py:944
  95.6 11.4 %collective-permute-start.9 = (bf16[48,1152]{1,0:T(8,128)(2,1)S(1)}, bf16[48,1152]{1,0:T(8,128)(2,1)S(1)}, u32[]{:S(2)}, u32[]{:S(2)}) collective-permute-start(bf16[48,1152]{1,0:T(8,128)(2,1)S(1)} %get-tuple-element.133), channel_id=1, source_target_pairs={{0,16},{2,18},{4,20},{6,22},{8,24},{10,26},{12,28},{14,30},{16,0},... | collective-permute-start | bytes 331784 | tf_op jit(solution)/shard_map/ppermute | solution.py:944
  106.3 12.2 %collective-permute-start.14 = (bf16[48,1152]{1,0:T(8,128)(2,1)S(1)}, bf16[48,1152]{1,0:T(8,128)(2,1)S(1)}, u32[]{:S(2)}, u32[]{:S(2)}) collective-permute-start(bf16[48,1152]{1,0:T(8,128)(2,1)S(1)} %get-tuple-element.140), channel_id=1, source_target_pairs={{0,8},{2,10},{4,12},{6,14},{8,0},{10,2},{12,4},{14,6},{16,24},{18,... | collective-permute-start | bytes 331784 | tf_op jit(solution)/shard_map/ppermute | solution.py:944
  108.3 10.2 %collective-permute-start.15 = (bf16[48,1152]{1,0:T(8,128)(2,1)S(1)}, bf16[48,1152]{1,0:T(8,128)(2,1)S(1)}, u32[]{:S(2)}, u32[]{:S(2)}) collective-permute-start(bf16[48,1152]{1,0:T(8,128)(2,1)S(1)} %get-tuple-element.177), channel_id=1, source_target_pairs={{0,8},{2,10},{4,12},{6,14},{8,0},{10,2},{12,4},{14,6},{16,24},{18,... | collective-permute-start | bytes 331784 | tf_op jit(solution)/shard_map/ppermute | solution.py:944
  110.0 11.5 %collective-permute-start.16 = (bf16[48,1152]{1,0:T(8,128)(2,1)S(1)}, bf16[48,1152]{1,0:T(8,128)(2,1)S(1)}, u32[]{:S(2)}, u32[]{:S(2)}) collective-permute-start(bf16[48,1152]{1,0:T(8,128)(2,1)S(1)} %get-tuple-element.176), channel_id=1, source_target_pairs={{0,16},{2,18},{4,20},{6,22},{8,24},{10,26},{12,28},{14,30},{16,0},... | collective-permute-start | bytes 331784 | tf_op jit(solution)/shard_map/ppermute | solution.py:944
  112.6 8.9 %collective-permute-start.17 = (bf16[48,1152]{1,0:T(8,128)(2,1)S(1)}, bf16[48,1152]{1,0:T(8,128)(2,1)S(1)}, u32[]{:S(2)}, u32[]{:S(2)}) collective-permute-start(bf16[48,1152]{1,0:T(8,128)(2,1)S(1)} %get-tuple-element.175), channel_id=1, source_target_pairs={{0,24},{2,26},{4,28},{6,30},{8,16},{10,18},{12,20},{14,22},{16,8},... | collective-permute-start | bytes 331784 | tf_op jit(solution)/shard_map/ppermute | solution.py:944
  113.6 13.1 %all-to-all-start = ((f32[32,8,128]{2,1,0:T(8,128)}), f32[32,8,128]{2,1,0:T(8,128)S(1)}, u32[]{:S(2)}, u32[]{:S(2)}) async-start(f32[32,8,128]{2,1,0:T(8,128)} %get-tuple-element.139), calls=%async_computation | async-start | bytes 262144 | tf_op jit(solution)/shard_map/all_to_all | solution.py:1067
  121.5 16.0 %copy-start.6 = (f32[48,3,384]{2,0,1:T(8,128)S(1)}, f32[48,3,384]{2,0,1:T(8,128)}, u32[]{:S(2)}) copy-start(f32[48,3,384]{2,0,1:T(8,128)} %param.38) | copy-start | bytes 663556
  121.5 16.0 %copy-start.7 = (f32[48,3,384]{2,0,1:T(8,128)S(1)}, f32[48,3,384]{2,0,1:T(8,128)}, u32[]{:S(2)}) copy-start(f32[48,3,384]{2,0,1:T(8,128)} %param.39) | copy-start | bytes 663556
  121.5 16.0 %copy-start.8 = (f32[48,3,384]{2,0,1:T(8,128)S(1)}, f32[48,3,384]{2,0,1:T(8,128)}, u32[]{:S(2)}) copy-start(f32[48,3,384]{2,0,1:T(8,128)} %param.40) | copy-start | bytes 663556
  127.5 10.0 %all-to-all-start.1 = ((f32[32,1,128]{2,1,0:T(1,128)}), f32[32,1,128]{2,1,0:T(1,128)S(1)}, u32[]{:S(2)}, u32[]{:S(2)}) async-start(f32[32,1,128]{2,1,0:T(1,128)} %bitcast.19), calls=%async_computation.1 | async-start | bytes 32768 | tf_op jit(solution)/shard_map/all_to_all | solution.py:1073
  (30 other events, 359.5 us)

commit v7 on v6

--- a/solution.py
+++ b/solution.py
@@ -29,7 +29,7 @@
 PAIR = 2
 MEGA = 1024 * 1024
 GATHER_COST = 3000000000
-FRONT_UNROLL = 8
+FRONT_UNROLL = 16
 MIDDLE_UNROLL = 8
 
 F32 = jnp.float32

time: 140 us -> 138 us (0.986)
  Pallas kernels: 87.4 us -> 85.9 us
    pallas_call x1, Pallas kernels: 40.6 us -> 39.2 us  [front(): pl.pallas_call(front_kernel, grid=(mols // PAIR,), out_shape=[o[0] for o...]
where the time goes in v7:
time: 138 us
  Pallas kernels  85.9 us (62%)
  starting transfers between devices  26.8 us (19%)
  waiting for transfers between devices  16.1 us (12%)
  local copies, waits for them, and re-layouts  4.06 us (3%)
  other arithmetic  3.78 us (3%)
    pallas_call x1, Pallas kernels, front(): pl.pallas_call(front_kernel, grid=(mols // PAIR,), out_shape=[o[0] for o...  39.2 us
    ppermute x12, starting transfers between devices, hop(): return lax.ppermute(value, 'dp', [(i, i ^ flip) for i in range(size)])  17.2 us
    pallas_call x1, Pallas kernels, middle(): pl.pallas_call(middle_own_kernel, out_shape=[dx] + [jax.ShapeDtypeStruct(...  11.6 us
    pallas_call x1, Pallas kernels, middle(): pl.pallas_call(middle_kernel, out_shape=[dx, jax.ShapeDtypeStruct(gshape,...  11.3 us
    pallas_call x1, Pallas kernels, back(): pl.pallas_call(back_kernel, grid=(mols // PAIR,), out_shape=[jax.ShapeDty...  10.7 us
    all_to_all x1, waiting for transfers between devices, on_device(): lax.all_to_all(squares.reshape(world, 1, lanes), ('dp', 'mp'), 0, 0, tile...  6.92 us
    pallas_call x1, Pallas kernels, embed(): pl.pallas_call(embed_kernel, grid=(mols // PAIR,), out_shape=[jax.ShapeDt...  6.83 us
    all_to_all x1, waiting for transfers between devices, on_device(): got = lax.all_to_all(small, ('dp', 'mp'), 0, 0, tiled=True)  4.92 us
  transfers between devices with their start and end apart: 20, of which 5 were waited for; matrix products, arithmetic and copies ran while one was open for 4% of the time, Pallas kernels for 32%

profile of v7, /device:TPU:0, one launch (start us, length us, event | category | flops | bytes accessed | tf_op | source)
XLA Modules:
  0.0 137.8 jit_solution(13924335514155198313)
XLA Ops:
  1.8 6.8 %embed.1 = (f32[768,1024]{1,0:T(8,128)}, bf16[768,1024]{1,0:T(8,128)(2,1)}, bf16[256,1024]{1,0:T(8,128)(2,1)}, bf16[768,1024]{1,0:T(8,128)(2,1)}) custom-call(bf16[8,128,768]{2,1,0:T(8,128)(2,1)} %tok_ref.1, bf16[8,128,768]{2,1,0:T(8,128)(2,1)} %cot_ref.1, s32[8,1,128]{2,1,0:T(1,128)} %bitcast.67, s32[8,2,128]{2,1,0:T(2,128)} %bitcast.66, ...), custom_call_target="tpu_custom_call" | custom-call | flops 8000000000 | bytes 10000000 | tf_op jit(solution)/shard_map/embed/pallas_call | solution.py:725
  8.7 1.3 copy-done.25
  10.1 39.2 %front.1 = (f32[768,1024]{1,0:T(8,128)}, f32[768,1024]{1,0:T(8,128)}, bf16[768,1024]{1,0:T(8,128)(2,1)}, bf16[8,1024,128]{2,1,0:T(8,128)(2,1)}, bf16[8,1024,128]...) custom-call(s32[8]{0:T(128)S(1)} %copy-done.29, ...), custom_call_target="tpu_custom_call" | custom-call | flops 60000002048 | bytes 50000000 | tf_op jit(solution)/shard_map/front/pallas_call | solution.py:775
  49.8 11.3 %middle_peer.1 = (bf16[1152,1024]{1,0:T(8,128)(2,1)}, bf16[16,48,1152]{2,1,0:T(8,128)(2,1)}) custom-call(bf16[768,1024]{1,0:T(8,128)(2,1)S(1)} %copy-done, bf16[8,1024,128]{2,1,0:T(8,128)(2,1)} %get-tuple-element.101.q_ref, bf16[8,1024,128]{2,1,0:T(8,128)(2,1)} %get-tuple-element.102.k_ref, bf16[8,1024,128]{2,1,0:T(8,128)(2,1)} %get-tuple-element.103.v_ref, ...), custom_call_target="tpu_custom_call" | custom-call | flops 200000000 | bytes 120000 | tf_op jit(solution)/shard_map/middle_peer/pallas_call | solution.py:826
  61.2 1.9 %add_convert_fusion = bf16[16,48,1152]{2,1,0:T(8,128)(2,1)S(1)} fusion(bf16[16,48,1152]{2,1,0:T(8,128)(2,1)} %collective-permute-done.4, bf16[16,48,1152]{2,1,0:T(8,128)(2,1)S(1)} %copy-done.33), kind=kLoop, calls=%fused_computation | loop fusion | flops 3538944 | bytes 5308416 | tf_op jit(solution)/shard_map/convert_element_type | solution.py:1029
  63.3 3.0 %collective-permute-start.5 = (bf16[4,48,1152]{2,1,0:T(8,128)(2,1)S(1)}, bf16[4,48,1152]{2,1,0:T(8,128)(2,1)}, u32[]{:S(2)}, u32[]{:S(2)}) collective-permute-start(bf16[4,48,1152]{2,1,0:T(8,128)(2,1)S(1)} %get-tuple-element.108), channel_id=1, source_target_pairs={{0,2},{2,0},{4,6},{6,4},{8,10},{10,8},{12,14},{14,12},{16,18},{18,... | collective-permute-start | bytes 1327112 | tf_op jit(solution)/shard_map/ppermute | solution.py:944
  66.3 1.5 %collective-permute-start.6 = (bf16[4,48,1152]{2,1,0:T(8,128)(2,1)S(1)}, bf16[4,48,1152]{2,1,0:T(8,128)(2,1)}, u32[]{:S(2)}, u32[]{:S(2)}) collective-permute-start(bf16[4,48,1152]{2,1,0:T(8,128)(2,1)S(1)} %get-tuple-element.109), channel_id=1, source_target_pairs={{0,4},{2,6},{4,0},{6,2},{8,12},{10,14},{12,8},{14,10},{16,20},{18,... | collective-permute-start | bytes 1327112 | tf_op jit(solution)/shard_map/ppermute | solution.py:944
  67.8 1.2 copy-done.32
  69.0 11.6 %middle_own.1 = (bf16[1152,1024]{1,0:T(8,128)(2,1)}, bf16[4,48,1152]{2,1,0:T(8,128)(2,1)S(1)}, bf16[4,48,1152]{2,1,0:T(8,128)(2,1)S(1)}, bf16[4,48,1152]{2,1,0:T(8,128)(2,1)S(1)}, bf16[4,48,1152]{2,1,0:T(8,128)(2,1)S(1)}) custom-call(s32[1]{0:T(128)} %bitcast.9.plane_ref, bf16[768,1024]{1,0:T(8,128)(2,1)} %get-tuple-element.97.na_ref, ...), custom_call_target="tpu_custom_call" | custom-call | flops 200000000 | bytes 120000 | tf_op jit(solution)/shard_map/middle_own/pallas_call | solution.py:836
  80.7 1.9 %collective-permute-start.11 = (bf16[4,48,1152]{2,1,0:T(8,128)(2,1)S(1)}, bf16[4,48,1152]{2,1,0:T(8,128)(2,1)S(1)}, u32[]{:S(2)}, u32[]{:S(2)}) collective-permute-start(bf16[4,48,1152]{2,1,0:T(8,128)(2,1)S(1)} %get-tuple-element.136), channel_id=1, source_target_pairs={{0,2},{2,0},{4,6},{6,4},{8,10},{10,8},{12,14},{14,12},{16,18},{18,... | collective-permute-start | bytes 1327112 | tf_op jit(solution)/shard_map/ppermute | solution.py:944
  82.6 1.5 %collective-permute-start.12 = (bf16[4,48,1152]{2,1,0:T(8,128)(2,1)S(1)}, bf16[4,48,1152]{2,1,0:T(8,128)(2,1)S(1)}, u32[]{:S(2)}, u32[]{:S(2)}) collective-permute-start(bf16[4,48,1152]{2,1,0:T(8,128)(2,1)S(1)} %get-tuple-element.137), channel_id=1, source_target_pairs={{0,4},{2,6},{4,0},{6,2},{8,12},{10,14},{12,8},{14,10},{16,20},{18,... | collective-permute-start | bytes 1327112 | tf_op jit(solution)/shard_map/ppermute | solution.py:944
  84.2 3.9 %finish_output.1 = bf16[8,128,768]{2,1,0:T(8,128)(2,1)} custom-call(f32[768,1024]{1,0:T(8,128)S(1)} %copy-done.1, bf16[768,1024]{1,0:T(8,128)(2,1)S(1)} %copy-done.2, bf16[384,768]{1,0:T(8,128)(2,1)S(1)} %copy-done.3, bf16[384,768]{1,0:T(8,128)(2,1)S(1)} %copy-done.5), custom_call_target="tpu_custom_call" | custom-call | flops 60000000 | bytes 70000 | tf_op jit(solution)/shard_map/finish_output/pallas_call | solution.py:851
  88.4 1.6 %add_convert_fusion.2 = bf16[4,48,1152]{2,1,0:T(8,128)(2,1)S(1)} fusion(bf16[4,48,1152]{2,1,0:T(8,128)(2,1)} %collective-permute-done.7, bf16[4,48,1152]{2,1,0:T(8,128)(2,1)} %collective-permute-done.6, bf16[4,48,1152]{2,1,0:T(8,128)(2,1)} %collective-permute-done.5, bf16[4,48,1152]{2,1,0:T(8,128)(2,1)S(1)} %get-tuple-element.121), kind=kLoop, calls=%fused_computation.2 | loop fusion | flops 1769472 | bytes 2211840 | tf_op jit(solution)/shard_map/convert_element_type | solution.py:955
  90.1 4.0 %collective-permute-start.10 = (bf16[48,1152]{1,0:T(8,128)(2,1)S(1)}, bf16[48,1152]{1,0:T(8,128)(2,1)S(1)}, u32[]{:S(2)}, u32[]{:S(2)}) collective-permute-start(bf16[48,1152]{1,0:T(8,128)(2,1)S(1)} %get-tuple-element.134), channel_id=1, source_target_pairs={{0,24},{2,26},{4,28},{6,30},{8,16},{10,18},{12,20},{14,22},{16,8},... | collective-permute-start | bytes 331784 | tf_op jit(solution)/shard_map/ppermute | solution.py:944
  94.2 10.7 %back.1 = (f32[8,128,768]{2,1,0:T(8,128)}, f32[32,8,128]{2,1,0:T(8,128)}) custom-call(bf16[1152,1024]{1,0:T(8,128)(2,1)S(1)} %copy-done.23, bf16[1152,1024]{1,0:T(8,128)(2,1)} %get-tuple-element.127.dxp_ref, bf16[3,768,384]{2,1,0:T(8,128)(2,1)S(1)} %bitcast.57, bf16[3,768,384]{2,1,0:T(8,128)(2,1)S(1)} %copy-done.26, f32[768,1024]{1,0:T(8,128)} %get-tuple-element.96.h0_ref, ...), custom_call_target="tpu_custom_call" | custom-call | flops 17999998976 | bytes 15000000 | tf_op jit(solution)/shard_map/back/pallas_call | solution.py:870
  105.5 1.0 collective-permute-done.12
  106.9 1.6 %collective-permute-start.15 = (bf16[48,1152]{1,0:T(8,128)(2,1)S(1)}, bf16[48,1152]{1,0:T(8,128)(2,1)S(1)}, u32[]{:S(2)}, u32[]{:S(2)}) collective-permute-start(bf16[48,1152]{1,0:T(8,128)(2,1)S(1)} %get-tuple-element.177), channel_id=1, source_target_pairs={{0,8},{2,10},{4,12},{6,14},{8,0},{10,2},{12,4},{14,6},{16,24},{18,... | collective-permute-start | bytes 331784 | tf_op jit(solution)/shard_map/ppermute | solution.py:944
  108.5 2.6 %collective-permute-start.16 = (bf16[48,1152]{1,0:T(8,128)(2,1)S(1)}, bf16[48,1152]{1,0:T(8,128)(2,1)S(1)}, u32[]{:S(2)}, u32[]{:S(2)}) collective-permute-start(bf16[48,1152]{1,0:T(8,128)(2,1)S(1)} %get-tuple-element.176), channel_id=1, source_target_pairs={{0,16},{2,18},{4,20},{6,22},{8,24},{10,26},{12,28},{14,30},{16,0},... | collective-permute-start | bytes 331784 | tf_op jit(solution)/shard_map/ppermute | solution.py:944
  112.2 4.9 %all-to-all-start = ((f32[32,8,128]{2,1,0:T(8,128)}), f32[32,8,128]{2,1,0:T(8,128)S(1)}, u32[]{:S(2)}, u32[]{:S(2)}) async-start(f32[32,8,128]{2,1,0:T(8,128)} %get-tuple-element.139), calls=%async_computation | async-start | bytes 262144 | tf_op jit(solution)/shard_map/all_to_all | solution.py:1067
  117.1 3.0 %collective-permute-done.16.refs_6_ = bf16[48,1152]{1,0:T(8,128)(2,1)S(1)} collective-permute-done((bf16[48,1152]{1,0:T(8,128)(2,1)S(1)}, bf16[48,1152]{1,0:T(8,128)(2,1)S(1)}, u32[]{:S(2)}, u32[]{:S(2)}) %collective-permute-start.16) | collective-permute-done | bytes 110624 | tf_op jit(solution)/shard_map/ppermute | solution.py:944
  120.4 4.9 %all-to-all-done.got_ref = f32[32,8,128]{2,1,0:T(8,128)S(1)} async-done(((f32[32,8,128]{2,1,0:T(8,128)}), f32[32,8,128]{2,1,0:T(8,128)S(1)}, u32[]{:S(2)}, u32[]{:S(2)}) %all-to-all-start) | async-done | bytes 131104 | tf_op jit(solution)/shard_map/all_to_all | solution.py:1067
  126.1 2.9 %all-to-all-start.1 = ((f32[32,1,128]{2,1,0:T(1,128)}), f32[32,1,128]{2,1,0:T(1,128)S(1)}, u32[]{:S(2)}, u32[]{:S(2)}) async-start(f32[32,1,128]{2,1,0:T(1,128)} %bitcast.19), calls=%async_computation.1 | async-start | bytes 32768 | tf_op jit(solution)/shard_map/all_to_all | solution.py:1073
  129.2 6.9 %all-to-all-done.1 = f32[32,1,128]{2,1,0:T(1,128)S(1)} async-done(((f32[32,1,128]{2,1,0:T(1,128)}), f32[32,1,128]{2,1,0:T(1,128)S(1)}, u32[]{:S(2)}, u32[]{:S(2)}) %all-to-all-start.1) | async-done | bytes 16416 | tf_op jit(solution)/shard_map/all_to_all | solution.py:1073
  136.2 1.5 %adam.1 = (f32[1,128]{1,0:T(1,128)}, f32[3,48,384]{2,1,0:T(8,128)}, f32[3,48,384]{2,1,0:T(8,128)}, f32[3,48,384]{2,1,0:T(8,128)}, f32[24,768]{1,0:T(8,128)}, /*i...) custom-call(f32[32,128]{1,0:T(8,128)S(1)} %bitcast.51, ...), custom_call_target="tpu_custom_call" | custom-call | tf_op jit(solution)/shard_map/adam/pallas_call | solution.py:929
  (102 shorter events, 5.6 us)
Async XLA Ops:
  0.7 8.0 %collective-permute-start = (bf16[3,768,384]{2,1,0:T(8,128)(2,1)}, bf16[3,768,384]{2,1,0:T(8,128)(2,1)S(1)}, u32[]{:S(2)}, u32[]{:S(2)}) collective-permute-start(bf16[3,768,384]{2,1,0:T(8,128)(2,1)} %bitcast.55), channel_id=1, source_target_pairs={{0,1},{1,0},{2,3},{3,2},{4,5},{5,4},{6,7},{7,6},{8,9},{9,8},{10,11... | collective-permute-start | bytes 5308424 | tf_op jit(solution)/shard_map/ppermute | solution.py:939
  1.2 7.4 %collective-permute-start.3 = (bf16[384,768]{1,0:T(8,128)(2,1)}, bf16[384,768]{1,0:T(8,128)(2,1)S(1)}, u32[]{:S(2)}, u32[]{:S(2)}) collective-permute-start(bf16[384,768]{1,0:T(8,128)(2,1)} %down_o.3), channel_id=1, source_target_pairs={{0,1},{1,0},{2,3},{3,2},{4,5},{5,4},{6,7},{7,6},{8,9},{9,8},{10,11... | collective-permute-start | bytes 1769480 | tf_op jit(solution)/shard_map/ppermute | solution.py:939
  1.3 7.4 %collective-permute-start.1 = (bf16[384,768]{1,0:T(8,128)(2,1)}, bf16[384,768]{1,0:T(8,128)(2,1)}, u32[]{:S(2)}, u32[]{:S(2)}) collective-permute-start(bf16[384,768]{1,0:T(8,128)(2,1)} %out_o.1), channel_id=1, source_target_pairs={{0,1},{1,0},{2,3},{3,2},{4,5},{5,4},{6,7},{7,6},{8,9},{9,8},{10,11... | collective-permute-start | bytes 1769480 | tf_op jit(solution)/shard_map/ppermute | solution.py:939
  1.7 7.0 %collective-permute-start.2 = (bf16[768,384]{1,0:T(8,128)(2,1)}, bf16[768,384]{1,0:T(8,128)(2,1)}, u32[]{:S(2)}, u32[]{:S(2)}) collective-permute-start(bf16[768,384]{1,0:T(8,128)(2,1)} %up_o.1), channel_id=1, source_target_pairs={{0,1},{1,0},{2,3},{3,2},{4,5},{5,4},{6,7},{7,6},{8,9},{9,8},{10,11... | collective-permute-start | bytes 1769480 | tf_op jit(solution)/shard_map/ppermute | solution.py:939
  10.1 39.7 %copy-start = (bf16[768,1024]{1,0:T(8,128)(2,1)S(1)}, bf16[768,1024]{1,0:T(8,128)(2,1)}, u32[]{:S(2)}) copy-start(bf16[768,1024]{1,0:T(8,128)(2,1)} %get-tuple-element.97.na_ref) | copy-start | bytes 4718596
  49.3 11.9 %collective-permute-start.4 = (bf16[16,48,1152]{2,1,0:T(8,128)(2,1)}, bf16[16,48,1152]{2,1,0:T(8,128)(2,1)}, u32[]{:S(2)}, u32[]{:S(2)}) collective-permute-start(bf16[16,48,1152]{2,1,0:T(8,128)(2,1)} %get-tuple-element.100), channel_id=1, source_target_pairs={{0,1},{1,0},{2,3},{3,2},{4,5},{5,4},{6,7},{7,6},{8,9},{9,8},{10,11... | collective-permute-start | bytes 5308424 | tf_op jit(solution)/shard_map/ppermute | solution.py:939
  61.1 6.7 %collective-permute-start.8 = (bf16[16,48,1152]{2,1,0:T(8,128)(2,1)}, bf16[16,48,1152]{2,1,0:T(8,128)(2,1)S(1)}, u32[]{:S(2)}, u32[]{:S(2)}) collective-permute-start(bf16[16,48,1152]{2,1,0:T(8,128)(2,1)} %get-tuple-element.113), channel_id=1, source_target_pairs={{0,1},{1,0},{2,3},{3,2},{4,5},{5,4},{6,7},{7,6},{8,9},{9,8},{10,11... | collective-permute-start | bytes 5308424 | tf_op jit(solution)/shard_map/ppermute | solution.py:939
  63.3 24.8 %collective-permute-start.5 = (bf16[4,48,1152]{2,1,0:T(8,128)(2,1)S(1)}, bf16[4,48,1152]{2,1,0:T(8,128)(2,1)}, u32[]{:S(2)}, u32[]{:S(2)}) collective-permute-start(bf16[4,48,1152]{2,1,0:T(8,128)(2,1)S(1)} %get-tuple-element.108), channel_id=1, source_target_pairs={{0,2},{2,0},{4,6},{6,4},{8,10},{10,8},{12,14},{14,12},{16,18},{18,... | collective-permute-start | bytes 1327112 | tf_op jit(solution)/shard_map/ppermute | solution.py:944
  66.3 21.9 %collective-permute-start.6 = (bf16[4,48,1152]{2,1,0:T(8,128)(2,1)S(1)}, bf16[4,48,1152]{2,1,0:T(8,128)(2,1)}, u32[]{:S(2)}, u32[]{:S(2)}) collective-permute-start(bf16[4,48,1152]{2,1,0:T(8,128)(2,1)S(1)} %get-tuple-element.109), channel_id=1, source_target_pairs={{0,4},{2,6},{4,0},{6,2},{8,12},{10,14},{12,8},{14,10},{16,20},{18,... | collective-permute-start | bytes 1327112 | tf_op jit(solution)/shard_map/ppermute | solution.py:944
  67.8 20.6 %collective-permute-start.7 = (bf16[4,48,1152]{2,1,0:T(8,128)(2,1)S(1)}, bf16[4,48,1152]{2,1,0:T(8,128)(2,1)}, u32[]{:S(2)}, u32[]{:S(2)}) collective-permute-start(bf16[4,48,1152]{2,1,0:T(8,128)(2,1)S(1)} %get-tuple-element.110), channel_id=1, source_target_pairs={{0,6},{2,4},{4,2},{6,0},{8,14},{10,12},{12,10},{14,8},{16,22},{18,... | collective-permute-start | bytes 1327112 | tf_op jit(solution)/shard_map/ppermute | solution.py:944
  80.7 24.9 %collective-permute-start.11 = (bf16[4,48,1152]{2,1,0:T(8,128)(2,1)S(1)}, bf16[4,48,1152]{2,1,0:T(8,128)(2,1)S(1)}, u32[]{:S(2)}, u32[]{:S(2)}) collective-permute-start(bf16[4,48,1152]{2,1,0:T(8,128)(2,1)S(1)} %get-tuple-element.136), channel_id=1, source_target_pairs={{0,2},{2,0},{4,6},{6,4},{8,10},{10,8},{12,14},{14,12},{16,18},{18,... | collective-permute-start | bytes 1327112 | tf_op jit(solution)/shard_map/ppermute | solution.py:944
  82.6 24.0 %collective-permute-start.12 = (bf16[4,48,1152]{2,1,0:T(8,128)(2,1)S(1)}, bf16[4,48,1152]{2,1,0:T(8,128)(2,1)S(1)}, u32[]{:S(2)}, u32[]{:S(2)}) collective-permute-start(bf16[4,48,1152]{2,1,0:T(8,128)(2,1)S(1)} %get-tuple-element.137), channel_id=1, source_target_pairs={{0,4},{2,6},{4,0},{6,2},{8,12},{10,14},{12,8},{14,10},{16,20},{18,... | collective-permute-start | bytes 1327112 | tf_op jit(solution)/shard_map/ppermute | solution.py:944
  88.1 18.5 %collective-permute-start.13 = (bf16[4,48,1152]{2,1,0:T(8,128)(2,1)S(1)}, bf16[4,48,1152]{2,1,0:T(8,128)(2,1)S(1)}, u32[]{:S(2)}, u32[]{:S(2)}) collective-permute-start(bf16[4,48,1152]{2,1,0:T(8,128)(2,1)S(1)} %get-tuple-element.138), channel_id=1, source_target_pairs={{0,6},{2,4},{4,2},{6,0},{8,14},{10,12},{12,10},{14,8},{16,22},{18,... | collective-permute-start | bytes 1327112 | tf_op jit(solution)/shard_map/ppermute | solution.py:944
  90.1 14.7 %collective-permute-start.10 = (bf16[48,1152]{1,0:T(8,128)(2,1)S(1)}, bf16[48,1152]{1,0:T(8,128)(2,1)S(1)}, u32[]{:S(2)}, u32[]{:S(2)}) collective-permute-start(bf16[48,1152]{1,0:T(8,128)(2,1)S(1)} %get-tuple-element.134), channel_id=1, source_target_pairs={{0,24},{2,26},{4,28},{6,30},{8,16},{10,18},{12,20},{14,22},{16,8},... | collective-permute-start | bytes 331784 | tf_op jit(solution)/shard_map/ppermute | solution.py:944
  94.1 11.4 %collective-permute-start.9 = (bf16[48,1152]{1,0:T(8,128)(2,1)S(1)}, bf16[48,1152]{1,0:T(8,128)(2,1)S(1)}, u32[]{:S(2)}, u32[]{:S(2)}) collective-permute-start(bf16[48,1152]{1,0:T(8,128)(2,1)S(1)} %get-tuple-element.133), channel_id=1, source_target_pairs={{0,16},{2,18},{4,20},{6,22},{8,24},{10,26},{12,28},{14,30},{16,0},... | collective-permute-start | bytes 331784 | tf_op jit(solution)/shard_map/ppermute | solution.py:944
  104.9 12.2 %collective-permute-start.14 = (bf16[48,1152]{1,0:T(8,128)(2,1)S(1)}, bf16[48,1152]{1,0:T(8,128)(2,1)S(1)}, u32[]{:S(2)}, u32[]{:S(2)}) collective-permute-start(bf16[48,1152]{1,0:T(8,128)(2,1)S(1)} %get-tuple-element.140), channel_id=1, source_target_pairs={{0,8},{2,10},{4,12},{6,14},{8,0},{10,2},{12,4},{14,6},{16,24},{18,... | collective-permute-start | bytes 331784 | tf_op jit(solution)/shard_map/ppermute | solution.py:944
  106.9 10.2 %collective-permute-start.15 = (bf16[48,1152]{1,0:T(8,128)(2,1)S(1)}, bf16[48,1152]{1,0:T(8,128)(2,1)S(1)}, u32[]{:S(2)}, u32[]{:S(2)}) collective-permute-start(bf16[48,1152]{1,0:T(8,128)(2,1)S(1)} %get-tuple-element.177), channel_id=1, source_target_pairs={{0,8},{2,10},{4,12},{6,14},{8,0},{10,2},{12,4},{14,6},{16,24},{18,... | collective-permute-start | bytes 331784 | tf_op jit(solution)/shard_map/ppermute | solution.py:944
  108.5 11.5 %collective-permute-start.16 = (bf16[48,1152]{1,0:T(8,128)(2,1)S(1)}, bf16[48,1152]{1,0:T(8,128)(2,1)S(1)}, u32[]{:S(2)}, u32[]{:S(2)}) collective-permute-start(bf16[48,1152]{1,0:T(8,128)(2,1)S(1)} %get-tuple-element.176), channel_id=1, source_target_pairs={{0,16},{2,18},{4,20},{6,22},{8,24},{10,26},{12,28},{14,30},{16,0},... | collective-permute-start | bytes 331784 | tf_op jit(solution)/shard_map/ppermute | solution.py:944
  111.1 9.0 %collective-permute-start.17 = (bf16[48,1152]{1,0:T(8,128)(2,1)S(1)}, bf16[48,1152]{1,0:T(8,128)(2,1)S(1)}, u32[]{:S(2)}, u32[]{:S(2)}) collective-permute-start(bf16[48,1152]{1,0:T(8,128)(2,1)S(1)} %get-tuple-element.175), channel_id=1, source_target_pairs={{0,24},{2,26},{4,28},{6,30},{8,16},{10,18},{12,20},{14,22},{16,8},... | collective-permute-start | bytes 331784 | tf_op jit(solution)/shard_map/ppermute | solution.py:944
  112.2 13.1 %all-to-all-start = ((f32[32,8,128]{2,1,0:T(8,128)}), f32[32,8,128]{2,1,0:T(8,128)S(1)}, u32[]{:S(2)}, u32[]{:S(2)}) async-start(f32[32,8,128]{2,1,0:T(8,128)} %get-tuple-element.139), calls=%async_computation | async-start | bytes 262144 | tf_op jit(solution)/shard_map/all_to_all | solution.py:1067
  120.1 16.0 %copy-start.6 = (f32[48,3,384]{2,0,1:T(8,128)S(1)}, f32[48,3,384]{2,0,1:T(8,128)}, u32[]{:S(2)}) copy-start(f32[48,3,384]{2,0,1:T(8,128)} %param.38) | copy-start | bytes 663556
  120.1 16.0 %copy-start.7 = (f32[48,3,384]{2,0,1:T(8,128)S(1)}, f32[48,3,384]{2,0,1:T(8,128)}, u32[]{:S(2)}) copy-start(f32[48,3,384]{2,0,1:T(8,128)} %param.39) | copy-start | bytes 663556
  120.1 16.0 %copy-start.8 = (f32[48,3,384]{2,0,1:T(8,128)S(1)}, f32[48,3,384]{2,0,1:T(8,128)}, u32[]{:S(2)}) copy-start(f32[48,3,384]{2,0,1:T(8,128)} %param.40) | copy-start | bytes 663556
  126.1 10.0 %all-to-all-start.1 = ((f32[32,1,128]{2,1,0:T(1,128)}), f32[32,1,128]{2,1,0:T(1,128)S(1)}, u32[]{:S(2)}, u32[]{:S(2)}) async-start(f32[32,1,128]{2,1,0:T(1,128)} %bitcast.19), calls=%async_computation.1 | async-start | bytes 32768 | tf_op jit(solution)/shard_map/all_to_all | solution.py:1073
  (30 other events, 359.4 us)
